TPU v7x, 256 devices: a whole 4x4x8 slice. The times are simulated.
256 devices in a mesh: alpha: 16 (over x, z_lo), beta: 8 (over y, core), ints: 2 (over z_hi).
Axes of the slice: x: 4, y: 4, z: 8 (z_hi: 2, z_lo: 4; z = z_hi * 4 + z_lo), core: 2. Of those that a mesh axis runs over, the one named last changes fastest.
Arguments:
- ci_vector: float32 [4096, 4096], P('beta', 'alpha'), may hold values from -6 to 6
- integrals: float32 [32, 32], P('ints'), may hold values from -1 to 1
- alpha_source: int32 [32, 4096], P('ints', 'alpha'), may hold values from 0 to 4095
- alpha_sign: int32 [32, 4096], P('ints', 'alpha'), may hold values from -1 to 1
- beta_tiles: int32 [32, 32], replicated, may hold values from 0 to 31, each once within a row
- beta_offsets: int32 [32, 32, 128], replicated, may hold values from 0 to 127, each once within a row
- beta_sign: int32 [32, 4096], replicated, may hold values from -1 to 1
Outputs:
- sigma: float32 [4096, 4096], P('beta', 'alpha')
Inputs may be any that keep to these rules, and one draw needn't show every extreme that they name: Each row of beta_tiles names every tile once. Each row of beta_offsets names every position of a tile once.
All inputs are finite; a program needn't handle non-finite values.
Results may differ from a plain program's by a relative error of at most 0.00007.
Values sent between devices are 32-bit elements; how exact they have to be, the bound alone decides.
No kernel may reach another device: no remote copies, remote signals or barrier semaphores. Data moves between devices by JAX's collectives and lax.ppermute only.
A program may use at most 128 MiB of HBM per device.

v0:
```python
import jax
import jax.numpy as jnp
from jax import lax
from jax.sharding import PartitionSpec as P


def local(ci_vector, integrals, alpha_source, alpha_sign, beta_tiles, beta_offsets, beta_sign):
    rows_b = ci_vector.shape[0]
    cols_a = ci_vector.shape[1]
    tile = beta_offsets.shape[2]
    asign = alpha_sign.astype(jnp.float32)
    bsign = beta_sign.astype(jnp.float32)
    columns = lax.all_gather(ci_vector, "alpha", axis=1, tiled=True)

    def excite(idx, sgn):
        return jnp.take(columns, idx, axis=1) * sgn[None, :]

    excited = jax.vmap(excite)(alpha_source, asign)
    mixed = jnp.einsum("kl,kba->lba", integrals, excited, precision=lax.Precision.HIGHEST)
    local_pairs = mixed.shape[0]
    inverse = jnp.argsort(beta_tiles, axis=1, stable=True)
    my_tiles = rows_b // tile
    my_first = lax.axis_index("beta") * my_tiles
    tiles_here = lax.axis_size("beta") * rows_b // tile

    def step(item, term):
        pair = item // my_tiles
        slot = item % my_tiles
        target = inverse[pair, my_first + slot]
        inside = ((target >= 0) & (target < tiles_here)).astype(jnp.float32)
        safe = jnp.clip(target, 0, tiles_here - 1)
        offsets = beta_offsets[pair, target]
        signs = lax.dynamic_slice_in_dim(bsign[pair], target * tile, tile)
        plane = lax.dynamic_index_in_dim(mixed, pair, 0, keepdims=False)
        values = jnp.take(plane, slot * tile + offsets, axis=0) * (signs * inside)[:, None]
        old = lax.dynamic_slice_in_dim(term, safe * tile, tile, 0)
        return lax.dynamic_update_slice_in_dim(term, old + values, safe * tile, 0)

    zeros = jnp.zeros((lax.axis_size("beta") * rows_b, cols_a), jnp.float32)
    partial_sigma = lax.psum_scatter(
        lax.fori_loop(0, local_pairs * my_tiles, step, zeros),
        "beta",
        scatter_dimension=0,
        tiled=True,
    )
    return lax.psum(partial_sigma, "ints")


def solution(mesh):
    return jax.shard_map(
        local,
        mesh=mesh,
        in_specs=(
            P("beta", "alpha"),
            P("ints", None),
            P("ints", "alpha"),
            P("ints", "alpha"),
            P(),
            P(),
            P(),
        ),
        out_specs=P("beta", "alpha"),
        check_vma=False,
    )
```

profile of v0, /device:TPU:8, one launch (start us, length us, event | category | flops | bytes accessed | tf_op | source)
XLA Modules:
  0.0 1761.3 jit_solution(851516658184296317)
XLA Ops:
  13.5 186.3 %all-gather.2.cloned.1.call-done = f32[512,4096]{0,1:T(8,128)} async-done(((f32[512,256]{0,1:T(8,128)}), f32[512,4096]{0,1:T(8,128)}) %all-gather.2.cloned.1.call-update) | async-done | bytes 8388624 | tf_op jit(solution)/shard_map/all_gather | solution.py:13
  199.8 21.4 %gather_fusion.1 = f32[4096,512]{1,0:T(8,128)} fusion(f32[512,4096]{0,1:T(8,128)} %all-gather.2.cloned.1.call-done, s32[4096]{0:T(1024)S(1)} %broadcast_clamp_fusion), kind=kCustom, calls=%fused_computation.1 | custom fusion | bytes 16793600 | tf_op jit(solution)/shard_map/vmap(jit(_take))/gather | solution.py:16
  221.2 10.3 copy.13
  231.5 18.2 %convolution_bitcast_fusion = f32[32,512,256]{2,0,1:T(8,128)} fusion(f32[16,256,512]{1,0,2:T(8,128)} %copy.13, f32[16,256]{1,0:T(8,128)S(1)} %convert_element_type.17, pred[16,256]{1,0:T(8,128)(4,1)S(1)} %compare_and_fusion.1, f32[16,32]{1,0:T(8,128)S(1)} %copy-done), kind=kOutput, calls=%fused_computation.13 | convolution fusion | flops 809500672 | bytes 25188352 | tf_op jit(solution)/shard_map/kl,kba->lba/dot_general | solution.py:19
  251.9 1405.5 %while.16 = (s32[]{:T(128)}, f32[4096,256]{1,0:T(8,128)}, s32[]{:T(128)}, s32[32,32]{0,1:T(8,128)S(1)}, s32[32,32,128]{2,1,0:T(8,128)}, /*index=5*/f32[32,512,25...) while((s32[]{:T(128)}, f32[4096,256]{1,0:T(8,128)}, ...), condition=%wide.region_2.3_spmd, body=%wide.region_1.2_spmd.sunk | while | flops 100777 | bytes 2762096 | solution.py:41
  255.1 2.6 constant_dynamic-slice_fusion.3
  266.1 2.6 constant_dynamic-slice_fusion.3
  321.0 2.6 constant_dynamic-slice_fusion.3
  332.0 2.6 constant_dynamic-slice_fusion.3
  353.9 2.6 constant_dynamic-slice_fusion.3
  375.9 2.6 constant_dynamic-slice_fusion.3
  397.9 2.6 constant_dynamic-slice_fusion.3
  419.8 2.6 constant_dynamic-slice_fusion.3
  430.8 2.6 constant_dynamic-slice_fusion.3
  463.7 2.6 constant_dynamic-slice_fusion.3
  474.7 2.6 constant_dynamic-slice_fusion.3
  485.7 2.6 constant_dynamic-slice_fusion.3
  496.7 2.6 constant_dynamic-slice_fusion.3
  507.7 2.6 constant_dynamic-slice_fusion.3
  518.7 2.6 constant_dynamic-slice_fusion.3
  540.6 2.6 constant_dynamic-slice_fusion.3
  551.6 2.6 constant_dynamic-slice_fusion.3
  1657.4 34.9 %reduce-scatter.2.cloned.1.call-done = f32[512,256]{1,0:T(8,128)} async-done(((f32[4096,256]{1,0:T(8,128)}), f32[512,256]{1,0:T(8,128)}) %reduce-scatter.2.cloned.1.call-update) | async-done | bytes 524304 | tf_op jit(solution)/shard_map/reduce_scatter | solution.py:40
  1692.4 60.5 %all-reduce.2.cloned.1.call-done = f32[512,256]{1,0:T(8,128)} async-done(((f32[512,256]{1,0:T(8,128)}), f32[512,256]{1,0:T(8,128)}) %all-reduce.2.cloned.1.call-update) | async-done | bytes 524304 | tf_op jit(solution)/shard_map/psum | solution.py:46
  (1155 shorter events, 786.2 us)
Async XLA Ops:
  6.5 225.0 %copy-start = (f32[16,32]{1,0:T(8,128)S(1)}, f32[16,32]{1,0:T(8,128)}, u32[]{:S(2)}) copy-start(f32[16,32]{1,0:T(8,128)} %param.10) | copy-start | bytes 6148
  6.5 193.3 %all-gather.2.cloned.1.call-start = ((), (), s32[]{:S(2)}) async-start(), calls=%async_computation.1 | async-start | bytes 8912896 | tf_op jit(solution)/shard_map/all_gather | solution.py:13
  8.6 1683.8 %reduce-scatter.2.cloned.1.call-start = ((), (), s32[]{:S(2)}) async-start(), calls=%async_computation.2 | async-start | bytes 4718592 | tf_op jit(solution)/shard_map/reduce_scatter | solution.py:40
  1657.4 95.5 %all-reduce.2.cloned.1.call-start = ((), (), s32[]{:S(2)}) async-start(), calls=%async_computation.3 | async-start | bytes 1048576 | tf_op jit(solution)/shard_map/psum | solution.py:46
Sparse Core Ops, SparseCore 0:
  9.1 190.6 all-gather.1
  1657.5 34.8 reduce-scatter.1
  1695.0 57.9 all-reduce.1
where the time goes:
time: 1780 us; the launch traced here: 1760 us
  loops' own time  587 us (33%)
  local copies, waits for them, and re-layouts  542 us (30%)
  other arithmetic  319 us (18%)
  waiting for transfers between devices  282 us (16%)
  matrix products  18.2 us (1%)
    another operation x1, loops' own time, local(): lax.fori_loop(0, local_pairs * my_tiles, step, zeros)  587 us
    dynamic_slice x256, local copies, waits for them, and re-layouts, step(): plane = lax.dynamic_index_in_dim(mixed, pair, 0, keepdims=False)  332 us
    dynamic_update_slice x128, other arithmetic, step(): return lax.dynamic_update_slice_in_dim(term, old + values, safe * tile, 0)  213 us
    all_gather x1, waiting for transfers between devices, local(): columns = lax.all_gather(ci_vector, 'alpha', axis=1, tiled=True)  186 us
    gather x128, local copies, waits for them, and re-layouts, step(): jnp.take(plane, slot * tile + offsets, axis=0) * (signs * inside)[:, None]  96.6 us
    and x128, other arithmetic, step(): jnp.take(plane, slot * tile + offsets, axis=0) * (signs * inside)[:, None]  90.4 us
    dynamic_slice x128, local copies, waits for them, and re-layouts, step(): target = inverse[pair, my_first + slot]  74.6 us
    psum x1, waiting for transfers between devices, local(): return lax.psum(partial_sigma, 'ints')  60.5 us
  transfers between devices with their start and end apart: 3, of which 3 were waited for; matrix products, arithmetic and copies ran while one was open for 0% of the time, Pallas kernels for 0%

commit v1 on v0

v1 whole, which is shorter than its diff:
```python
import functools

import jax
import jax.numpy as jnp
from jax import lax
from jax.experimental import pallas as pl
from jax.experimental.pallas import tpu as pltpu
from jax.sharding import PartitionSpec as P

LANES = 128
GROUP = 8
RING = 4
AXES = ("alpha", "ints")


def chip(x, z, ints):
    run = RING
    full = run * ints
    x, z = x % RING, z % full
    return (x * run + z % run) * ints + z // run


def shift(value, dx, dz):
    ints = lax.axis_size("ints")
    rows = lax.axis_size("alpha") // RING
    pairs = [
        (chip(x, z, ints), chip(x + dx, z + dz, ints))
        for x in range(rows)
        for z in range(RING * ints)
    ]
    return lax.ppermute(value, AXES, pairs)


def spread(block, first, second):
    n = block.shape[0]
    half = n // 2
    ahead = shift(block, *[-s for s in first])
    behind = shift(block, *first)
    over_a = shift(ahead[:half], *[-s for s in first])
    over_b = shift(behind[half:], *first)
    line = jnp.concatenate([block, ahead, behind, over_a, over_b], 0)
    next_ahead = shift(line, *[-s for s in second])
    next_behind = shift(line, *second)
    last_a = shift(next_ahead[: 2 * n], *[-s for s in second])
    last_b = shift(next_behind[2 * n :], *second)
    pieces = []
    for step, array, lo, hi in (
        (0, line, 0, 4),
        (1, next_ahead, 0, 4),
        (3, next_behind, 0, 4),
        (2, last_a, 0, 2),
        (2, last_b, 2, 4),
    ):
        for at in range(lo, hi):
            along = (0, 1, 3, 2)[at]
            place = (first[0] * along + second[0] * step, first[1] * along + second[1] * step)
            pieces.append((place, array, (at - lo) * n))
    return pieces


def kernel(copies, steps, pairs, slots, *refs):
    arrays = refs[: len({c[0] for c in copies})]
    base_ref, src_ref, tgt_ref, sign_ref, vb_ref, off_ref, bs_ref, out_ref = refs[len(arrays) : len(arrays) + 8]
    table, g_ref, y_ref, vhi_ref, vlo_ref, sems = refs[len(arrays) + 8 :]
    dmas = []
    for n, (which, start, rows, slot, inner) in enumerate(copies):
        dmas.append(
            pltpu.make_async_copy(
                arrays[which].at[pl.ds(start, rows)],
                table.at[pl.ds(base_ref[slot] + inner, rows)],
                sems.at[n],
            )
        )
    for dma in dmas:
        dma.start()
    v = vb_ref[...]
    high = v.astype(jnp.bfloat16)
    vhi_ref[...] = high
    vlo_ref[...] = (v - high.astype(jnp.float32)).astype(jnp.bfloat16)
    out_ref[...] = jnp.zeros_like(out_ref)
    for dma in dmas:
        dma.wait()

    rows = GROUP * pairs
    quads = slots

    def mix(step, carry):
        for r in range(rows):
            g_ref[r] = table[src_ref[step * rows + r]]
        flat = g_ref.reshape(rows * quads, LANES)
        sign = sign_ref[pl.ds(step, 1), :].astype(jnp.bfloat16)
        left_hi = vhi_ref[...] * sign
        left_lo = vlo_ref[...] * sign
        for q in range(quads):
            g = flat[pl.ds(q, rows, stride=quads), :]
            hi = g.astype(jnp.bfloat16)
            lo = (g - hi.astype(jnp.float32)).astype(jnp.bfloat16)
            got = (
                jnp.dot(left_hi, hi, preferred_element_type=jnp.float32)
                + jnp.dot(left_hi, lo, preferred_element_type=jnp.float32)
                + jnp.dot(left_lo, hi, preferred_element_type=jnp.float32)
            )
            y_ref[:, q, pl.ds(step * GROUP, GROUP), :] = got.reshape(pairs, GROUP, LANES)
        return carry

    lax.fori_loop(0, steps, mix, 0)
    tiles = out_ref.shape[0]
    lines = lax.broadcasted_iota(jnp.int32, (LANES, LANES), 0)

    def place(pair, carry):
        for q in range(quads):
            t = tgt_ref[pair * quads + q]
            off = off_ref[pl.ds(pair * tiles + t, 1), :]
            sgn = bs_ref[pl.ds(pair * tiles + t, 1), :]
            hot = jnp.where(lines == off, sgn, 0.0).astype(jnp.bfloat16)
            y = y_ref[pair, q]
            hi = y.astype(jnp.bfloat16)
            lo = (y - hi.astype(jnp.float32)).astype(jnp.bfloat16)
            got = jnp.dot(hi, hot, preferred_element_type=jnp.float32) + jnp.dot(
                lo, hot, preferred_element_type=jnp.float32
            )
            out_ref[t] += got
        return carry

    lax.fori_loop(0, pairs, place, 0)


def local(ci_vector, integrals, alpha_source, alpha_sign, beta_tiles, beta_offsets, beta_sign):
    rows_b, cols_a = ci_vector.shape
    pairs, tiles, tile = beta_offsets.shape
    slots = rows_b // tile
    ints = lax.axis_size("ints")
    mine = lax.axis_index("ints")
    cols = cols_a // ints
    alpha = lax.axis_index("alpha")
    x, z = alpha // RING, alpha % RING

    swap = [(0, 1), (1, 0)]
    both = jnp.stack([alpha_source, alpha_sign])
    keep = lax.dynamic_slice_in_dim(both, mine * cols, cols, 2)
    give = lax.dynamic_slice_in_dim(both, (1 - mine) * cols, cols, 2)
    got = lax.ppermute(give, "ints", swap)
    v_got = lax.ppermute(integrals, "ints", swap)
    first = mine == 0
    full = jnp.concatenate([jnp.where(first, keep, got), jnp.where(first, got, keep)], 1)
    v = jnp.concatenate([jnp.where(first, integrals, v_got), jnp.where(first, v_got, integrals)], 0)
    flat = full.transpose(0, 2, 1).reshape(2, cols * pairs)
    source = flat[0]
    steps = cols // GROUP
    sign = flat[1].reshape(steps, GROUP * pairs).astype(jnp.float32)
    eye = jnp.eye(GROUP, dtype=jnp.float32)
    vb = (v.T[:, None, None, :] * eye[None, :, :, None]).reshape(pairs * GROUP, GROUP * pairs)

    my_first = lax.axis_index("beta") * slots
    wanted = my_first + jnp.arange(slots, dtype=jnp.int32)
    hit = beta_tiles[:, :, None] == wanted[None, None, :]
    target = jnp.sum(jnp.where(hit, jnp.arange(tiles, dtype=jnp.int32)[None, :, None], 0), axis=1).reshape(-1)

    columns = ci_vector.T.reshape(cols_a, slots, tile)
    n = cols_a // 2
    pieces_a = spread(columns[:n], (0, 1), (1, 0))
    pieces_b = spread(columns[n:], (1, 0), (0, 1))
    arrays, copies = [], []
    for inner, pieces in ((0, pieces_a), (n, pieces_b)):
        for (dx, dz), array, start in pieces:
            if not any(array is a for a in arrays):
                arrays.append(array)
            which = next(i for i, a in enumerate(arrays) if a is array)
            copies.append((which, start, n, (dx % RING) * RING + dz % RING, inner))
    d = jnp.arange(RING * RING, dtype=jnp.int32)
    base = (((x + d // RING) % RING) * RING + (z + d % RING) % RING) * cols_a

    smem = pl.BlockSpec(memory_space=pltpu.SMEM)
    vmem = pl.BlockSpec(memory_space=pltpu.VMEM)
    partial = pl.pallas_call(
        functools.partial(kernel, tuple(copies), steps, pairs, slots),
        out_shape=jax.ShapeDtypeStruct((tiles, cols, tile), jnp.float32),
        in_specs=[pl.BlockSpec(memory_space=pl.ANY)] * len(arrays) + [smem] * 3 + [vmem] * 4,
        out_specs=vmem,
        scratch_shapes=[
            pltpu.VMEM((lax.axis_size("alpha") * cols_a, slots, tile), jnp.float32),
            pltpu.VMEM((GROUP * pairs, slots, tile), jnp.float32),
            pltpu.VMEM((pairs, slots, cols, tile), jnp.float32),
            pltpu.VMEM((GROUP * pairs, GROUP * pairs), jnp.bfloat16),
            pltpu.VMEM((GROUP * pairs, GROUP * pairs), jnp.bfloat16),
            pltpu.SemaphoreType.DMA((len(copies),)),
        ],
        compiler_params=pltpu.CompilerParams(vmem_limit_bytes=40 * 1024 * 1024),
        name="sigma_partial",
    )(
        *arrays,
        base,
        source,
        target,
        sign,
        vb,
        beta_offsets.reshape(pairs * tiles, tile),
        beta_sign.astype(jnp.float32).reshape(pairs * tiles, tile),
    )
    summed = lax.psum_scatter(partial, "beta", scatter_dimension=0, tiled=True)
    other = lax.ppermute(summed, "ints", swap)
    left = jnp.where(first, summed, other)
    right = jnp.where(first, other, summed)
    joined = jnp.concatenate([left, right], 1)
    return joined.transpose(0, 2, 1).reshape(rows_b, cols_a)


def solution(mesh):
    return jax.shard_map(
        local,
        mesh=mesh,
        in_specs=(
            P("beta", "alpha"),
            P("ints", None),
            P("ints", "alpha"),
            P("ints", "alpha"),
            P(),
            P(),
            P(),
        ),
        out_specs=P("beta", "alpha"),
        check_vma=False,
    )
```

time: 1780 us -> 164 us (0.09)
  the two profiles are of different devices: /device:TPU:8 before, /device:TPU:25 now
where the time goes in v1:
time: 164 us; the launch traced here: 163 us
  waiting for transfers between devices  63.8 us (39%)
  starting transfers between devices  35.5 us (22%)
  Pallas kernels  26.1 us (16%)
  local copies, waits for them, and re-layouts  19.9 us (12%)
  between operations  13.6 us (8%)
  other arithmetic  4.37 us (3%)
    reduce_scatter x1, waiting for transfers between devices, local(): summed = lax.psum_scatter(partial, 'beta', scatter_dimension=0, tiled=True)  38.1 us
    pallas_call x1, Pallas kernels, local(): pl.pallas_call(functools.partial(kernel, tuple(copies), steps, pairs, slo...  26.1 us
    ppermute x16, starting transfers between devices, shift(): return lax.ppermute(value, AXES, pairs)  24.8 us
    ppermute x16, waiting for transfers between devices, shift(): return lax.ppermute(value, AXES, pairs)  14 us
    ppermute x1, waiting for transfers between devices, local(): other = lax.ppermute(summed, 'ints', swap)  11.6 us
    unnamed x20, local copies, waits for them, and re-layouts  7.75 us
    ppermute x1, starting transfers between devices, local(): other = lax.ppermute(summed, 'ints', swap)  5.28 us
    ppermute x1, starting transfers between devices, local(): v_got = lax.ppermute(integrals, 'ints', swap)  3.92 us
  transfers between devices with their start and end apart: 20, of which 6 were waited for; matrix products, arithmetic and copies ran while one was open for 12% of the time, Pallas kernels for 0%

profile of v1, /device:TPU:25, one launch (start us, length us, event | category | flops | bytes accessed | tf_op | source)
XLA Modules:
  0.0 163.3 jit_solution(2991302096871601860)
XLA Ops:
  7.8 1.7 %collective-permute-start.1 = (f32[128,4,128]{2,1,0:T(4,128)S(1)}, f32[128,4,128]{2,1,0:T(4,128)S(1)}, u32[]{:S(2)}, u32[]{:S(2)}) collective-permute-start(f32[128,4,128]{2,1,0:T(4,128)S(1)} %copy.25), channel_id=1, source_target_pairs={{0,16},{16,32},{32,48},{48,1},{1,17},{17,33},{33,49},{49,0},{64,80... | collective-permute-start | bytes 786440 | tf_op jit(solution)/shard_map/ppermute | solution.py:31
  9.5 4.0 %collective-permute-start = (f32[128,4,128]{2,1,0:T(4,128)S(1)}, f32[128,4,128]{2,1,0:T(4,128)S(1)}, u32[]{:S(2)}, u32[]{:S(2)}) collective-permute-start(f32[128,4,128]{2,1,0:T(4,128)S(1)} %copy.25), channel_id=1, source_target_pairs={{0,49},{16,0},{32,16},{48,32},{1,48},{17,1},{33,17},{49,33},{64,11... | collective-permute-start | bytes 786440 | tf_op jit(solution)/shard_map/ppermute | solution.py:31
  13.7 1.3 collective-permute-start.9
  15.0 1.5 collective-permute-start.8
  16.4 3.9 %collective-permute-start.17 = (f32[16,32]{1,0:T(8,128)S(1)}, f32[16,32]{1,0:T(8,128)S(1)}, u32[]{:S(2)}, u32[]{:S(2)}) collective-permute-start(f32[16,32]{1,0:T(8,128)S(1)} %copy-done.5), channel_id=1, source_target_pairs={{0,1},{1,0},{2,3},{3,2},{4,5},{5,4},{6,7},{7,6},{8,9},{9,8},{10,11... | collective-permute-start | bytes 6152 | tf_op jit(solution)/shard_map/ppermute | solution.py:143
  22.0 2.7 %collective-permute-start.2 = (f32[64,4,128]{2,1,0:T(4,128)S(1)}, f32[64,4,128]{2,1,0:T(4,128)S(1)}, u32[]{:S(2)}, u32[]{:S(2)}) collective-permute-start(f32[64,4,128]{2,1,0:T(4,128)S(1)} %slice.59), channel_id=1, source_target_pairs={{0,49},{16,0},{32,16},{48,32},{1,48},{17,1},{33,17},{49,33},{64,11... | collective-permute-start | bytes 393224 | tf_op jit(solution)/shard_map/ppermute | solution.py:31
  24.8 2.7 %collective-permute-start.10 = (f32[64,4,128]{2,1,0:T(4,128)S(1)}, f32[64,4,128]{2,1,0:T(4,128)S(1)}, u32[]{:S(2)}, u32[]{:S(2)}) collective-permute-start(f32[64,4,128]{2,1,0:T(4,128)S(1)} %slice.64), channel_id=1, source_target_pairs={{0,192},{16,208},{32,224},{48,240},{1,193},{17,209},{33,225},{49,2... | collective-permute-start | bytes 393224 | tf_op jit(solution)/shard_map/ppermute | solution.py:31
  31.8 2.7 %collective-permute-start.12 = (f32[512,4,128]{2,1,0:T(4,128)}, f32[512,4,128]{2,1,0:T(4,128)S(1)}, u32[]{:S(2)}, u32[]{:S(2)}) collective-permute-start(f32[512,4,128]{2,1,0:T(4,128)} %constant_dynamic-update-slice_fusion.5.refs_5_), channel_id=1, source_target_pairs={{0,49},{16,0},{32,16},{48,32},{1,48},{17,1},{33,17},{49,33},{64,11... | collective-permute-start | bytes 3145736 | tf_op jit(solution)/shard_map/ppermute | solution.py:31
  35.8 2.7 %collective-permute-start.4 = (f32[512,4,128]{2,1,0:T(4,128)}, f32[512,4,128]{2,1,0:T(4,128)}, u32[]{:S(2)}, u32[]{:S(2)}) collective-permute-start(f32[512,4,128]{2,1,0:T(4,128)} %constant_dynamic-update-slice_fusion.refs_0_), channel_id=1, source_target_pairs={{0,192},{16,208},{32,224},{48,240},{1,193},{17,209},{33,225},{49,2... | collective-permute-start | bytes 3145736 | tf_op jit(solution)/shard_map/ppermute | solution.py:31
  38.9 1.9 %convert_element_type.18 = f32[32,4096]{1,0:T(8,128)} convert(s32[32,4096]{1,0:T(8,128)} %param.13) | non-fusion elementwise | flops 131072 | bytes 1048576 | tf_op jit(solution)/shard_map/convert_element_type | solution.py:198
  40.8 1.9 %reshape.41.refs_16_ = f32[1024,128]{1,0:T(8,128)} reshape(f32[32,4096]{1,0:T(8,128)} %convert_element_type.18) | data formatting | bytes 1048576 | tf_op jit(solution)/shard_map/reshape | solution.py:198
  42.7 1.5 collective-permute-start.16
  44.3 1.2 broadcast_multiply_fusion
  45.5 1.5 mul.40.refs_14_
  47.0 8.0 %collective-permute-done.13.refs_7_ = f32[512,4,128]{2,1,0:T(4,128)S(1)} collective-permute-done((f32[512,4,128]{2,1,0:T(4,128)}, f32[512,4,128]{2,1,0:T(4,128)S(1)}, u32[]{:S(2)}, u32[]{:S(2)}) %collective-permute-start.13) | collective-permute-done | bytes 1048608 | tf_op jit(solution)/shard_map/ppermute | solution.py:31
  56.7 2.7 %collective-permute-start.14 = (f32[256,4,128]{2,1,0:T(4,128)}, f32[256,4,128]{2,1,0:T(4,128)}, u32[]{:S(2)}, u32[]{:S(2)}) collective-permute-start(f32[256,4,128]{2,1,0:T(4,128)} %slice.66), channel_id=1, source_target_pairs={{0,49},{16,0},{32,16},{48,32},{1,48},{17,1},{33,17},{49,33},{64,11... | collective-permute-start | bytes 1572872 | tf_op jit(solution)/shard_map/ppermute | solution.py:31
  60.2 1.9 %slice.61 = f32[256,4,128]{2,1,0:T(4,128)} slice(f32[512,4,128]{2,1,0:T(4,128)} %collective-permute-done.4.refs_1_), slice={[0:256], [0:4], [0:128]} | slice | bytes 1048576 | tf_op jit(solution)/shard_map/slice | solution.py:44
  62.1 2.7 %collective-permute-start.6 = (f32[256,4,128]{2,1,0:T(4,128)}, f32[256,4,128]{2,1,0:T(4,128)}, u32[]{:S(2)}, u32[]{:S(2)}) collective-permute-start(f32[256,4,128]{2,1,0:T(4,128)} %slice.61), channel_id=1, source_target_pairs={{0,192},{16,208},{32,224},{48,240},{1,193},{17,209},{33,225},{49,2... | collective-permute-start | bytes 1572872 | tf_op jit(solution)/shard_map/ppermute | solution.py:31
  65.1 1.1 collective-permute-done.15.refs_9_
  66.3 3.8 %collective-permute-done.7.refs_4_ = f32[256,4,128]{2,1,0:T(4,128)} collective-permute-done((f32[256,4,128]{2,1,0:T(4,128)}, f32[256,4,128]{2,1,0:T(4,128)}, u32[]{:S(2)}, u32[]{:S(2)}) %collective-permute-start.7) | collective-permute-done | bytes 524320 | tf_op jit(solution)/shard_map/ppermute | solution.py:31
  73.3 26.1 %sigma_partial.1 = f32[32,128,128]{2,1,0:T(8,128)} custom-call(f32[512,4,128]{2,1,0:T(4,128)} %constant_dynamic-update-slice_fusion.refs_0_, f32[512,4,128]{2,1,0:T(4,128)} %collective-permute-done.4.refs_1_, f32[512,4,128]{2,1,0:T(4,128)S(1)} %collective-permute-done.5.refs_2_, f32[256,4,128]{2,1,0:T(4,128)} %collective-permute-done.6.refs_3_, ...), custom_call_target="tpu_custom_call" | custom-call | tf_op jit(solution)/shard_map/sigma_partial/pallas_call | solution.py:175
  99.4 38.1 %reduce-scatter.2.cloned.1.call-done = f32[4,128,128]{2,1,0:T(8,128)} async-done(((f32[32,128,128]{2,1,0:T(8,128)}), f32[4,128,128]{2,1,0:T(8,128)}) %reduce-scatter.2.cloned.1.call-update) | async-done | bytes 262160 | tf_op jit(solution)/shard_map/reduce_scatter | solution.py:200
  137.5 5.3 %collective-permute-start.18 = (f32[4,128,128]{2,1,0:T(8,128)}, f32[4,128,128]{2,1,0:T(8,128)S(1)}, u32[]{:S(2)}, u32[]{:S(2)}) collective-permute-start(f32[4,128,128]{2,1,0:T(8,128)} %reduce-scatter.2.cloned.1.call-done), channel_id=1, source_target_pairs={{0,1},{1,0},{2,3},{3,2},{4,5},{5,4},{6,7},{7,6},{8,9},{9,8},{10,11... | collective-permute-start | bytes 786440 | tf_op jit(solution)/shard_map/ppermute | solution.py:201
  142.8 11.6 %collective-permute-done.18 = f32[4,128,128]{2,1,0:T(8,128)S(1)} collective-permute-done((f32[4,128,128]{2,1,0:T(8,128)}, f32[4,128,128]{2,1,0:T(8,128)S(1)}, u32[]{:S(2)}, u32[]{:S(2)}) %collective-permute-start.18) | collective-permute-done | bytes 262176 | tf_op jit(solution)/shard_map/ppermute | solution.py:201
  (75 shorter events, 17.2 us)
Async XLA Ops:
  6.5 9.9 %copy-start.5 = (f32[16,32]{1,0:T(8,128)S(1)}, f32[16,32]{1,0:T(8,128)}, u32[]{:S(2)}) copy-start(f32[16,32]{1,0:T(8,128)} %param.8) | copy-start | bytes 6148
  6.5 130.9 %reduce-scatter.2.cloned.1.call-start = ((), (), s32[]{:S(2)}) async-start(), calls=%async_computation.1 | async-start | bytes 2359296 | tf_op jit(solution)/shard_map/reduce_scatter | solution.py:200
  7.8 14.0 %collective-permute-start.1 = (f32[128,4,128]{2,1,0:T(4,128)S(1)}, f32[128,4,128]{2,1,0:T(4,128)S(1)}, u32[]{:S(2)}, u32[]{:S(2)}) collective-permute-start(f32[128,4,128]{2,1,0:T(4,128)S(1)} %copy.25), channel_id=1, source_target_pairs={{0,16},{16,32},{32,48},{48,1},{1,17},{17,33},{33,49},{49,0},{64,80... | collective-permute-start | bytes 786440 | tf_op jit(solution)/shard_map/ppermute | solution.py:31
  9.5 12.4 %collective-permute-start = (f32[128,4,128]{2,1,0:T(4,128)S(1)}, f32[128,4,128]{2,1,0:T(4,128)S(1)}, u32[]{:S(2)}, u32[]{:S(2)}) collective-permute-start(f32[128,4,128]{2,1,0:T(4,128)S(1)} %copy.25), channel_id=1, source_target_pairs={{0,49},{16,0},{32,16},{48,32},{1,48},{17,1},{33,17},{49,33},{64,11... | collective-permute-start | bytes 786440 | tf_op jit(solution)/shard_map/ppermute | solution.py:31
  13.7 11.0 %collective-permute-start.9 = (f32[128,4,128]{2,1,0:T(4,128)S(1)}, f32[128,4,128]{2,1,0:T(4,128)S(1)}, u32[]{:S(2)}, u32[]{:S(2)}) collective-permute-start(f32[128,4,128]{2,1,0:T(4,128)S(1)} %copy.26), channel_id=1, source_target_pairs={{0,64},{16,80},{32,96},{48,112},{1,65},{17,81},{33,97},{49,113},{6... | collective-permute-start | bytes 786440 | tf_op jit(solution)/shard_map/ppermute | solution.py:31
  15.0 9.8 %collective-permute-start.8 = (f32[128,4,128]{2,1,0:T(4,128)S(1)}, f32[128,4,128]{2,1,0:T(4,128)S(1)}, u32[]{:S(2)}, u32[]{:S(2)}) collective-permute-start(f32[128,4,128]{2,1,0:T(4,128)S(1)} %copy.26), channel_id=1, source_target_pairs={{0,192},{16,208},{32,224},{48,240},{1,193},{17,209},{33,225},{49,2... | collective-permute-start | bytes 786440 | tf_op jit(solution)/shard_map/ppermute | solution.py:31
  16.4 26.3 %collective-permute-start.17 = (f32[16,32]{1,0:T(8,128)S(1)}, f32[16,32]{1,0:T(8,128)S(1)}, u32[]{:S(2)}, u32[]{:S(2)}) collective-permute-start(f32[16,32]{1,0:T(8,128)S(1)} %copy-done.5), channel_id=1, source_target_pairs={{0,1},{1,0},{2,3},{3,2},{4,5},{5,4},{6,7},{7,6},{8,9},{9,8},{10,11... | collective-permute-start | bytes 6152 | tf_op jit(solution)/shard_map/ppermute | solution.py:143
  21.8 16.6 %copy-start.2 = (s32[16,256]{1,0:T(8,128)S(1)}, s32[16,256]{1,0:T(8,128)}, u32[]{:S(2)}) copy-start(s32[16,256]{1,0:T(8,128)} %param.9) | copy-start | bytes 49156
  21.8 16.6 %copy-start.3 = (s32[16,256]{1,0:T(8,128)S(1)}, s32[16,256]{1,0:T(8,128)}, u32[]{:S(2)}) copy-start(s32[16,256]{1,0:T(8,128)} %param.10) | copy-start | bytes 49156
  21.8 16.7 %copy-start.4 = (s32[32,32]{1,0:T(8,128)S(1)}, s32[32,32]{1,0:T(8,128)}, u32[]{:S(2)}) copy-start(s32[32,32]{1,0:T(8,128)} %param.11) | copy-start | bytes 12292
  21.8 13.3 %collective-permute-start.3 = (f32[64,4,128]{2,1,0:T(4,128)S(1)}, f32[64,4,128]{2,1,0:T(4,128)S(1)}, u32[]{:S(2)}, u32[]{:S(2)}) collective-permute-start(f32[64,4,128]{2,1,0:T(4,128)S(1)} %slice.60), channel_id=1, source_target_pairs={{0,16},{16,32},{32,48},{48,1},{1,17},{17,33},{33,49},{49,0},{64,80... | collective-permute-start | bytes 393224 | tf_op jit(solution)/shard_map/ppermute | solution.py:31
  22.0 12.5 %collective-permute-start.2 = (f32[64,4,128]{2,1,0:T(4,128)S(1)}, f32[64,4,128]{2,1,0:T(4,128)S(1)}, u32[]{:S(2)}, u32[]{:S(2)}) collective-permute-start(f32[64,4,128]{2,1,0:T(4,128)S(1)} %slice.59), channel_id=1, source_target_pairs={{0,49},{16,0},{32,16},{48,32},{1,48},{17,1},{33,17},{49,33},{64,11... | collective-permute-start | bytes 393224 | tf_op jit(solution)/shard_map/ppermute | solution.py:31
  24.7 6.4 %collective-permute-start.11 = (f32[64,4,128]{2,1,0:T(4,128)S(1)}, f32[64,4,128]{2,1,0:T(4,128)S(1)}, u32[]{:S(2)}, u32[]{:S(2)}) collective-permute-start(f32[64,4,128]{2,1,0:T(4,128)S(1)} %slice.65), channel_id=1, source_target_pairs={{0,64},{16,80},{32,96},{48,112},{1,65},{17,81},{33,97},{49,113},{6... | collective-permute-start | bytes 393224 | tf_op jit(solution)/shard_map/ppermute | solution.py:31
  24.8 5.6 %collective-permute-start.10 = (f32[64,4,128]{2,1,0:T(4,128)S(1)}, f32[64,4,128]{2,1,0:T(4,128)S(1)}, u32[]{:S(2)}, u32[]{:S(2)}) collective-permute-start(f32[64,4,128]{2,1,0:T(4,128)S(1)} %slice.64), channel_id=1, source_target_pairs={{0,192},{16,208},{32,224},{48,240},{1,193},{17,209},{33,225},{49,2... | collective-permute-start | bytes 393224 | tf_op jit(solution)/shard_map/ppermute | solution.py:31
  31.8 23.2 %collective-permute-start.13 = (f32[512,4,128]{2,1,0:T(4,128)}, f32[512,4,128]{2,1,0:T(4,128)S(1)}, u32[]{:S(2)}, u32[]{:S(2)}) collective-permute-start(f32[512,4,128]{2,1,0:T(4,128)} %constant_dynamic-update-slice_fusion.5.refs_5_), channel_id=1, source_target_pairs={{0,16},{16,32},{32,48},{48,1},{1,17},{17,33},{33,49},{49,0},{64,80... | collective-permute-start | bytes 3145736 | tf_op jit(solution)/shard_map/ppermute | solution.py:31
  31.8 24.1 %collective-permute-start.12 = (f32[512,4,128]{2,1,0:T(4,128)}, f32[512,4,128]{2,1,0:T(4,128)S(1)}, u32[]{:S(2)}, u32[]{:S(2)}) collective-permute-start(f32[512,4,128]{2,1,0:T(4,128)} %constant_dynamic-update-slice_fusion.5.refs_5_), channel_id=1, source_target_pairs={{0,49},{16,0},{32,16},{48,32},{1,48},{17,1},{33,17},{49,33},{64,11... | collective-permute-start | bytes 3145736 | tf_op jit(solution)/shard_map/ppermute | solution.py:31
  35.8 23.6 %collective-permute-start.5 = (f32[512,4,128]{2,1,0:T(4,128)}, f32[512,4,128]{2,1,0:T(4,128)S(1)}, u32[]{:S(2)}, u32[]{:S(2)}) collective-permute-start(f32[512,4,128]{2,1,0:T(4,128)} %constant_dynamic-update-slice_fusion.refs_0_), channel_id=1, source_target_pairs={{0,64},{16,80},{32,96},{48,112},{1,65},{17,81},{33,97},{49,113},{6... | collective-permute-start | bytes 3145736 | tf_op jit(solution)/shard_map/ppermute | solution.py:31
  35.8 24.4 %collective-permute-start.4 = (f32[512,4,128]{2,1,0:T(4,128)}, f32[512,4,128]{2,1,0:T(4,128)}, u32[]{:S(2)}, u32[]{:S(2)}) collective-permute-start(f32[512,4,128]{2,1,0:T(4,128)} %constant_dynamic-update-slice_fusion.refs_0_), channel_id=1, source_target_pairs={{0,192},{16,208},{32,224},{48,240},{1,193},{17,209},{33,225},{49,2... | collective-permute-start | bytes 3145736 | tf_op jit(solution)/shard_map/ppermute | solution.py:31
  42.7 22.0 %collective-permute-start.16 = (s32[2,16,128]{2,1,0:T(8,128)S(1)}, s32[2,16,128]{2,1,0:T(8,128)S(1)}, u32[]{:S(2)}, u32[]{:S(2)}) collective-permute-start(s32[2,16,128]{2,1,0:T(8,128)S(1)} %fusion), channel_id=1, source_target_pairs={{0,1},{1,0},{2,3},{3,2},{4,5},{5,4},{6,7},{7,6},{8,9},{9,8},{10,11... | collective-permute-start | bytes 49160 | tf_op jit(solution)/shard_map/ppermute | solution.py:142
  55.8 10.5 %collective-permute-start.15 = (f32[256,4,128]{2,1,0:T(4,128)}, f32[256,4,128]{2,1,0:T(4,128)}, u32[]{:S(2)}, u32[]{:S(2)}) collective-permute-start(f32[256,4,128]{2,1,0:T(4,128)} %slice.67), channel_id=1, source_target_pairs={{0,16},{16,32},{32,48},{48,1},{1,17},{17,33},{33,49},{49,0},{64,80... | collective-permute-start | bytes 1572872 | tf_op jit(solution)/shard_map/ppermute | solution.py:31
  56.7 9.6 %collective-permute-start.14 = (f32[256,4,128]{2,1,0:T(4,128)}, f32[256,4,128]{2,1,0:T(4,128)}, u32[]{:S(2)}, u32[]{:S(2)}) collective-permute-start(f32[256,4,128]{2,1,0:T(4,128)} %slice.66), channel_id=1, source_target_pairs={{0,49},{16,0},{32,16},{48,32},{1,48},{17,1},{33,17},{49,33},{64,11... | collective-permute-start | bytes 1572872 | tf_op jit(solution)/shard_map/ppermute | solution.py:31
  60.2 9.9 %collective-permute-start.7 = (f32[256,4,128]{2,1,0:T(4,128)}, f32[256,4,128]{2,1,0:T(4,128)}, u32[]{:S(2)}, u32[]{:S(2)}) collective-permute-start(f32[256,4,128]{2,1,0:T(4,128)} %slice.62), channel_id=1, source_target_pairs={{0,64},{16,80},{32,96},{48,112},{1,65},{17,81},{33,97},{49,113},{6... | collective-permute-start | bytes 1572872 | tf_op jit(solution)/shard_map/ppermute | solution.py:31
  62.1 9.1 %collective-permute-start.6 = (f32[256,4,128]{2,1,0:T(4,128)}, f32[256,4,128]{2,1,0:T(4,128)}, u32[]{:S(2)}, u32[]{:S(2)}) collective-permute-start(f32[256,4,128]{2,1,0:T(4,128)} %slice.61), channel_id=1, source_target_pairs={{0,192},{16,208},{32,224},{48,240},{1,193},{17,209},{33,225},{49,2... | collective-permute-start | bytes 1572872 | tf_op jit(solution)/shard_map/ppermute | solution.py:31
  137.5 16.9 %collective-permute-start.18 = (f32[4,128,128]{2,1,0:T(8,128)}, f32[4,128,128]{2,1,0:T(8,128)S(1)}, u32[]{:S(2)}, u32[]{:S(2)}) collective-permute-start(f32[4,128,128]{2,1,0:T(8,128)} %reduce-scatter.2.cloned.1.call-done), channel_id=1, source_target_pairs={{0,1},{1,0},{2,3},{3,2},{4,5},{5,4},{6,7},{7,6},{8,9},{9,8},{10,11... | collective-permute-start | bytes 786440 | tf_op jit(solution)/shard_map/ppermute | solution.py:201
  (2 other events, 2.1 us)
Sparse Core Ops, SparseCore 0:
  99.5 37.9 reduce-scatter.1

commit v2 on v1

v2 whole, which is shorter than its diff:
```python
import functools

import jax
import jax.numpy as jnp
from jax import lax
from jax.experimental import pallas as pl
from jax.experimental.pallas import tpu as pltpu
from jax.sharding import PartitionSpec as P

LANES = 128
GROUP = 8
RING = 4
CORES = 2
AXES = ("alpha", "ints")


def chip(x, z, ints):
    run = RING
    full = run * ints
    x, z = x % RING, z % full
    return (x * run + z % run) * ints + z // run


def shift(value, dx, dz):
    ints = lax.axis_size("ints")
    rows = lax.axis_size("alpha") // RING
    pairs = [
        (chip(x, z, ints), chip(x + dx, z + dz, ints))
        for x in range(rows)
        for z in range(RING * ints)
    ]
    return lax.ppermute(value, AXES, pairs)


def spread(block, first, second):
    n = block.shape[0]
    fore = lambda value, axis: shift(value, *[-s for s in axis])
    back = lambda value, axis: shift(value, *axis)
    ahead = fore(block, first)
    behind = back(block, first)
    early = jnp.concatenate([block, ahead], 0)
    over = fore(ahead, first)
    late = jnp.concatenate([behind, over], 0)
    early_ahead, early_behind = fore(early, second), back(early, second)
    late_ahead, late_behind = fore(late, second), back(late, second)
    early_over = fore(early_ahead, second)
    late_over = back(late_behind, second)
    pieces = []
    for step, array, steps in (
        (0, (block,), (0,)),
        (0, (ahead,), (1,)),
        (0, (behind,), (3,)),
        (0, (over,), (2,)),
        (1, early_ahead, (0, 1)),
        (3, early_behind, (0, 1)),
        (1, late_ahead, (3, 2)),
        (3, late_behind, (3, 2)),
        (2, early_over, (0, 1)),
        (2, late_over, (3, 2)),
    ):
        array = array[0] if isinstance(array, tuple) else array
        for at, along in enumerate(steps):
            place = (first[0] * along + second[0] * step, first[1] * along + second[1] * step)
            pieces.append((place, array, at * n))
    return pieces


def kernel(copies, steps, pairs, slots, *refs):
    arrays = refs[: len({c[0] for c in copies})]
    base_ref, src_ref, tgt_ref, sign_ref, vb_ref, off_hbm, bs_hbm, keep_hbm, give_hbm = refs[
        len(arrays) : len(arrays) + 9
    ]
    table, g_ref, y_ref, vhi_ref, vlo_ref, off_ref, bs_ref, acc_ref, sems, sem_off, sem_bs, sem_out = refs[
        len(arrays) + 9 :
    ]
    dmas = []
    for n, (which, start, rows, slot, inner) in enumerate(copies):
        dmas.append(
            pltpu.make_async_copy(
                arrays[which].at[pl.ds(start, rows)],
                table.at[pl.ds(base_ref[slot] + inner, rows)],
                sems.at[n],
            )
        )
    for dma in dmas:
        dma.start()
    load_off = pltpu.make_async_copy(off_hbm, off_ref, sem_off)
    load_bs = pltpu.make_async_copy(bs_hbm, bs_ref, sem_bs)
    load_off.start()
    load_bs.start()
    v = vb_ref[...]
    high = v.astype(jnp.bfloat16)
    vhi_ref[...] = high
    vlo_ref[...] = (v - high.astype(jnp.float32)).astype(jnp.bfloat16)
    acc_ref[...] = jnp.zeros_like(acc_ref)
    for dma in dmas:
        dma.wait()

    rows = GROUP * pairs

    def fetch(step, buffer):
        for r in range(rows):
            g_ref[buffer, r] = table[src_ref[step * rows + r]]

    def mix(step, buffer):
        flat = g_ref.at[buffer].reshape(rows * slots, LANES)
        sign = sign_ref[pl.ds(step, 1), :].astype(jnp.bfloat16)
        left_hi = vhi_ref[...] * sign
        left_lo = vlo_ref[...] * sign
        g = jnp.concatenate([flat[pl.ds(q, rows, stride=slots), :] for q in range(slots)], 1)
        hi = g.astype(jnp.bfloat16)
        lo = (g - hi.astype(jnp.float32)).astype(jnp.bfloat16)
        got = (
            jnp.dot(left_hi, hi, preferred_element_type=jnp.float32)
            + jnp.dot(left_hi, lo, preferred_element_type=jnp.float32)
            + jnp.dot(left_lo, hi, preferred_element_type=jnp.float32)
        )
        for q in range(slots):
            part = got[:, q * LANES : (q + 1) * LANES]
            y_ref[:, q, pl.ds(step * GROUP, GROUP), :] = part.reshape(pairs, GROUP, LANES)

    fetch(0, 0)

    def two(half, carry):
        step = half * 2
        fetch(step + 1, 1)
        mix(step, 0)
        fetch(jnp.minimum(step + 2, steps - 1), 0)
        mix(step + 1, 1)
        return carry

    lax.fori_loop(0, steps // 2, two, 0)
    load_off.wait()
    load_bs.wait()
    lines = lax.broadcasted_iota(jnp.int32, (LANES, LANES), 0)
    tiles = acc_ref.shape[0]

    def place(pair):
        found = []
        for q in range(slots):
            t = tgt_ref[pair * slots + q]
            spot = tgt_ref[(pairs + pair) * slots + q]
            off = off_ref[pl.ds(pair * tiles + t, 1), :]
            sgn = bs_ref[pl.ds(pair * tiles + t, 1), :].astype(jnp.float32)
            hot = jnp.where(lines == off, sgn, 0.0).astype(jnp.bfloat16)
            y = y_ref[pair, q]
            hi = y.astype(jnp.bfloat16)
            lo = (y - hi.astype(jnp.float32)).astype(jnp.bfloat16)
            left = jnp.concatenate([hi, lo], 1)
            right = jnp.concatenate([hot, hot], 0)
            found.append((spot, jnp.dot(left, right, preferred_element_type=jnp.float32)))
        for spot, value in found:
            acc_ref[spot] += value

    def two_pairs(half, carry):
        place(half * 2)
        place(half * 2 + 1)
        return carry

    lax.fori_loop(0, pairs // 2, two_pairs, 0)
    half = tiles // 2
    store_give = pltpu.make_async_copy(acc_ref.at[pl.ds(half, half)], give_hbm, sem_out.at[0])
    store_keep = pltpu.make_async_copy(acc_ref.at[pl.ds(0, half)], keep_hbm, sem_out.at[1])
    store_give.start()
    store_keep.start()
    store_give.wait()
    store_keep.wait()


def local(ci_vector, integrals, alpha_source, alpha_sign, beta_tiles, beta_offsets, beta_sign):
    rows_b, cols_a = ci_vector.shape
    pairs, tiles, tile = beta_offsets.shape
    slots = rows_b // tile
    ints = lax.axis_size("ints")
    mine = lax.axis_index("ints")
    cols = cols_a // ints
    alpha = lax.axis_index("alpha")
    x, z = alpha // RING, alpha % RING

    swap = [(0, 1), (1, 0)]
    both = jnp.stack([alpha_source, alpha_sign])
    keep = lax.dynamic_slice_in_dim(both, mine * cols, cols, 2)
    give = lax.dynamic_slice_in_dim(both, (1 - mine) * cols, cols, 2)
    got = lax.ppermute(give, "ints", swap)
    v_got = lax.ppermute(integrals, "ints", swap)
    first = mine == 0
    full = jnp.concatenate([jnp.where(first, keep, got), jnp.where(first, got, keep)], 1)
    v = jnp.concatenate([jnp.where(first, integrals, v_got), jnp.where(first, v_got, integrals)], 0)
    flat = full.transpose(0, 2, 1).reshape(2, cols * pairs)
    source = flat[0]
    steps = cols // GROUP
    sign = flat[1].reshape(steps, GROUP * pairs).astype(jnp.float32)
    eye = jnp.eye(GROUP, dtype=jnp.float32)
    vb = (v.T[:, None, None, :] * eye[None, :, :, None]).reshape(pairs * GROUP, GROUP * pairs)

    beta = lax.axis_index("beta")
    betas = lax.axis_size("beta")
    rings = betas // CORES
    y, core = beta // CORES, beta % CORES
    wanted = beta * slots + jnp.arange(slots, dtype=jnp.int32)
    hit = beta_tiles[:, :, None] == wanted[None, None, :]
    target = jnp.sum(jnp.where(hit, jnp.arange(tiles, dtype=jnp.int32)[None, :, None], 0), axis=1).reshape(-1)
    owner = target // slots
    away = (owner // CORES - y) % rings
    spot = ((owner % CORES) ^ core) * (tiles // CORES) + away * slots + target % slots
    target = jnp.concatenate([target, spot])

    columns = ci_vector.T.reshape(cols_a, slots, tile)
    n = cols_a // 2
    pieces_a = spread(columns[:n], (0, 1), (1, 0))
    pieces_b = spread(columns[n:], (1, 0), (0, 1))
    arrays, copies = [], []
    for inner, pieces in ((0, pieces_a), (n, pieces_b)):
        for (dx, dz), array, start in pieces:
            if not any(array is a for a in arrays):
                arrays.append(array)
            which = next(i for i, a in enumerate(arrays) if a is array)
            copies.append((which, start, n, (dx % RING) * RING + dz % RING, inner))
    d = jnp.arange(RING * RING, dtype=jnp.int32)
    base = (((x + d // RING) % RING) * RING + (z + d % RING) % RING) * cols_a

    smem = pl.BlockSpec(memory_space=pltpu.SMEM)
    vmem = pl.BlockSpec(memory_space=pltpu.VMEM)
    hbm = pl.BlockSpec(memory_space=pl.ANY)
    half = jax.ShapeDtypeStruct((tiles // CORES, cols, tile), jnp.float32)
    keep, give = pl.pallas_call(
        functools.partial(kernel, tuple(copies), steps, pairs, slots),
        out_shape=(half, half),
        in_specs=[hbm] * len(arrays) + [smem] * 3 + [vmem] * 2 + [hbm] * 2,
        out_specs=(hbm, hbm),
        scratch_shapes=[
            pltpu.VMEM((lax.axis_size("alpha") * cols_a, slots, tile), jnp.float32),
            pltpu.VMEM((2, GROUP * pairs, slots, tile), jnp.float32),
            pltpu.VMEM((pairs, slots, cols, tile), jnp.float32),
            pltpu.VMEM((GROUP * pairs, GROUP * pairs), jnp.bfloat16),
            pltpu.VMEM((GROUP * pairs, GROUP * pairs), jnp.bfloat16),
            pltpu.VMEM((pairs * tiles, tile), jnp.int32),
            pltpu.VMEM((pairs * tiles, tile), jnp.int32),
            pltpu.VMEM((tiles, cols, tile), jnp.float32),
            pltpu.SemaphoreType.DMA((len(copies),)),
            pltpu.SemaphoreType.DMA,
            pltpu.SemaphoreType.DMA,
            pltpu.SemaphoreType.DMA((2,)),
        ],
        compiler_params=pltpu.CompilerParams(vmem_limit_bytes=40 * 1024 * 1024),
        name="sigma_partial",
    )(
        *arrays,
        base,
        source,
        target,
        sign,
        vb,
        beta_offsets.reshape(pairs * tiles, tile),
        beta_sign.reshape(pairs * tiles, tile),
    )
    across = [(b, b ^ 1) for b in range(betas)]
    came = lax.ppermute(give, "beta", across)
    total = keep[:slots] + came[:slots]
    for far in (2, 1, 3):
        pairs_y = [(b, (b + far * CORES) % betas) for b in range(betas)]
        part = keep[far * slots : (far + 1) * slots] + came[far * slots : (far + 1) * slots]
        total = total + lax.ppermute(part, "beta", pairs_y)
    summed = total.transpose(0, 2, 1).reshape(rows_b, cols)
    other = lax.ppermute(summed, "ints", swap)
    return jnp.concatenate([jnp.where(first, summed, other), jnp.where(first, other, summed)], 1)


def solution(mesh):
    return jax.shard_map(
        local,
        mesh=mesh,
        in_specs=(
            P("beta", "alpha"),
            P("ints", None),
            P("ints", "alpha"),
            P("ints", "alpha"),
            P(),
            P(),
            P(),
        ),
        out_specs=P("beta", "alpha"),
        check_vma=False,
    )
```

time: 164 us -> 132 us (0.80)
  the two profiles are of different devices: /device:TPU:25 before, /device:TPU:8 now
where the time goes in v2:
time: 132 us; the launch traced here: 131 us
  waiting for transfers between devices  58.9 us (45%)
  starting transfers between devices  41.3 us (31%)
  Pallas kernels  17.6 us (13%)
  local copies, waits for them, and re-layouts  9.73 us (7%)
  other arithmetic  3.54 us (3%)
    ppermute x18, waiting for transfers between devices, shift(): return lax.ppermute(value, AXES, pairs)  29.3 us
    ppermute x18, starting transfers between devices, shift(): return lax.ppermute(value, AXES, pairs)  26.7 us
    pallas_call x1, Pallas kernels, local(): pl.pallas_call(functools.partial(kernel, tuple(copies), steps, pairs, slo...  17.6 us
    ppermute x1, waiting for transfers between devices, local(): other = lax.ppermute(summed, 'ints', swap)  15 us
    ppermute x3, waiting for transfers between devices, local(): total = total + lax.ppermute(part, 'beta', pairs_y)  11.3 us
    unnamed x18, local copies, waits for them, and re-layouts  4.55 us
    ppermute x1, starting transfers between devices, local(): v_got = lax.ppermute(integrals, 'ints', swap)  4.48 us
    ppermute x3, starting transfers between devices, local(): total = total + lax.ppermute(part, 'beta', pairs_y)  4.4 us
  transfers between devices with their start and end apart: 25, of which 12 were waited for; matrix products, arithmetic and copies ran while one was open for 6% of the time, Pallas kernels for 0%

profile of v2, /device:TPU:8, one launch (start us, length us, event | category | flops | bytes accessed | tf_op | source)
XLA Modules:
  0.0 131.3 jit_solution(3493457375381811704)
XLA Ops:
  1.2 2.0 %collective-permute-start.1 = (f32[128,4,128]{2,1,0:T(4,128)S(1)}, f32[128,4,128]{2,1,0:T(4,128)S(1)}, u32[]{:S(2)}, u32[]{:S(2)}) collective-permute-start(f32[128,4,128]{2,1,0:T(4,128)S(1)} %copy.25.refs_0_), channel_id=1, source_target_pairs={{0,16},{16,32},{32,48},{48,1},{1,17},{17,33},{33,49},{49,0},{64,80... | collective-permute-start | bytes 786440 | tf_op jit(solution)/shard_map/ppermute | solution.py:32
  3.2 4.0 %collective-permute-start = (f32[128,4,128]{2,1,0:T(4,128)S(1)}, f32[128,4,128]{2,1,0:T(4,128)S(1)}, u32[]{:S(2)}, u32[]{:S(2)}) collective-permute-start(f32[128,4,128]{2,1,0:T(4,128)S(1)} %copy.25.refs_0_), channel_id=1, source_target_pairs={{0,49},{16,0},{32,16},{48,32},{1,48},{17,1},{33,17},{49,33},{64,11... | collective-permute-start | bytes 786440 | tf_op jit(solution)/shard_map/ppermute | solution.py:32
  7.4 1.6 %collective-permute-start.10 = (f32[128,4,128]{2,1,0:T(4,128)S(1)}, f32[128,4,128]{2,1,0:T(4,128)S(1)}, u32[]{:S(2)}, u32[]{:S(2)}) collective-permute-start(f32[128,4,128]{2,1,0:T(4,128)S(1)} %copy.26.refs_10_), channel_id=1, source_target_pairs={{0,64},{16,80},{32,96},{48,112},{1,65},{17,81},{33,97},{49,113},{6... | collective-permute-start | bytes 786440 | tf_op jit(solution)/shard_map/ppermute | solution.py:32
  9.0 1.7 %collective-permute-start.9 = (f32[128,4,128]{2,1,0:T(4,128)S(1)}, f32[128,4,128]{2,1,0:T(4,128)S(1)}, u32[]{:S(2)}, u32[]{:S(2)}) collective-permute-start(f32[128,4,128]{2,1,0:T(4,128)S(1)} %copy.26.refs_10_), channel_id=1, source_target_pairs={{0,192},{16,208},{32,224},{48,240},{1,193},{17,209},{33,225},{49,2... | collective-permute-start | bytes 786440 | tf_op jit(solution)/shard_map/ppermute | solution.py:32
  10.7 4.5 %collective-permute-start.19 = (f32[16,32]{1,0:T(8,128)S(1)}, f32[16,32]{1,0:T(8,128)S(1)}, u32[]{:S(2)}, u32[]{:S(2)}) collective-permute-start(f32[16,32]{1,0:T(8,128)S(1)} %copy-done.7), channel_id=1, source_target_pairs={{0,1},{1,0},{2,3},{3,2},{4,5},{5,4},{6,7},{7,6},{8,9},{9,8},{10,11... | collective-permute-start | bytes 6152 | tf_op jit(solution)/shard_map/ppermute | solution.py:185
  17.6 3.0 %collective-permute-start.3 = (f32[256,4,128]{2,1,0:T(4,128)S(1)}, f32[256,4,128]{2,1,0:T(4,128)}, u32[]{:S(2)}, u32[]{:S(2)}) collective-permute-start(f32[256,4,128]{2,1,0:T(4,128)S(1)} %pad_maximum_fusion), channel_id=1, source_target_pairs={{0,192},{16,208},{32,224},{48,240},{1,193},{17,209},{33,225},{49,2... | collective-permute-start | bytes 1572872 | tf_op jit(solution)/shard_map/ppermute | solution.py:32
  23.9 11.8 %collective-permute-done.11.refs_13_ = f32[128,4,128]{2,1,0:T(4,128)S(1)} collective-permute-done((f32[128,4,128]{2,1,0:T(4,128)S(1)}, f32[128,4,128]{2,1,0:T(4,128)S(1)}, u32[]{:S(2)}, u32[]{:S(2)}) %collective-permute-start.11) | collective-permute-done | bytes 262176 | tf_op jit(solution)/shard_map/ppermute | solution.py:32
  35.7 2.8 %collective-permute-start.18 = (s32[2,16,128]{2,1,0:T(8,128)S(1)}, s32[2,16,128]{2,1,0:T(8,128)S(1)}, u32[]{:S(2)}, u32[]{:S(2)}) collective-permute-start(s32[2,16,128]{2,1,0:T(8,128)S(1)} %fusion.4), channel_id=1, source_target_pairs={{0,1},{1,0},{2,3},{3,2},{4,5},{5,4},{6,7},{7,6},{8,9},{9,8},{10,11... | collective-permute-start | bytes 49160 | tf_op jit(solution)/shard_map/ppermute | solution.py:184
  39.9 3.2 %collective-permute-start.12 = (f32[256,4,128]{2,1,0:T(4,128)}, f32[256,4,128]{2,1,0:T(4,128)}, u32[]{:S(2)}, u32[]{:S(2)}) collective-permute-start(f32[256,4,128]{2,1,0:T(4,128)} %pad_maximum_fusion.1), channel_id=1, source_target_pairs={{0,49},{16,0},{32,16},{48,32},{1,48},{17,1},{33,17},{49,33},{64,11... | collective-permute-start | bytes 1572872 | tf_op jit(solution)/shard_map/ppermute | solution.py:32
  45.6 2.5 %collective-permute-start.5 = (f32[256,4,128]{2,1,0:T(4,128)}, f32[256,4,128]{2,1,0:T(4,128)}, u32[]{:S(2)}, u32[]{:S(2)}) collective-permute-start(f32[256,4,128]{2,1,0:T(4,128)} %constant_dynamic-update-slice_fusion), channel_id=1, source_target_pairs={{0,192},{16,208},{32,224},{48,240},{1,193},{17,209},{33,225},{49,2... | collective-permute-start | bytes 1572872 | tf_op jit(solution)/shard_map/ppermute | solution.py:32
  49.3 1.5 %mul.53.refs_24_ = f32[256,256]{1,0:T(8,128)S(1)} reshape(f32[32,8,8,32]{3,2,1,0:T(8,128)} %broadcast_multiply_fusion) | data formatting | bytes 524288 | tf_op jit(solution)/shard_map/mul | solution.py:194
  50.9 4.7 %collective-permute-done.13.refs_15_ = f32[256,4,128]{2,1,0:T(4,128)} collective-permute-done((f32[256,4,128]{2,1,0:T(4,128)}, f32[256,4,128]{2,1,0:T(4,128)}, u32[]{:S(2)}, u32[]{:S(2)}) %collective-permute-start.13) | collective-permute-done | bytes 524320 | tf_op jit(solution)/shard_map/ppermute | solution.py:32
  56.2 3.0 %collective-permute-start.7 = (f32[256,4,128]{2,1,0:T(4,128)}, f32[256,4,128]{2,1,0:T(4,128)}, u32[]{:S(2)}, u32[]{:S(2)}) collective-permute-start(f32[256,4,128]{2,1,0:T(4,128)} %collective-permute-done.3.refs_4_), channel_id=1, source_target_pairs={{0,192},{16,208},{32,224},{48,240},{1,193},{17,209},{33,225},{49,2... | collective-permute-start | bytes 1572872 | tf_op jit(solution)/shard_map/ppermute | solution.py:32
  59.8 2.2 %collective-permute-start.8 = (f32[256,4,128]{2,1,0:T(4,128)}, f32[256,4,128]{2,1,0:T(4,128)}, u32[]{:S(2)}, u32[]{:S(2)}) collective-permute-start(f32[256,4,128]{2,1,0:T(4,128)} %collective-permute-done.6.refs_7_), channel_id=1, source_target_pairs={{0,64},{16,80},{32,96},{48,112},{1,65},{17,81},{33,97},{49,113},{6... | collective-permute-start | bytes 1572872 | tf_op jit(solution)/shard_map/ppermute | solution.py:32
  63.7 4.9 %collective-permute-done.14.refs_16_ = f32[256,4,128]{2,1,0:T(4,128)} collective-permute-done((f32[256,4,128]{2,1,0:T(4,128)}, f32[256,4,128]{2,1,0:T(4,128)}, u32[]{:S(2)}, u32[]{:S(2)}) %collective-permute-start.14) | collective-permute-done | bytes 524320 | tf_op jit(solution)/shard_map/ppermute | solution.py:32
  68.6 5.6 %collective-permute-done.16.refs_18_ = f32[256,4,128]{2,1,0:T(4,128)} collective-permute-done((f32[256,4,128]{2,1,0:T(4,128)}, f32[256,4,128]{2,1,0:T(4,128)}, u32[]{:S(2)}, u32[]{:S(2)}) %collective-permute-start.16) | collective-permute-done | bytes 524320 | tf_op jit(solution)/shard_map/ppermute | solution.py:32
  76.3 17.6 %sigma_partial.1 = (f32[16,128,128]{2,1,0:T(8,128)S(1)}, f32[16,128,128]{2,1,0:T(8,128)S(1)}) custom-call(f32[128,4,128]{2,1,0:T(4,128)S(1)} %copy.25.refs_0_, f32[128,4,128]{2,1,0:T(4,128)S(1)} %collective-permute-done.refs_1_, f32[128,4,128]{2,1,0:T(4,128)S(1)} %collective-permute-done.1.refs_2_, f32[128,4,128]{2,1,0:T(4,128)S(1)} %collective-permute-done.2.refs_3_, ...), custom_call_target="tpu_custom_call" | custom-call | tf_op jit(solution)/shard_map/sigma_partial/pallas_call | solution.py:226
  94.0 2.6 %collective-permute-done.20 = f32[16,128,128]{2,1,0:T(8,128)S(1)} collective-permute-done((f32[16,128,128]{2,1,0:T(8,128)S(1)}, f32[16,128,128]{2,1,0:T(8,128)S(1)}, u32[]{:S(2)}, u32[]{:S(2)}) %collective-permute-start.20) | collective-permute-done | bytes 1048608 | tf_op jit(solution)/shard_map/ppermute | solution.py:258
  96.7 2.4 %collective-permute-start.21 = (f32[4,128,128]{2,1,0:T(8,128)S(1)}, f32[4,128,128]{2,1,0:T(8,128)S(1)}, u32[]{:S(2)}, u32[]{:S(2)}) collective-permute-start(f32[4,128,128]{2,1,0:T(8,128)S(1)} %get-tuple-element.9), channel_id=1, source_target_pairs={{0,8},{2,10},{4,12},{6,14},{8,0},{10,2},{12,4},{14,6},{1,9},{3,11}... | collective-permute-start | bytes 786440 | tf_op jit(solution)/shard_map/ppermute | solution.py:263
  99.1 1.3 %collective-permute-start.23 = (f32[4,128,128]{2,1,0:T(8,128)S(1)}, f32[4,128,128]{2,1,0:T(8,128)S(1)}, u32[]{:S(2)}, u32[]{:S(2)}) collective-permute-start(f32[4,128,128]{2,1,0:T(8,128)S(1)} %get-tuple-element.10), channel_id=1, source_target_pairs={{0,12},{2,14},{4,0},{6,2},{8,4},{10,6},{12,8},{14,10},{1,13},{3,15... | collective-permute-start | bytes 786440 | tf_op jit(solution)/shard_map/ppermute | solution.py:263
  101.1 6.4 %collective-permute-done.21 = f32[4,128,128]{2,1,0:T(8,128)S(1)} collective-permute-done((f32[4,128,128]{2,1,0:T(8,128)S(1)}, f32[4,128,128]{2,1,0:T(8,128)S(1)}, u32[]{:S(2)}, u32[]{:S(2)}) %collective-permute-start.21) | collective-permute-done | bytes 262176 | tf_op jit(solution)/shard_map/ppermute | solution.py:263
  107.5 4.8 %collective-permute-done.23 = f32[4,128,128]{2,1,0:T(8,128)S(1)} collective-permute-done((f32[4,128,128]{2,1,0:T(8,128)S(1)}, f32[4,128,128]{2,1,0:T(8,128)S(1)}, u32[]{:S(2)}, u32[]{:S(2)}) %collective-permute-start.23) | collective-permute-done | bytes 262176 | tf_op jit(solution)/shard_map/ppermute | solution.py:263
  112.6 2.9 %collective-permute-start.24 = (f32[512,128]{1,0:T(8,128)S(1)}, f32[512,128]{1,0:T(8,128)S(1)}, u32[]{:S(2)}, u32[]{:S(2)}) collective-permute-start(f32[512,128]{1,0:T(8,128)S(1)} %bitcast.19), channel_id=1, source_target_pairs={{0,1},{1,0},{2,3},{3,2},{4,5},{5,4},{6,7},{7,6},{8,9},{9,8},{10,11... | collective-permute-start | bytes 786440 | tf_op jit(solution)/shard_map/ppermute | solution.py:265
  115.5 15.0 %collective-permute-done.24 = f32[512,128]{1,0:T(8,128)S(1)} collective-permute-done((f32[512,128]{1,0:T(8,128)S(1)}, f32[512,128]{1,0:T(8,128)S(1)}, u32[]{:S(2)}, u32[]{:S(2)}) %collective-permute-start.24) | collective-permute-done | bytes 262176 | tf_op jit(solution)/shard_map/ppermute | solution.py:265
  (79 shorter events, 19.2 us)
Async XLA Ops:
  1.2 20.4 %collective-permute-start.1 = (f32[128,4,128]{2,1,0:T(4,128)S(1)}, f32[128,4,128]{2,1,0:T(4,128)S(1)}, u32[]{:S(2)}, u32[]{:S(2)}) collective-permute-start(f32[128,4,128]{2,1,0:T(4,128)S(1)} %copy.25.refs_0_), channel_id=1, source_target_pairs={{0,16},{16,32},{32,48},{48,1},{1,17},{17,33},{33,49},{49,0},{64,80... | collective-permute-start | bytes 786440 | tf_op jit(solution)/shard_map/ppermute | solution.py:32
  3.2 13.9 %collective-permute-start = (f32[128,4,128]{2,1,0:T(4,128)S(1)}, f32[128,4,128]{2,1,0:T(4,128)S(1)}, u32[]{:S(2)}, u32[]{:S(2)}) collective-permute-start(f32[128,4,128]{2,1,0:T(4,128)S(1)} %copy.25.refs_0_), channel_id=1, source_target_pairs={{0,49},{16,0},{32,16},{48,32},{1,48},{17,1},{33,17},{49,33},{64,11... | collective-permute-start | bytes 786440 | tf_op jit(solution)/shard_map/ppermute | solution.py:32
  7.4 10.2 %collective-permute-start.10 = (f32[128,4,128]{2,1,0:T(4,128)S(1)}, f32[128,4,128]{2,1,0:T(4,128)S(1)}, u32[]{:S(2)}, u32[]{:S(2)}) collective-permute-start(f32[128,4,128]{2,1,0:T(4,128)S(1)} %copy.26.refs_10_), channel_id=1, source_target_pairs={{0,64},{16,80},{32,96},{48,112},{1,65},{17,81},{33,97},{49,113},{6... | collective-permute-start | bytes 786440 | tf_op jit(solution)/shard_map/ppermute | solution.py:32
  9.0 11.6 %collective-permute-start.9 = (f32[128,4,128]{2,1,0:T(4,128)S(1)}, f32[128,4,128]{2,1,0:T(4,128)S(1)}, u32[]{:S(2)}, u32[]{:S(2)}) collective-permute-start(f32[128,4,128]{2,1,0:T(4,128)S(1)} %copy.26.refs_10_), channel_id=1, source_target_pairs={{0,192},{16,208},{32,224},{48,240},{1,193},{17,209},{33,225},{49,2... | collective-permute-start | bytes 786440 | tf_op jit(solution)/shard_map/ppermute | solution.py:32
  10.7 29.2 %collective-permute-start.19 = (f32[16,32]{1,0:T(8,128)S(1)}, f32[16,32]{1,0:T(8,128)S(1)}, u32[]{:S(2)}, u32[]{:S(2)}) collective-permute-start(f32[16,32]{1,0:T(8,128)S(1)} %copy-done.7), channel_id=1, source_target_pairs={{0,1},{1,0},{2,3},{3,2},{4,5},{5,4},{6,7},{7,6},{8,9},{9,8},{10,11... | collective-permute-start | bytes 6152 | tf_op jit(solution)/shard_map/ppermute | solution.py:185
  17.3 27.5 %collective-permute-start.4 = (f32[256,4,128]{2,1,0:T(4,128)S(1)}, f32[256,4,128]{2,1,0:T(4,128)S(1)}, u32[]{:S(2)}, u32[]{:S(2)}) collective-permute-start(f32[256,4,128]{2,1,0:T(4,128)S(1)} %pad_maximum_fusion), channel_id=1, source_target_pairs={{0,64},{16,80},{32,96},{48,112},{1,65},{17,81},{33,97},{49,113},{6... | collective-permute-start | bytes 1572872 | tf_op jit(solution)/shard_map/ppermute | solution.py:32
  17.6 30.5 %collective-permute-start.3 = (f32[256,4,128]{2,1,0:T(4,128)S(1)}, f32[256,4,128]{2,1,0:T(4,128)}, u32[]{:S(2)}, u32[]{:S(2)}) collective-permute-start(f32[256,4,128]{2,1,0:T(4,128)S(1)} %pad_maximum_fusion), channel_id=1, source_target_pairs={{0,192},{16,208},{32,224},{48,240},{1,193},{17,209},{33,225},{49,2... | collective-permute-start | bytes 1572872 | tf_op jit(solution)/shard_map/ppermute | solution.py:32
  20.6 15.1 %collective-permute-start.11 = (f32[128,4,128]{2,1,0:T(4,128)S(1)}, f32[128,4,128]{2,1,0:T(4,128)S(1)}, u32[]{:S(2)}, u32[]{:S(2)}) collective-permute-start(f32[128,4,128]{2,1,0:T(4,128)S(1)} %collective-permute-done.9.refs_11_), channel_id=1, source_target_pairs={{0,192},{16,208},{32,224},{48,240},{1,193},{17,209},{33,225},{49,2... | collective-permute-start | bytes 786440 | tf_op jit(solution)/shard_map/ppermute | solution.py:32
  21.6 17.6 %collective-permute-start.2 = (f32[128,4,128]{2,1,0:T(4,128)S(1)}, f32[128,4,128]{2,1,0:T(4,128)S(1)}, u32[]{:S(2)}, u32[]{:S(2)}) collective-permute-start(f32[128,4,128]{2,1,0:T(4,128)S(1)} %collective-permute-done.refs_1_), channel_id=1, source_target_pairs={{0,49},{16,0},{32,16},{48,32},{1,48},{17,1},{33,17},{49,33},{64,11... | collective-permute-start | bytes 786440 | tf_op jit(solution)/shard_map/ppermute | solution.py:32
  35.7 8.1 %collective-permute-start.18 = (s32[2,16,128]{2,1,0:T(8,128)S(1)}, s32[2,16,128]{2,1,0:T(8,128)S(1)}, u32[]{:S(2)}, u32[]{:S(2)}) collective-permute-start(s32[2,16,128]{2,1,0:T(8,128)S(1)} %fusion.4), channel_id=1, source_target_pairs={{0,1},{1,0},{2,3},{3,2},{4,5},{5,4},{6,7},{7,6},{8,9},{9,8},{10,11... | collective-permute-start | bytes 49160 | tf_op jit(solution)/shard_map/ppermute | solution.py:184
  39.2 16.4 %collective-permute-start.13 = (f32[256,4,128]{2,1,0:T(4,128)}, f32[256,4,128]{2,1,0:T(4,128)}, u32[]{:S(2)}, u32[]{:S(2)}) collective-permute-start(f32[256,4,128]{2,1,0:T(4,128)} %pad_maximum_fusion.1), channel_id=1, source_target_pairs={{0,16},{16,32},{32,48},{48,1},{1,17},{17,33},{33,49},{49,0},{64,80... | collective-permute-start | bytes 1572872 | tf_op jit(solution)/shard_map/ppermute | solution.py:32
  39.9 16.3 %collective-permute-start.12 = (f32[256,4,128]{2,1,0:T(4,128)}, f32[256,4,128]{2,1,0:T(4,128)}, u32[]{:S(2)}, u32[]{:S(2)}) collective-permute-start(f32[256,4,128]{2,1,0:T(4,128)} %pad_maximum_fusion.1), channel_id=1, source_target_pairs={{0,49},{16,0},{32,16},{48,32},{1,48},{17,1},{33,17},{49,33},{64,11... | collective-permute-start | bytes 1572872 | tf_op jit(solution)/shard_map/ppermute | solution.py:32
  43.8 15.4 %collective-permute-start.6 = (f32[256,4,128]{2,1,0:T(4,128)}, f32[256,4,128]{2,1,0:T(4,128)}, u32[]{:S(2)}, u32[]{:S(2)}) collective-permute-start(f32[256,4,128]{2,1,0:T(4,128)} %constant_dynamic-update-slice_fusion), channel_id=1, source_target_pairs={{0,64},{16,80},{32,96},{48,112},{1,65},{17,81},{33,97},{49,113},{6... | collective-permute-start | bytes 1572872 | tf_op jit(solution)/shard_map/ppermute | solution.py:32
  45.6 14.2 %collective-permute-start.5 = (f32[256,4,128]{2,1,0:T(4,128)}, f32[256,4,128]{2,1,0:T(4,128)}, u32[]{:S(2)}, u32[]{:S(2)}) collective-permute-start(f32[256,4,128]{2,1,0:T(4,128)} %constant_dynamic-update-slice_fusion), channel_id=1, source_target_pairs={{0,192},{16,208},{32,224},{48,240},{1,193},{17,209},{33,225},{49,2... | collective-permute-start | bytes 1572872 | tf_op jit(solution)/shard_map/ppermute | solution.py:32
  48.1 15.2 %collective-permute-start.15 = (f32[256,4,128]{2,1,0:T(4,128)}, f32[256,4,128]{2,1,0:T(4,128)}, u32[]{:S(2)}, u32[]{:S(2)}) collective-permute-start(f32[256,4,128]{2,1,0:T(4,128)} %constant_dynamic-update-slice_fusion.2), channel_id=1, source_target_pairs={{0,16},{16,32},{32,48},{48,1},{1,17},{17,33},{33,49},{49,0},{64,80... | collective-permute-start | bytes 1572872 | tf_op jit(solution)/shard_map/ppermute | solution.py:32
  55.6 13.0 %collective-permute-start.14 = (f32[256,4,128]{2,1,0:T(4,128)}, f32[256,4,128]{2,1,0:T(4,128)}, u32[]{:S(2)}, u32[]{:S(2)}) collective-permute-start(f32[256,4,128]{2,1,0:T(4,128)} %constant_dynamic-update-slice_fusion.2), channel_id=1, source_target_pairs={{0,49},{16,0},{32,16},{48,32},{1,48},{17,1},{33,17},{49,33},{64,11... | collective-permute-start | bytes 1572872 | tf_op jit(solution)/shard_map/ppermute | solution.py:32
  56.2 12.4 %collective-permute-start.7 = (f32[256,4,128]{2,1,0:T(4,128)}, f32[256,4,128]{2,1,0:T(4,128)}, u32[]{:S(2)}, u32[]{:S(2)}) collective-permute-start(f32[256,4,128]{2,1,0:T(4,128)} %collective-permute-done.3.refs_4_), channel_id=1, source_target_pairs={{0,192},{16,208},{32,224},{48,240},{1,193},{17,209},{33,225},{49,2... | collective-permute-start | bytes 1572872 | tf_op jit(solution)/shard_map/ppermute | solution.py:32
  59.2 15.0 %collective-permute-start.16 = (f32[256,4,128]{2,1,0:T(4,128)}, f32[256,4,128]{2,1,0:T(4,128)}, u32[]{:S(2)}, u32[]{:S(2)}) collective-permute-start(f32[256,4,128]{2,1,0:T(4,128)} %collective-permute-done.12.refs_14_), channel_id=1, source_target_pairs={{0,49},{16,0},{32,16},{48,32},{1,48},{17,1},{33,17},{49,33},{64,11... | collective-permute-start | bytes 1572872 | tf_op jit(solution)/shard_map/ppermute | solution.py:32
  59.8 14.5 %collective-permute-start.8 = (f32[256,4,128]{2,1,0:T(4,128)}, f32[256,4,128]{2,1,0:T(4,128)}, u32[]{:S(2)}, u32[]{:S(2)}) collective-permute-start(f32[256,4,128]{2,1,0:T(4,128)} %collective-permute-done.6.refs_7_), channel_id=1, source_target_pairs={{0,64},{16,80},{32,96},{48,112},{1,65},{17,81},{33,97},{49,113},{6... | collective-permute-start | bytes 1572872 | tf_op jit(solution)/shard_map/ppermute | solution.py:32
  63.3 11.9 %collective-permute-start.17 = (f32[256,4,128]{2,1,0:T(4,128)}, f32[256,4,128]{2,1,0:T(4,128)}, u32[]{:S(2)}, u32[]{:S(2)}) collective-permute-start(f32[256,4,128]{2,1,0:T(4,128)} %collective-permute-done.15.refs_17_), channel_id=1, source_target_pairs={{0,16},{16,32},{32,48},{48,1},{1,17},{17,33},{33,49},{49,0},{64,80... | collective-permute-start | bytes 1572872 | tf_op jit(solution)/shard_map/ppermute | solution.py:32
  96.7 10.8 %collective-permute-start.21 = (f32[4,128,128]{2,1,0:T(8,128)S(1)}, f32[4,128,128]{2,1,0:T(8,128)S(1)}, u32[]{:S(2)}, u32[]{:S(2)}) collective-permute-start(f32[4,128,128]{2,1,0:T(8,128)S(1)} %get-tuple-element.9), channel_id=1, source_target_pairs={{0,8},{2,10},{4,12},{6,14},{8,0},{10,2},{12,4},{14,6},{1,9},{3,11}... | collective-permute-start | bytes 786440 | tf_op jit(solution)/shard_map/ppermute | solution.py:263
  99.1 13.2 %collective-permute-start.23 = (f32[4,128,128]{2,1,0:T(8,128)S(1)}, f32[4,128,128]{2,1,0:T(8,128)S(1)}, u32[]{:S(2)}, u32[]{:S(2)}) collective-permute-start(f32[4,128,128]{2,1,0:T(8,128)S(1)} %get-tuple-element.10), channel_id=1, source_target_pairs={{0,12},{2,14},{4,0},{6,2},{8,4},{10,6},{12,8},{14,10},{1,13},{3,15... | collective-permute-start | bytes 786440 | tf_op jit(solution)/shard_map/ppermute | solution.py:263
  100.4 12.0 %collective-permute-start.22 = (f32[4,128,128]{2,1,0:T(8,128)S(1)}, f32[4,128,128]{2,1,0:T(8,128)S(1)}, u32[]{:S(2)}, u32[]{:S(2)}) collective-permute-start(f32[4,128,128]{2,1,0:T(8,128)S(1)} %get-tuple-element.11), channel_id=1, source_target_pairs={{0,4},{2,6},{4,8},{6,10},{8,12},{10,14},{12,0},{14,2},{1,5},{3,7},... | collective-permute-start | bytes 786440 | tf_op jit(solution)/shard_map/ppermute | solution.py:263
  112.6 17.8 %collective-permute-start.24 = (f32[512,128]{1,0:T(8,128)S(1)}, f32[512,128]{1,0:T(8,128)S(1)}, u32[]{:S(2)}, u32[]{:S(2)}) collective-permute-start(f32[512,128]{1,0:T(8,128)S(1)} %bitcast.19), channel_id=1, source_target_pairs={{0,1},{1,0},{2,3},{3,2},{4,5},{5,4},{6,7},{7,6},{8,9},{9,8},{10,11... | collective-permute-start | bytes 786440 | tf_op jit(solution)/shard_map/ppermute | solution.py:265
  (9 other events, 50.5 us)

commit v3 on v0

v3 whole, which is shorter than its diff:
```python
import functools

import jax
import jax.numpy as jnp
from jax import lax
from jax.experimental import pallas as pl
from jax.experimental.pallas import tpu as pltpu
from jax.sharding import PartitionSpec as P

LANES = 128
GROUP = 8
RING = 4
CORES = 2
CHUNKS = 2
UNROLL = 4
FLIGHT = 5
AXES = ("alpha", "beta", "ints")


def device(x, z, y, core):
    ints = lax.axis_size("ints")
    x, z = x % RING, z % (RING * ints)
    alpha = x * RING + z % RING
    return (alpha * lax.axis_size("beta") + y * CORES + core) * ints + z // RING


def move(value, axis, step):
    pairs = []
    for x in range(lax.axis_size("alpha") // RING):
        for z in range(RING * lax.axis_size("ints")):
            for y in range(lax.axis_size("beta") // CORES):
                for core in range(CORES):
                    dx, dz = (step, 0) if axis != core else (0, step)
                    pairs.append((device(x, z, y, core), device(x + dx, z + dz, y, core)))
    return lax.ppermute(value, AXES, pairs)


def spread(block, packet):
    held = {"own": block}
    order = []

    def send(name, source, axis, step):
        value = held[source]
        if len(order) >= FLIGHT:
            value, _ = lax.optimization_barrier((value, held[order[-FLIGHT]]))
        held[name] = move(value, axis, step)
        order.append(name)

    send("ahead", "own", 0, -1)
    send("behind", "own", 0, 1)
    send("own_ahead", "own", 1, -1)
    send("own_behind", "own", 1, 1)
    send("over", "ahead", 0, -1)
    send("behind_behind", "behind", 1, 1)
    send("ahead_ahead", "ahead", 1, -1)
    send("ahead_behind", "ahead", 1, 1)
    send("behind_ahead", "behind", 1, -1)
    packet, _ = lax.optimization_barrier((packet, held[order[-FLIGHT]]))
    held["packet"] = lax.ppermute(packet, "ints", [(0, 1), (1, 0)])
    order.append("packet")
    send("over_behind", "over", 1, 1)
    send("over_ahead", "over", 1, -1)
    send("own_over", "own_behind", 1, 1)
    send("ahead_over", "ahead_ahead", 1, -1)
    send("behind_over", "behind_behind", 1, 1)
    send("over_over", "over_behind", 1, 1)
    along = {"own": 0, "ahead": 1, "over": 2, "behind": 3}
    pieces = [(0, at, held[name]) for name, at in along.items()]
    for name, at in along.items():
        pieces += [(1, at, held[name + "_ahead"]), (3, at, held[name + "_behind"]), (2, at, held[name + "_over"])]
    return pieces, held["packet"]


def assemble(copies, base_ref, *refs):
    arrays, table, sems = refs[:-2], refs[-2], refs[-1]
    dmas = []
    for n, slot in enumerate(copies):
        rows = arrays[n].shape[0]
        dmas.append(pltpu.make_async_copy(arrays[n], table.at[pl.ds(base_ref[slot], rows)], sems.at[n]))
    for dma in dmas:
        dma.start()
    for dma in dmas:
        dma.wait()


def kernel(
    steps, pairs, slots,
    table, src_ref, tgt_ref, sign_ref, vb_ref, off_ref, bs_ref, keep_hbm, give_hbm,
    g_ref, y_ref, vhi_ref, vlo_ref, acc_ref, sem_out,
):
    v = vb_ref[...]
    high = v.astype(jnp.bfloat16)
    vhi_ref[...] = high
    vlo_ref[...] = (v - high.astype(jnp.float32)).astype(jnp.bfloat16)
    acc_ref[...] = jnp.zeros_like(acc_ref)
    rows = GROUP * pairs

    def fetch(step, buffer):
        for r in range(rows):
            g_ref[buffer, r] = table[src_ref[step * rows + r]]

    def mix(step, buffer):
        flat = g_ref.at[buffer].reshape(rows * slots, LANES)
        sign = sign_ref[pl.ds(step, 1), :].astype(jnp.bfloat16)
        left_hi = vhi_ref[...] * sign
        left_lo = vlo_ref[...] * sign
        g = jnp.concatenate([flat[pl.ds(q, rows, stride=slots), :] for q in range(slots)], 1)
        hi = g.astype(jnp.bfloat16)
        lo = (g - hi.astype(jnp.float32)).astype(jnp.bfloat16)
        got = jnp.dot(
            jnp.concatenate([left_hi, left_lo, left_hi], 1),
            jnp.concatenate([hi, hi, lo], 0),
            preferred_element_type=jnp.float32,
        )
        for q in range(slots):
            part = got[:, q * LANES : (q + 1) * LANES]
            y_ref[:, q, pl.ds(step * GROUP, GROUP), :] = part.reshape(pairs, GROUP, LANES)

    fetch(0, 0)

    def two(half, carry):
        step = half * 2
        fetch(step + 1, 1)
        mix(step, 0)
        fetch(jnp.minimum(step + 2, steps - 1), 0)
        mix(step + 1, 1)
        return carry

    lax.fori_loop(0, steps // 2, two, 0)
    lines = lax.broadcasted_iota(jnp.int32, (LANES, LANES), 0)
    tiles = acc_ref.shape[0]

    def place(pair):
        found = []
        for q in range(slots):
            t = tgt_ref[pair * slots + q]
            spot = tgt_ref[(pairs + pair) * slots + q]
            off = off_ref[pl.ds(pair * tiles + t, 1), :]
            sgn = bs_ref[pl.ds(pair * tiles + t, 1), :].astype(jnp.float32)
            hot = jnp.where(lines == off, sgn, 0.0).astype(jnp.bfloat16)
            y = y_ref[pair, q]
            hi = y.astype(jnp.bfloat16)
            lo = (y - hi.astype(jnp.float32)).astype(jnp.bfloat16)
            left = jnp.concatenate([hi, lo], 1)
            right = jnp.concatenate([hot, hot], 0)
            found.append((spot, jnp.dot(left, right, preferred_element_type=jnp.float32)))
        for spot, value in found:
            acc_ref[spot] += value

    def some_pairs(part, carry):
        for n in range(UNROLL):
            place(part * UNROLL + n)
        return carry

    lax.fori_loop(0, pairs // UNROLL, some_pairs, 0)
    half = tiles // 2
    store_give = pltpu.make_async_copy(acc_ref.at[pl.ds(half, half)], give_hbm, sem_out.at[0])
    store_keep = pltpu.make_async_copy(acc_ref.at[pl.ds(0, half)], keep_hbm, sem_out.at[1])
    store_give.start()
    store_keep.start()
    store_give.wait()
    store_keep.wait()


def local(ci_vector, integrals, alpha_source, alpha_sign, beta_tiles, beta_offsets, beta_sign):
    rows_b, cols_a = ci_vector.shape
    pairs, tiles, tile = beta_offsets.shape
    slots = rows_b // tile
    ints = lax.axis_size("ints")
    mine = lax.axis_index("ints")
    cols = cols_a // ints
    alpha = lax.axis_index("alpha")
    x, z = alpha // RING, alpha % RING

    beta = lax.axis_index("beta")
    betas = lax.axis_size("beta")
    rings = betas // CORES
    y, core = beta // CORES, beta % CORES

    columns = ci_vector.T.reshape(cols_a, slots, tile)

    swap = [(0, 1), (1, 0)]
    first = mine == 0
    share = integrals.shape[0]
    both = jnp.stack([alpha_source, alpha_sign]).astype(jnp.float32)
    keep = lax.dynamic_slice_in_dim(both, mine * cols, cols, 2)
    give = lax.dynamic_slice_in_dim(both, (1 - mine) * cols, cols, 2)
    packet = jnp.concatenate([give.reshape(2 * share, cols), jnp.pad(integrals, ((0, 0), (0, cols - pairs)))], 0)
    pieces, packet = spread(columns, packet)
    got = packet[: 2 * share].reshape(2, share, cols)
    v_got = packet[2 * share :, :pairs]
    full = jnp.concatenate([jnp.where(first, keep, got), jnp.where(first, got, keep)], 1)
    v = jnp.concatenate([jnp.where(first, integrals, v_got), jnp.where(first, v_got, integrals)], 0)
    flat = full.transpose(0, 2, 1).reshape(2, cols * pairs)
    source = flat[0].astype(jnp.int32)
    steps = cols // GROUP
    sign = flat[1].reshape(steps, GROUP * pairs)
    eye = jnp.eye(GROUP, dtype=jnp.float32)
    vb = (v.T[:, None, None, :] * eye[None, :, :, None]).reshape(pairs * GROUP, GROUP * pairs)

    wanted = beta * slots + jnp.arange(slots, dtype=jnp.int32)
    hit = beta_tiles[:, :, None] == wanted[None, None, :]
    target = jnp.sum(jnp.where(hit, jnp.arange(tiles, dtype=jnp.int32)[None, :, None], 0), axis=1).reshape(-1)
    owner = target // slots
    away = (owner // CORES - y) % rings
    spot = ((owner % CORES) ^ core) * (tiles // CORES) + away * slots + target % slots
    target = jnp.concatenate([target, spot])

    arrays = [array for _, _, array in pieces]
    copies = [on_one * RING + on_zero for on_one, on_zero, _ in pieces]
    d = jnp.arange(RING * RING, dtype=jnp.int32)
    dx = jnp.where(core == 0, d // RING, d % RING)
    dz = jnp.where(core == 0, d % RING, d // RING)
    base = (((x + dx) % RING) * RING + (z + dz) % RING) * cols_a

    smem = pl.BlockSpec(memory_space=pltpu.SMEM)
    vmem = pl.BlockSpec(memory_space=pltpu.VMEM)
    hbm = pl.BlockSpec(memory_space=pl.ANY)
    table = pl.pallas_call(
        functools.partial(assemble, tuple(copies)),
        out_shape=jax.ShapeDtypeStruct((lax.axis_size("alpha") * cols_a, slots, tile), jnp.float32),
        in_specs=[smem] + [hbm] * len(arrays),
        out_specs=vmem,
        scratch_shapes=[pltpu.SemaphoreType.DMA((len(copies),))],
        compiler_params=pltpu.CompilerParams(vmem_limit_bytes=12 * 1024 * 1024),
        name="assemble",
    )(base, *arrays)
    width = cols // CHUNKS
    offsets = beta_offsets.reshape(pairs * tiles, tile)
    signs = beta_sign.reshape(pairs * tiles, tile)
    across = [(b, b ^ 1) for b in range(betas)]
    half = jax.ShapeDtypeStruct((tiles // CORES, width, tile), jnp.float32)
    part_steps = steps // CHUNKS
    sums = []
    for chunk in range(CHUNKS):
        keep, give = pl.pallas_call(
            functools.partial(kernel, part_steps, pairs, slots),
            out_shape=(half, half),
            in_specs=[vmem] + [smem] * 2 + [vmem] * 4,
            out_specs=(hbm, hbm),
            scratch_shapes=[
                pltpu.VMEM((2, GROUP * pairs, slots, tile), jnp.float32),
                pltpu.VMEM((pairs, slots, width, tile), jnp.float32),
                pltpu.VMEM((GROUP * pairs, GROUP * pairs), jnp.bfloat16),
                pltpu.VMEM((GROUP * pairs, GROUP * pairs), jnp.bfloat16),
                pltpu.VMEM((tiles, width, tile), jnp.float32),
                pltpu.SemaphoreType.DMA((2,)),
            ],
            compiler_params=pltpu.CompilerParams(vmem_limit_bytes=12 * 1024 * 1024),
            cost_estimate=pl.CostEstimate(flops=4 * 10**9, bytes_accessed=2**23, transcendentals=0),
            name="sigma_partial",
        )(
            table,
            lax.slice_in_dim(source, chunk * width * pairs, (chunk + 1) * width * pairs),
            target,
            lax.slice_in_dim(sign, chunk * part_steps, (chunk + 1) * part_steps),
            vb,
            offsets,
            signs,
        )
        came = lax.ppermute(give, "beta", across)
        total = keep[:slots] + came[:slots]
        for far in (2, 1, 3):
            pairs_y = [(b, (b + far * CORES) % betas) for b in range(betas)]
            part = keep[far * slots : (far + 1) * slots] + came[far * slots : (far + 1) * slots]
            total = total + lax.ppermute(part, "beta", pairs_y)
        sums.append((total, lax.ppermute(total, "ints", swap)))
    mine_all = jnp.concatenate([m for m, _ in sums], 1)
    other_all = jnp.concatenate([o for _, o in sums], 1)
    joined = jnp.concatenate([jnp.where(first, mine_all, other_all), jnp.where(first, other_all, mine_all)], 1)
    return joined.transpose(0, 2, 1).reshape(rows_b, cols_a)


def solution(mesh):
    return jax.shard_map(
        local,
        mesh=mesh,
        in_specs=(
            P("beta", "alpha"),
            P("ints", None),
            P("ints", "alpha"),
            P("ints", "alpha"),
            P(),
            P(),
            P(),
        ),
        out_specs=P("beta", "alpha"),
        check_vma=False,
    )
```

time: 1780 us -> 120 us (0.07)
  loops' own time: 587 us -> 0 us
  local copies, waits for them, and re-layouts: 542 us -> 6.81 us
  other arithmetic: 319 us -> 4.6 us
  waiting for transfers between devices: 282 us -> 48.9 us
  starting transfers between devices: 0.09 us -> 39.1 us
  Pallas kernels: 0 us -> 19.3 us
  matrix products: 18.2 us -> 0 us
    another operation x1 -> x0, loops' own time: 587 us -> none  [local(): lax.fori_loop(0, local_pairs * my_tiles, step, zeros)]
    dynamic_slice x384 -> x1, local copies, waits for them, and re-layouts: 407 us -> 0.01 us  [local(): give = lax.dynamic_slice_in_dim(both, (1 - mine) * cols, cols, 2)]
    dynamic_update_slice x128 -> x0, other arithmetic: 213 us -> none  [step(): return lax.dynamic_update_slice_in_dim(term, old + values, safe * tile, 0)]
    all_gather x1 -> x0, waiting for transfers between devices: 186 us -> none  [local(): columns = lax.all_gather(ci_vector, 'alpha', axis=1, tiled=True)]
    gather x130 -> x0, local copies, waits for them, and re-layouts: 128 us -> none  [the longest x128 96.6 us: step(): jnp.take(plane, slot * tile + offsets, axis=0) * (signs * inside)[:, None]]
    and x129 -> x0, other arithmetic: 91.1 us -> none  [the longest x128 90.4 us: step(): jnp.take(plane, slot * tile + offsets, axis=0) * (signs * inside)[:, None]]
    psum x1 -> x0, waiting for transfers between devices: 60.5 us -> none  [local(): return lax.psum(partial_sigma, 'ints')]
    ppermute x0 -> x26, waiting for transfers between devices: none -> 48.9 us  [the longest x15 34 us: move(): return lax.ppermute(value, AXES, pairs)]
  transfers between devices with their start and end apart: 3 -> 26, of which waited for: 3 -> 11; matrix products, arithmetic and copies ran while one was open for 0% -> 8% of each run, Pallas kernels for 0% -> 7%
where the time goes in v3:
time: 120 us; the launch traced here: 119 us
  waiting for transfers between devices  48.9 us (41%)
  starting transfers between devices  39.1 us (33%)
  Pallas kernels  19.3 us (16%)
  local copies, waits for them, and re-layouts  6.81 us (6%)
  other arithmetic  4.6 us (4%)
    ppermute x15, waiting for transfers between devices, move(): return lax.ppermute(value, AXES, pairs)  34 us
    ppermute x15, starting transfers between devices, move(): return lax.ppermute(value, AXES, pairs)  25.1 us
    pallas_call x2, Pallas kernels, local(): pl.pallas_call(functools.partial(kernel, part_steps, pairs, slots), out_s...  15.9 us
    ppermute x2, waiting for transfers between devices, local(): sums.append((total, lax.ppermute(total, 'ints', swap)))  10 us
    ppermute x6, starting transfers between devices, local(): total = total + lax.ppermute(part, 'beta', pairs_y)  8.52 us
    ppermute x6, waiting for transfers between devices, local(): total = total + lax.ppermute(part, 'beta', pairs_y)  4.87 us
    ppermute x2, starting transfers between devices, local(): sums.append((total, lax.ppermute(total, 'ints', swap)))  4.69 us
    pallas_call x1, Pallas kernels, local(): pl.pallas_call(functools.partial(assemble, tuple(copies)), out_shape=jax....  3.37 us
  transfers between devices with their start and end apart: 26, of which 11 were waited for; matrix products, arithmetic and copies ran while one was open for 8% of the time, Pallas kernels for 7%

profile of v3, /device:TPU:8, one launch (start us, length us, event | category | flops | bytes accessed | tf_op | source)
XLA Modules:
  0.0 118.9 jit_solution(843039405431036097)
XLA Ops:
  1.3 5.9 %collective-permute-start = (f32[256,4,128]{2,1,0:T(4,128)S(1)}, f32[256,4,128]{2,1,0:T(4,128)S(1)}, u32[]{:S(2)}, u32[]{:S(2)}) collective-permute-start(f32[256,4,128]{2,1,0:T(4,128)S(1)} %copy.27.refs_0_), channel_id=1, source_target_pairs={{0,49},{2,194},{4,53},{6,198},{8,57},{10,202},{12,61},{14,206},{16... | collective-permute-start | bytes 1572872 | tf_op jit(solution)/shard_map/ppermute | solution.py:35
  11.6 6.5 %collective-permute-done.refs_1_ = f32[256,4,128]{2,1,0:T(4,128)S(1)} collective-permute-done((f32[256,4,128]{2,1,0:T(4,128)S(1)}, f32[256,4,128]{2,1,0:T(4,128)S(1)}, u32[]{:S(2)}, u32[]{:S(2)}) %collective-permute-start) | collective-permute-done | bytes 524320 | tf_op jit(solution)/shard_map/ppermute | solution.py:35
  18.1 3.7 %collective-permute-start.1 = (f32[256,4,128]{2,1,0:T(4,128)S(1)}, f32[256,4,128]{2,1,0:T(4,128)S(1)}, u32[]{:S(2)}, u32[]{:S(2)}) collective-permute-start(f32[256,4,128]{2,1,0:T(4,128)S(1)} %collective-permute-done.refs_1_), channel_id=1, source_target_pairs={{0,49},{2,194},{4,53},{6,198},{8,57},{10,202},{12,61},{14,206},{16... | collective-permute-start | bytes 1572872 | tf_op jit(solution)/shard_map/ppermute | solution.py:35
  21.8 2.6 %collective-permute-start.11 = (f32[256,4,128]{2,1,0:T(4,128)S(1)}, f32[256,4,128]{2,1,0:T(4,128)}, u32[]{:S(2)}, u32[]{:S(2)}) collective-permute-start(f32[256,4,128]{2,1,0:T(4,128)S(1)} %collective-permute-done.2.refs_3_), channel_id=1, source_target_pairs={{0,64},{2,18},{4,68},{6,22},{8,72},{10,26},{12,76},{14,30},{16,80}... | collective-permute-start | bytes 1572872 | tf_op jit(solution)/shard_map/ppermute | solution.py:35
  26.0 2.0 %collective-permute-start.8 = (f32[256,4,128]{2,1,0:T(4,128)S(1)}, f32[256,4,128]{2,1,0:T(4,128)}, u32[]{:S(2)}, u32[]{:S(2)}) collective-permute-start(f32[256,4,128]{2,1,0:T(4,128)S(1)} %collective-permute-done.2.refs_3_), channel_id=1, source_target_pairs={{0,192},{2,51},{4,196},{6,55},{8,200},{10,59},{12,204},{14,63},{16... | collective-permute-start | bytes 1572872 | tf_op jit(solution)/shard_map/ppermute | solution.py:35
  29.4 4.9 %collective-permute-done.1.refs_2_ = f32[256,4,128]{2,1,0:T(4,128)S(1)} collective-permute-done((f32[256,4,128]{2,1,0:T(4,128)S(1)}, f32[256,4,128]{2,1,0:T(4,128)S(1)}, u32[]{:S(2)}, u32[]{:S(2)}) %collective-permute-start.1) | collective-permute-done | bytes 524320 | tf_op jit(solution)/shard_map/ppermute | solution.py:35
  36.3 3.0 %collective-permute-done.8.refs_13_ = f32[256,4,128]{2,1,0:T(4,128)} collective-permute-done((f32[256,4,128]{2,1,0:T(4,128)S(1)}, f32[256,4,128]{2,1,0:T(4,128)}, u32[]{:S(2)}, u32[]{:S(2)}) %collective-permute-start.8) | collective-permute-done | bytes 524320 | tf_op jit(solution)/shard_map/ppermute | solution.py:35
  39.3 2.8 %collective-permute-start.9 = (f32[256,4,128]{2,1,0:T(4,128)}, f32[256,4,128]{2,1,0:T(4,128)}, u32[]{:S(2)}, u32[]{:S(2)}) collective-permute-start(f32[256,4,128]{2,1,0:T(4,128)} %collective-permute-done.7.refs_7_), channel_id=1, source_target_pairs={{0,192},{2,51},{4,196},{6,55},{8,200},{10,59},{12,204},{14,63},{16... | collective-permute-start | bytes 1572872 | tf_op jit(solution)/shard_map/ppermute | solution.py:35
  42.1 3.2 %collective-permute-start.10 = (f32[256,4,128]{2,1,0:T(4,128)S(1)}, f32[256,4,128]{2,1,0:T(4,128)}, u32[]{:S(2)}, u32[]{:S(2)}) collective-permute-start(f32[256,4,128]{2,1,0:T(4,128)S(1)} %collective-permute-done.1.refs_2_), channel_id=1, source_target_pairs={{0,192},{2,51},{4,196},{6,55},{8,200},{10,59},{12,204},{14,63},{16... | collective-permute-start | bytes 1572872 | tf_op jit(solution)/shard_map/ppermute | solution.py:35
  45.9 6.6 %collective-permute-done.12.refs_11_ = f32[256,4,128]{2,1,0:T(4,128)} collective-permute-done((f32[256,4,128]{2,1,0:T(4,128)S(1)}, f32[256,4,128]{2,1,0:T(4,128)}, u32[]{:S(2)}, u32[]{:S(2)}) %collective-permute-start.12) | collective-permute-done | bytes 524320 | tf_op jit(solution)/shard_map/ppermute | solution.py:35
  58.2 5.6 %collective-permute-done.15.refs_15_ = f32[256,4,128]{2,1,0:T(4,128)} collective-permute-done((f32[256,4,128]{2,1,0:T(4,128)}, f32[256,4,128]{2,1,0:T(4,128)}, u32[]{:S(2)}, u32[]{:S(2)}) %collective-permute-start.15) | collective-permute-done | bytes 524320 | tf_op jit(solution)/shard_map/ppermute | solution.py:35
  63.8 5.6 %collective-permute-done.13.refs_12_ = f32[256,4,128]{2,1,0:T(4,128)} collective-permute-done((f32[256,4,128]{2,1,0:T(4,128)}, f32[256,4,128]{2,1,0:T(4,128)}, u32[]{:S(2)}, u32[]{:S(2)}) %collective-permute-start.13) | collective-permute-done | bytes 524320 | tf_op jit(solution)/shard_map/ppermute | solution.py:35
  69.4 3.4 %assemble.1.table = f32[4096,4,128]{2,1,0:T(4,128)S(1)} custom-call(s32[16]{0:T(128)S(1)} %fusion.20.base_ref, f32[256,4,128]{2,1,0:T(4,128)S(1)} %copy.27.refs_0_, f32[256,4,128]{2,1,0:T(4,128)S(1)} %collective-permute-done.refs_1_, f32[256,4,128]{2,1,0:T(4,128)S(1)} %collective-permute-done.1.refs_2_, f32[256,4,128]{2,1,0:T(4,128)S(1)} %collective-permute-done.2.refs_3_, ...), custom_call_target="tpu_custom_call" | custom-call | tf_op jit(solution)/shard_map/assemble/pallas_call | solution.py:219
  72.8 7.9 %sigma_partial.2 = (f32[16,64,128]{2,1,0:T(8,128)S(1)}, f32[16,64,128]{2,1,0:T(8,128)S(1)}) custom-call(f32[4096,4,128]{2,1,0:T(4,128)S(1)} %assemble.1.table, s32[2048]{0:T(1024)S(1)} %slice.89.src_ref, s32[256]{0:T(256)S(1)} %pad_add_fusion.tgt_ref, f32[8,256]{1,0:T(8,128)S(1)} %slice.91.sign_ref, f32[256,256]{1,0:T(8,128)S(1)} %mul.53.vb_ref, ...), custom_call_target="tpu_custom_call" | custom-call | flops 4000000000 | bytes 8388608 | tf_op jit(solution)/shard_map/sigma_partial/pallas_call | solution.py:236
  81.4 7.9 %sigma_partial.3 = (f32[16,64,128]{2,1,0:T(8,128)S(1)}, f32[16,64,128]{2,1,0:T(8,128)S(1)}) custom-call(f32[4096,4,128]{2,1,0:T(4,128)S(1)} %assemble.1.table, s32[2048]{0:T(1024)S(1)} %slice.102.src_ref, s32[256]{0:T(256)S(1)} %pad_add_fusion.tgt_ref, f32[8,256]{1,0:T(8,128)S(1)} %slice.104.sign_ref, f32[256,256]{1,0:T(8,128)S(1)} %mul.53.vb_ref, ...), custom_call_target="tpu_custom_call" | custom-call | flops 4000000000 | bytes 8388608 | tf_op jit(solution)/shard_map/sigma_partial/pallas_call | solution.py:236
  89.5 2.4 %collective-permute-start.17 = (f32[4,64,128]{2,1,0:T(8,128)S(1)}, f32[4,64,128]{2,1,0:T(8,128)S(1)}, u32[]{:S(2)}, u32[]{:S(2)}) collective-permute-start(f32[4,64,128]{2,1,0:T(8,128)S(1)} %get-tuple-element.38), channel_id=1, source_target_pairs={{0,8},{2,10},{4,12},{6,14},{8,0},{10,2},{12,4},{14,6},{1,9},{3,11}... | collective-permute-start | bytes 393224 | tf_op jit(solution)/shard_map/ppermute | solution.py:266
  92.0 2.0 %collective-permute-start.19 = (f32[4,64,128]{2,1,0:T(8,128)S(1)}, f32[4,64,128]{2,1,0:T(8,128)S(1)}, u32[]{:S(2)}, u32[]{:S(2)}) collective-permute-start(f32[4,64,128]{2,1,0:T(8,128)S(1)} %get-tuple-element.39), channel_id=1, source_target_pairs={{0,12},{2,14},{4,0},{6,2},{8,4},{10,6},{12,8},{14,10},{1,13},{3,15... | collective-permute-start | bytes 393224 | tf_op jit(solution)/shard_map/ppermute | solution.py:266
  95.5 2.6 %collective-permute-start.22 = (f32[4,64,128]{2,1,0:T(8,128)S(1)}, f32[4,64,128]{2,1,0:T(8,128)S(1)}, u32[]{:S(2)}, u32[]{:S(2)}) collective-permute-start(f32[4,64,128]{2,1,0:T(8,128)S(1)} %get-tuple-element.37), channel_id=1, source_target_pairs={{0,4},{2,6},{4,8},{6,10},{8,12},{10,14},{12,0},{14,2},{1,5},{3,7},... | collective-permute-start | bytes 393224 | tf_op jit(solution)/shard_map/ppermute | solution.py:266
  98.1 2.3 %collective-permute-done.18 = f32[4,64,128]{2,1,0:T(8,128)S(1)} collective-permute-done((f32[4,64,128]{2,1,0:T(8,128)S(1)}, f32[4,64,128]{2,1,0:T(8,128)S(1)}, u32[]{:S(2)}, u32[]{:S(2)}) %collective-permute-start.18) | collective-permute-done | bytes 131104 | tf_op jit(solution)/shard_map/ppermute | solution.py:266
  100.5 2.6 %collective-permute-start.24 = (f32[4,64,128]{2,1,0:T(8,128)S(1)}, f32[4,64,128]{2,1,0:T(8,128)S(1)}, u32[]{:S(2)}, u32[]{:S(2)}) collective-permute-start(f32[4,64,128]{2,1,0:T(8,128)S(1)} %fusion.7), channel_id=1, source_target_pairs={{0,1},{1,0},{2,3},{3,2},{4,5},{5,4},{6,7},{7,6},{8,9},{9,8},{10,11... | collective-permute-start | bytes 393224 | tf_op jit(solution)/shard_map/ppermute | solution.py:267
  103.1 2.5 %collective-permute-done.22 = f32[4,64,128]{2,1,0:T(8,128)S(1)} collective-permute-done((f32[4,64,128]{2,1,0:T(8,128)S(1)}, f32[4,64,128]{2,1,0:T(8,128)S(1)}, u32[]{:S(2)}, u32[]{:S(2)}) %collective-permute-start.22) | collective-permute-done | bytes 131104 | tf_op jit(solution)/shard_map/ppermute | solution.py:266
  105.7 2.1 %collective-permute-start.25 = (f32[4,64,128]{2,1,0:T(8,128)S(1)}, f32[4,64,128]{2,1,0:T(8,128)S(1)}, u32[]{:S(2)}, u32[]{:S(2)}) collective-permute-start(f32[4,64,128]{2,1,0:T(8,128)S(1)} %fusion.4), channel_id=1, source_target_pairs={{0,1},{1,0},{2,3},{3,2},{4,5},{5,4},{6,7},{7,6},{8,9},{9,8},{10,11... | collective-permute-start | bytes 393224 | tf_op jit(solution)/shard_map/ppermute | solution.py:267
  107.8 6.4 %collective-permute-done.24 = f32[4,64,128]{2,1,0:T(8,128)S(1)} collective-permute-done((f32[4,64,128]{2,1,0:T(8,128)S(1)}, f32[4,64,128]{2,1,0:T(8,128)S(1)}, u32[]{:S(2)}, u32[]{:S(2)}) %collective-permute-start.24) | collective-permute-done | bytes 131104 | tf_op jit(solution)/shard_map/ppermute | solution.py:267
  114.2 3.7 %collective-permute-done.25 = f32[4,64,128]{2,1,0:T(8,128)S(1)} collective-permute-done((f32[4,64,128]{2,1,0:T(8,128)S(1)}, f32[4,64,128]{2,1,0:T(8,128)S(1)}, u32[]{:S(2)}, u32[]{:S(2)}) %collective-permute-start.25) | collective-permute-done | bytes 131104 | tf_op jit(solution)/shard_map/ppermute | solution.py:267
  (76 shorter events, 20.4 us)
Async XLA Ops:
  1.3 16.8 %collective-permute-start = (f32[256,4,128]{2,1,0:T(4,128)S(1)}, f32[256,4,128]{2,1,0:T(4,128)S(1)}, u32[]{:S(2)}, u32[]{:S(2)}) collective-permute-start(f32[256,4,128]{2,1,0:T(4,128)S(1)} %copy.27.refs_0_), channel_id=1, source_target_pairs={{0,49},{2,194},{4,53},{6,198},{8,57},{10,202},{12,61},{14,206},{16... | collective-permute-start | bytes 1572872 | tf_op jit(solution)/shard_map/ppermute | solution.py:35
  7.2 14.6 %collective-permute-start.2 = (f32[256,4,128]{2,1,0:T(4,128)S(1)}, f32[256,4,128]{2,1,0:T(4,128)S(1)}, u32[]{:S(2)}, u32[]{:S(2)}) collective-permute-start(f32[256,4,128]{2,1,0:T(4,128)S(1)} %copy.27.refs_0_), channel_id=1, source_target_pairs={{0,16},{2,66},{4,20},{6,70},{8,24},{10,74},{12,28},{14,78},{16,32}... | collective-permute-start | bytes 1572872 | tf_op jit(solution)/shard_map/ppermute | solution.py:35
  7.2 18.7 %collective-permute-start.4 = (f32[256,4,128]{2,1,0:T(4,128)S(1)}, f32[256,4,128]{2,1,0:T(4,128)S(1)}, u32[]{:S(2)}, u32[]{:S(2)}) collective-permute-start(f32[256,4,128]{2,1,0:T(4,128)S(1)} %copy.27.refs_0_), channel_id=1, source_target_pairs={{0,64},{2,18},{4,68},{6,22},{8,72},{10,26},{12,76},{14,30},{16,80}... | collective-permute-start | bytes 1572872 | tf_op jit(solution)/shard_map/ppermute | solution.py:35
  8.7 19.3 %collective-permute-start.3 = (f32[256,4,128]{2,1,0:T(4,128)S(1)}, f32[256,4,128]{2,1,0:T(4,128)S(1)}, u32[]{:S(2)}, u32[]{:S(2)}) collective-permute-start(f32[256,4,128]{2,1,0:T(4,128)S(1)} %copy.27.refs_0_), channel_id=1, source_target_pairs={{0,192},{2,51},{4,196},{6,55},{8,200},{10,59},{12,204},{14,63},{16... | collective-permute-start | bytes 1572872 | tf_op jit(solution)/shard_map/ppermute | solution.py:35
  18.1 16.2 %collective-permute-start.1 = (f32[256,4,128]{2,1,0:T(4,128)S(1)}, f32[256,4,128]{2,1,0:T(4,128)S(1)}, u32[]{:S(2)}, u32[]{:S(2)}) collective-permute-start(f32[256,4,128]{2,1,0:T(4,128)S(1)} %collective-permute-done.refs_1_), channel_id=1, source_target_pairs={{0,49},{2,194},{4,53},{6,198},{8,57},{10,202},{12,61},{14,206},{16... | collective-permute-start | bytes 1572872 | tf_op jit(solution)/shard_map/ppermute | solution.py:35
  21.8 20.3 %collective-permute-start.11 = (f32[256,4,128]{2,1,0:T(4,128)S(1)}, f32[256,4,128]{2,1,0:T(4,128)}, u32[]{:S(2)}, u32[]{:S(2)}) collective-permute-start(f32[256,4,128]{2,1,0:T(4,128)S(1)} %collective-permute-done.2.refs_3_), channel_id=1, source_target_pairs={{0,64},{2,18},{4,68},{6,22},{8,72},{10,26},{12,76},{14,30},{16,80}... | collective-permute-start | bytes 1572872 | tf_op jit(solution)/shard_map/ppermute | solution.py:35
  24.4 11.9 %collective-permute-start.7 = (f32[256,4,128]{2,1,0:T(4,128)S(1)}, f32[256,4,128]{2,1,0:T(4,128)}, u32[]{:S(2)}, u32[]{:S(2)}) collective-permute-start(f32[256,4,128]{2,1,0:T(4,128)S(1)} %collective-permute-done.refs_1_), channel_id=1, source_target_pairs={{0,192},{2,51},{4,196},{6,55},{8,200},{10,59},{12,204},{14,63},{16... | collective-permute-start | bytes 1572872 | tf_op jit(solution)/shard_map/ppermute | solution.py:35
  26.0 13.3 %collective-permute-start.8 = (f32[256,4,128]{2,1,0:T(4,128)S(1)}, f32[256,4,128]{2,1,0:T(4,128)}, u32[]{:S(2)}, u32[]{:S(2)}) collective-permute-start(f32[256,4,128]{2,1,0:T(4,128)S(1)} %collective-permute-done.2.refs_3_), channel_id=1, source_target_pairs={{0,192},{2,51},{4,196},{6,55},{8,200},{10,59},{12,204},{14,63},{16... | collective-permute-start | bytes 1572872 | tf_op jit(solution)/shard_map/ppermute | solution.py:35
  28.0 17.3 %collective-permute-start.5 = (f32[256,4,128]{2,1,0:T(4,128)S(1)}, f32[256,4,128]{2,1,0:T(4,128)}, u32[]{:S(2)}, u32[]{:S(2)}) collective-permute-start(f32[256,4,128]{2,1,0:T(4,128)S(1)} %collective-permute-done.refs_1_), channel_id=1, source_target_pairs={{0,64},{2,18},{4,68},{6,22},{8,72},{10,26},{12,76},{14,30},{16,80}... | collective-permute-start | bytes 1572872 | tf_op jit(solution)/shard_map/ppermute | solution.py:35
  34.4 11.0 %collective-permute-start.14 = (f32[48,128]{1,0:T(8,128)S(1)}, f32[48,128]{1,0:T(8,128)S(1)}, u32[]{:S(2)}, u32[]{:S(2)}) collective-permute-start(f32[48,128]{1,0:T(8,128)S(1)} %select_maximum_fusion), channel_id=1, source_target_pairs={{0,1},{1,0},{2,3},{3,2},{4,5},{5,4},{6,7},{7,6},{8,9},{9,8},{10,11... | collective-permute-start | bytes 73736 | tf_op jit(solution)/shard_map/ppermute | solution.py:59
  39.3 17.1 %collective-permute-start.9 = (f32[256,4,128]{2,1,0:T(4,128)}, f32[256,4,128]{2,1,0:T(4,128)}, u32[]{:S(2)}, u32[]{:S(2)}) collective-permute-start(f32[256,4,128]{2,1,0:T(4,128)} %collective-permute-done.7.refs_7_), channel_id=1, source_target_pairs={{0,192},{2,51},{4,196},{6,55},{8,200},{10,59},{12,204},{14,63},{16... | collective-permute-start | bytes 1572872 | tf_op jit(solution)/shard_map/ppermute | solution.py:35
  42.1 10.5 %collective-permute-start.12 = (f32[256,4,128]{2,1,0:T(4,128)S(1)}, f32[256,4,128]{2,1,0:T(4,128)}, u32[]{:S(2)}, u32[]{:S(2)}) collective-permute-start(f32[256,4,128]{2,1,0:T(4,128)S(1)} %collective-permute-done.1.refs_2_), channel_id=1, source_target_pairs={{0,64},{2,18},{4,68},{6,22},{8,72},{10,26},{12,76},{14,30},{16,80}... | collective-permute-start | bytes 1572872 | tf_op jit(solution)/shard_map/ppermute | solution.py:35
  42.1 14.3 %collective-permute-start.10 = (f32[256,4,128]{2,1,0:T(4,128)S(1)}, f32[256,4,128]{2,1,0:T(4,128)}, u32[]{:S(2)}, u32[]{:S(2)}) collective-permute-start(f32[256,4,128]{2,1,0:T(4,128)S(1)} %collective-permute-done.1.refs_2_), channel_id=1, source_target_pairs={{0,192},{2,51},{4,196},{6,55},{8,200},{10,59},{12,204},{14,63},{16... | collective-permute-start | bytes 1572872 | tf_op jit(solution)/shard_map/ppermute | solution.py:35
  45.3 12.9 %collective-permute-start.6 = (f32[256,4,128]{2,1,0:T(4,128)S(1)}, f32[256,4,128]{2,1,0:T(4,128)}, u32[]{:S(2)}, u32[]{:S(2)}) collective-permute-start(f32[256,4,128]{2,1,0:T(4,128)S(1)} %collective-permute-done.4.refs_5_), channel_id=1, source_target_pairs={{0,64},{2,18},{4,68},{6,22},{8,72},{10,26},{12,76},{14,30},{16,80}... | collective-permute-start | bytes 1572872 | tf_op jit(solution)/shard_map/ppermute | solution.py:35
  45.3 18.5 %collective-permute-start.15 = (f32[256,4,128]{2,1,0:T(4,128)}, f32[256,4,128]{2,1,0:T(4,128)}, u32[]{:S(2)}, u32[]{:S(2)}) collective-permute-start(f32[256,4,128]{2,1,0:T(4,128)} %collective-permute-done.11.refs_14_), channel_id=1, source_target_pairs={{0,64},{2,18},{4,68},{6,22},{8,72},{10,26},{12,76},{14,30},{16,80}... | collective-permute-start | bytes 1572872 | tf_op jit(solution)/shard_map/ppermute | solution.py:35
  52.6 16.9 %collective-permute-start.13 = (f32[256,4,128]{2,1,0:T(4,128)}, f32[256,4,128]{2,1,0:T(4,128)}, u32[]{:S(2)}, u32[]{:S(2)}) collective-permute-start(f32[256,4,128]{2,1,0:T(4,128)} %collective-permute-done.12.refs_11_), channel_id=1, source_target_pairs={{0,64},{2,18},{4,68},{6,22},{8,72},{10,26},{12,76},{14,30},{16,80}... | collective-permute-start | bytes 1572872 | tf_op jit(solution)/shard_map/ppermute | solution.py:35
  80.8 8.7 %collective-permute-start.16 = (f32[16,64,128]{2,1,0:T(8,128)S(1)}, f32[16,64,128]{2,1,0:T(8,128)S(1)}, u32[]{:S(2)}, u32[]{:S(2)}) collective-permute-start(f32[16,64,128]{2,1,0:T(8,128)S(1)} %get-tuple-element.32), channel_id=1, source_target_pairs={{0,2},{2,0},{4,6},{6,4},{8,10},{10,8},{12,14},{14,12},{1,3},{3,1},... | collective-permute-start | bytes 1572872 | tf_op jit(solution)/shard_map/ppermute | solution.py:261
  89.5 8.6 %collective-permute-start.17 = (f32[4,64,128]{2,1,0:T(8,128)S(1)}, f32[4,64,128]{2,1,0:T(8,128)S(1)}, u32[]{:S(2)}, u32[]{:S(2)}) collective-permute-start(f32[4,64,128]{2,1,0:T(8,128)S(1)} %get-tuple-element.38), channel_id=1, source_target_pairs={{0,8},{2,10},{4,12},{6,14},{8,0},{10,2},{12,4},{14,6},{1,9},{3,11}... | collective-permute-start | bytes 393224 | tf_op jit(solution)/shard_map/ppermute | solution.py:266
  91.9 8.5 %collective-permute-start.18 = (f32[4,64,128]{2,1,0:T(8,128)S(1)}, f32[4,64,128]{2,1,0:T(8,128)S(1)}, u32[]{:S(2)}, u32[]{:S(2)}) collective-permute-start(f32[4,64,128]{2,1,0:T(8,128)S(1)} %get-tuple-element.40), channel_id=1, source_target_pairs={{0,4},{2,6},{4,8},{6,10},{8,12},{10,14},{12,0},{14,2},{1,5},{3,7},... | collective-permute-start | bytes 393224 | tf_op jit(solution)/shard_map/ppermute | solution.py:266
  92.0 8.5 %collective-permute-start.19 = (f32[4,64,128]{2,1,0:T(8,128)S(1)}, f32[4,64,128]{2,1,0:T(8,128)S(1)}, u32[]{:S(2)}, u32[]{:S(2)}) collective-permute-start(f32[4,64,128]{2,1,0:T(8,128)S(1)} %get-tuple-element.39), channel_id=1, source_target_pairs={{0,12},{2,14},{4,0},{6,2},{8,4},{10,6},{12,8},{14,10},{1,13},{3,15... | collective-permute-start | bytes 393224 | tf_op jit(solution)/shard_map/ppermute | solution.py:266
  94.0 9.1 %collective-permute-start.21 = (f32[4,64,128]{2,1,0:T(8,128)S(1)}, f32[4,64,128]{2,1,0:T(8,128)S(1)}, u32[]{:S(2)}, u32[]{:S(2)}) collective-permute-start(f32[4,64,128]{2,1,0:T(8,128)S(1)} %get-tuple-element.35), channel_id=1, source_target_pairs={{0,8},{2,10},{4,12},{6,14},{8,0},{10,2},{12,4},{14,6},{1,9},{3,11}... | collective-permute-start | bytes 393224 | tf_op jit(solution)/shard_map/ppermute | solution.py:266
  95.5 10.2 %collective-permute-start.22 = (f32[4,64,128]{2,1,0:T(8,128)S(1)}, f32[4,64,128]{2,1,0:T(8,128)S(1)}, u32[]{:S(2)}, u32[]{:S(2)}) collective-permute-start(f32[4,64,128]{2,1,0:T(8,128)S(1)} %get-tuple-element.37), channel_id=1, source_target_pairs={{0,4},{2,6},{4,8},{6,10},{8,12},{10,14},{12,0},{14,2},{1,5},{3,7},... | collective-permute-start | bytes 393224 | tf_op jit(solution)/shard_map/ppermute | solution.py:266
  100.5 13.7 %collective-permute-start.24 = (f32[4,64,128]{2,1,0:T(8,128)S(1)}, f32[4,64,128]{2,1,0:T(8,128)S(1)}, u32[]{:S(2)}, u32[]{:S(2)}) collective-permute-start(f32[4,64,128]{2,1,0:T(8,128)S(1)} %fusion.7), channel_id=1, source_target_pairs={{0,1},{1,0},{2,3},{3,2},{4,5},{5,4},{6,7},{7,6},{8,9},{9,8},{10,11... | collective-permute-start | bytes 393224 | tf_op jit(solution)/shard_map/ppermute | solution.py:267
  105.7 12.1 %collective-permute-start.25 = (f32[4,64,128]{2,1,0:T(8,128)S(1)}, f32[4,64,128]{2,1,0:T(8,128)S(1)}, u32[]{:S(2)}, u32[]{:S(2)}) collective-permute-start(f32[4,64,128]{2,1,0:T(8,128)S(1)} %fusion.4), channel_id=1, source_target_pairs={{0,1},{1,0},{2,3},{3,2},{4,5},{5,4},{6,7},{7,6},{8,9},{9,8},{10,11... | collective-permute-start | bytes 393224 | tf_op jit(solution)/shard_map/ppermute | solution.py:267
  (4 other events, 45.0 us)

commit v4 on v3

--- a/solution.py
+++ b/solution.py
@@ -35,44 +35,50 @@
     return lax.ppermute(value, AXES, pairs)
 
 
+PLAN = (
+    ("own_behind", "own", 1, 1, ()),
+    ("ahead", "own", 0, -1, ()),
+    ("behind", "own", 0, 1, ()),
+    ("packet", "packet", 0, 1, ()),
+    ("over", "ahead", 0, -1, ("ahead",)),
+    ("ahead_behind", "ahead", 1, 1, ()),
+    ("ahead_ahead", "ahead", 1, -1, ("own_behind",)),
+    ("behind_behind", "behind", 1, 1, ("behind",)),
+    ("behind_ahead", "behind", 1, -1, ("packet",)),
+    ("own_over", "own_behind", 1, 1, ("over",)),
+    ("over_behind", "over", 1, 1, ("ahead_behind",)),
+    ("over_ahead", "over", 1, -1, ("ahead_ahead",)),
+    ("ahead_over", "ahead_behind", 1, 1, ("behind_behind",)),
+    ("over_over", "over_ahead", 1, -1, ("over_ahead",)),
+    ("own_ahead", "own", 1, -1, ("behind_ahead",)),
+    ("behind_over", "behind_behind", 1, 1, ("own_over",)),
+)
+LAST = ("ahead_over", "over_over", "own_ahead", "behind_over",)
+ALONG = {"own": 0, "ahead": 1, "over": 2, "behind": 3}
+ACROSS = {"": 0, "_ahead": 1, "_over": 2, "_behind": 3}
+
+
 def spread(block, packet):
     held = {"own": block}
-    order = []
-
-    def send(name, source, axis, step):
-        value = held[source]
-        if len(order) >= FLIGHT:
-            value, _ = lax.optimization_barrier((value, held[order[-FLIGHT]]))
-        held[name] = move(value, axis, step)
-        order.append(name)
-
-    send("ahead", "own", 0, -1)
-    send("behind", "own", 0, 1)
-    send("own_ahead", "own", 1, -1)
-    send("own_behind", "own", 1, 1)
-    send("over", "ahead", 0, -1)
-    send("behind_behind", "behind", 1, 1)
-    send("ahead_ahead", "ahead", 1, -1)
-    send("ahead_behind", "ahead", 1, 1)
-    send("behind_ahead", "behind", 1, -1)
-    packet, _ = lax.optimization_barrier((packet, held[order[-FLIGHT]]))
-    held["packet"] = lax.ppermute(packet, "ints", [(0, 1), (1, 0)])
-    order.append("packet")
-    send("over_behind", "over", 1, 1)
-    send("over_ahead", "over", 1, -1)
-    send("own_over", "own_behind", 1, 1)
-    send("ahead_over", "ahead_ahead", 1, -1)
-    send("behind_over", "behind_behind", 1, 1)
-    send("over_over", "over_behind", 1, 1)
-    along = {"own": 0, "ahead": 1, "over": 2, "behind": 3}
-    pieces = [(0, at, held[name]) for name, at in along.items()]
-    for name, at in along.items():
-        pieces += [(1, at, held[name + "_ahead"]), (3, at, held[name + "_behind"]), (2, at, held[name + "_over"])]
-    return pieces, held["packet"]
-
-
-def assemble(copies, base_ref, *refs):
-    arrays, table, sems = refs[:-2], refs[-2], refs[-1]
+    for name, source, axis, step, waits in PLAN:
+        value = packet if name == "packet" else held[source]
+        if waits:
+            value = lax.optimization_barrier((value, *[held[w] for w in waits]))[0]
+        if name == "packet":
+            held[name] = lax.ppermute(value, "ints", [(0, 1), (1, 0)])
+        else:
+            held[name] = move(value, axis, step)
+    packet = held.pop("packet")
+    return held, packet
+
+
+def slot_of(name):
+    first, _, second = name.partition("_")
+    return ACROSS["_" + second if second else ""] * RING + ALONG[first]
+
+
+def assemble(copies, held, base_ref, *refs):
+    arrays, table, sems = refs[: len(copies)], refs[-2], refs[-1]
     dmas = []
     for n, slot in enumerate(copies):
         rows = arrays[n].shape[0]
@@ -206,8 +212,6 @@
     spot = ((owner % CORES) ^ core) * (tiles // CORES) + away * slots + target % slots
     target = jnp.concatenate([target, spot])
 
-    arrays = [array for _, _, array in pieces]
-    copies = [on_one * RING + on_zero for on_one, on_zero, _ in pieces]
     d = jnp.arange(RING * RING, dtype=jnp.int32)
     dx = jnp.where(core == 0, d // RING, d % RING)
     dz = jnp.where(core == 0, d % RING, d // RING)
@@ -216,15 +220,19 @@
     smem = pl.BlockSpec(memory_space=pltpu.SMEM)
     vmem = pl.BlockSpec(memory_space=pltpu.VMEM)
     hbm = pl.BlockSpec(memory_space=pl.ANY)
-    table = pl.pallas_call(
-        functools.partial(assemble, tuple(copies)),
-        out_shape=jax.ShapeDtypeStruct((lax.axis_size("alpha") * cols_a, slots, tile), jnp.float32),
-        in_specs=[smem] + [hbm] * len(arrays),
-        out_specs=vmem,
-        scratch_shapes=[pltpu.SemaphoreType.DMA((len(copies),))],
-        compiler_params=pltpu.CompilerParams(vmem_limit_bytes=12 * 1024 * 1024),
-        name="assemble",
-    )(base, *arrays)
+    table = None
+    for names in (tuple(n for n in pieces if n not in LAST), LAST):
+        old = [] if table is None else [table]
+        table = pl.pallas_call(
+            functools.partial(assemble, tuple(slot_of(n) for n in names), len(old)),
+            out_shape=jax.ShapeDtypeStruct((lax.axis_size("alpha") * cols_a, slots, tile), jnp.float32),
+            in_specs=[smem] + [hbm] * len(names) + [vmem] * len(old),
+            out_specs=vmem,
+            scratch_shapes=[pltpu.SemaphoreType.DMA((len(names),))],
+            input_output_aliases={1 + len(names): 0} if old else {},
+            compiler_params=pltpu.CompilerParams(vmem_limit_bytes=12 * 1024 * 1024),
+            name="assemble",
+        )(base, *[pieces[n] for n in names], *old)
     width = cols // CHUNKS
     offsets = beta_offsets.reshape(pairs * tiles, tile)
     signs = beta_sign.reshape(pairs * tiles, tile)

time: 120 us -> 114 us (0.950)
  waiting for transfers between devices: 48.9 us -> 38.1 us
  starting transfers between devices: 39.1 us -> 43.2 us
  Pallas kernels: 19.3 us -> 20.7 us
    ppermute x15, waiting for transfers between devices: 34 us -> 23.2 us  [move(): return lax.ppermute(value, AXES, pairs)]
    ppermute x1, starting transfers between devices: 0.01 us -> 4.48 us  [spread(): held[name] = lax.ppermute(value, 'ints', [(0, 1), (1, 0)])]
    pallas_call x1 -> x2, Pallas kernels: 3.37 us -> 4.78 us  [local(): pl.pallas_call(functools.partial(assemble, tuple((slot_of(n) for n in nam...]
  transfers between devices with their start and end apart: 26 -> 26, of which waited for: 11 -> 12; matrix products, arithmetic and copies ran while one was open for 8% -> 8% of each run, Pallas kernels for 7% -> 9%
where the time goes in v4:
time: 114 us
  starting transfers between devices  43.2 us (38%)
  waiting for transfers between devices  38.1 us (33%)
  Pallas kernels  20.7 us (18%)
  local copies, waits for them, and re-layouts  6.81 us (6%)
  other arithmetic  4.59 us (4%)
    ppermute x15, starting transfers between devices, move(): return lax.ppermute(value, AXES, pairs)  24.5 us
    ppermute x15, waiting for transfers between devices, move(): return lax.ppermute(value, AXES, pairs)  23.2 us
    pallas_call x2, Pallas kernels, local(): pl.pallas_call(functools.partial(kernel, part_steps, pairs, slots), out_s...  15.9 us
    ppermute x2, waiting for transfers between devices, local(): sums.append((total, lax.ppermute(total, 'ints', swap)))  10.3 us
    ppermute x6, starting transfers between devices, local(): total = total + lax.ppermute(part, 'beta', pairs_y)  8.52 us
    ppermute x2, starting transfers between devices, local(): sums.append((total, lax.ppermute(total, 'ints', swap)))  4.97 us
    pallas_call x2, Pallas kernels, local(): pl.pallas_call(functools.partial(assemble, tuple((slot_of(n) for n in nam...  4.78 us
    ppermute x6, waiting for transfers between devices, local(): total = total + lax.ppermute(part, 'beta', pairs_y)  4.58 us
  transfers between devices with their start and end apart: 26, of which 12 were waited for; matrix products, arithmetic and copies ran while one was open for 8% of the time, Pallas kernels for 9%

profile of v4, /device:TPU:8, one launch (start us, length us, event | category | flops | bytes accessed | tf_op | source)
XLA Modules:
  0.0 113.6 jit_solution(14900156708166392366)
XLA Ops:
  1.3 2.0 %collective-permute-start.2 = (f32[256,4,128]{2,1,0:T(4,128)S(1)}, f32[256,4,128]{2,1,0:T(4,128)S(1)}, u32[]{:S(2)}, u32[]{:S(2)}) collective-permute-start(f32[256,4,128]{2,1,0:T(4,128)S(1)} %copy.28.refs_0_), channel_id=1, source_target_pairs={{0,16},{2,66},{4,20},{6,70},{8,24},{10,74},{12,28},{14,78},{16,32}... | collective-permute-start | bytes 1572872 | tf_op jit(solution)/shard_map/ppermute | solution.py:35
  3.3 4.0 %collective-permute-start = (f32[256,4,128]{2,1,0:T(4,128)S(1)}, f32[256,4,128]{2,1,0:T(4,128)S(1)}, u32[]{:S(2)}, u32[]{:S(2)}) collective-permute-start(f32[256,4,128]{2,1,0:T(4,128)S(1)} %copy.28.refs_0_), channel_id=1, source_target_pairs={{0,49},{2,194},{4,53},{6,198},{8,57},{10,202},{12,61},{14,206},{16... | collective-permute-start | bytes 1572872 | tf_op jit(solution)/shard_map/ppermute | solution.py:35
  10.2 4.5 %collective-permute-start.10 = (f32[48,128]{1,0:T(8,128)S(1)}, f32[48,128]{1,0:T(8,128)S(1)}, u32[]{:S(2)}, u32[]{:S(2)}) collective-permute-start(f32[48,128]{1,0:T(8,128)S(1)} %select_maximum_fusion), channel_id=1, source_target_pairs={{0,1},{1,0},{2,3},{3,2},{4,5},{5,4},{6,7},{7,6},{8,9},{9,8},{10,11... | collective-permute-start | bytes 73736 | tf_op jit(solution)/shard_map/ppermute | solution.py:68
  19.2 4.4 %collective-permute-start.5 = (f32[256,4,128]{2,1,0:T(4,128)S(1)}, f32[256,4,128]{2,1,0:T(4,128)S(1)}, u32[]{:S(2)}, u32[]{:S(2)}) collective-permute-start(f32[256,4,128]{2,1,0:T(4,128)S(1)} %collective-permute-done.refs_2_), channel_id=1, source_target_pairs={{0,49},{2,194},{4,53},{6,198},{8,57},{10,202},{12,61},{14,206},{16... | collective-permute-start | bytes 1572872 | tf_op jit(solution)/shard_map/ppermute | solution.py:35
  23.7 1.9 %reshape.54.bs_ref = s32[1024,128]{1,0:T(8,128)} reshape(s32[32,4096]{1,0:T(8,128)} %param.13) | data formatting | bytes 1048576 | tf_op jit(solution)/shard_map/reshape | solution.py:238
  29.0 7.0 %collective-permute-done.5.refs_4_ = f32[256,4,128]{2,1,0:T(4,128)S(1)} collective-permute-done((f32[256,4,128]{2,1,0:T(4,128)S(1)}, f32[256,4,128]{2,1,0:T(4,128)S(1)}, u32[]{:S(2)}, u32[]{:S(2)}) %collective-permute-start.5) | collective-permute-done | bytes 524320 | tf_op jit(solution)/shard_map/ppermute | solution.py:35
  38.5 4.2 %collective-permute-done.1.refs_5_ = f32[256,4,128]{2,1,0:T(4,128)} collective-permute-done((f32[256,4,128]{2,1,0:T(4,128)S(1)}, f32[256,4,128]{2,1,0:T(4,128)}, u32[]{:S(2)}, u32[]{:S(2)}) %collective-permute-start.1) | collective-permute-done | bytes 524320 | tf_op jit(solution)/shard_map/ppermute | solution.py:35
  42.7 3.2 %collective-permute-start.12 = (f32[256,4,128]{2,1,0:T(4,128)S(1)}, f32[256,4,128]{2,1,0:T(4,128)}, u32[]{:S(2)}, u32[]{:S(2)}) collective-permute-start(f32[256,4,128]{2,1,0:T(4,128)S(1)} %copy.28.refs_0_), channel_id=1, source_target_pairs={{0,192},{2,51},{4,196},{6,55},{8,200},{10,59},{12,204},{14,63},{16... | collective-permute-start | bytes 1572872 | tf_op jit(solution)/shard_map/ppermute | solution.py:35
  45.9 2.4 %collective-permute-done.13.refs_9_ = f32[256,4,128]{2,1,0:T(4,128)} collective-permute-done((f32[256,4,128]{2,1,0:T(4,128)S(1)}, f32[256,4,128]{2,1,0:T(4,128)}, u32[]{:S(2)}, u32[]{:S(2)}) %collective-permute-start.13) | collective-permute-done | bytes 524320 | tf_op jit(solution)/shard_map/ppermute | solution.py:35
  48.3 3.2 %collective-permute-start.9 = (f32[256,4,128]{2,1,0:T(4,128)}, f32[256,4,128]{2,1,0:T(4,128)}, u32[]{:S(2)}, u32[]{:S(2)}) collective-permute-start(f32[256,4,128]{2,1,0:T(4,128)} %collective-permute-done.8.refs_11_), channel_id=1, source_target_pairs={{0,192},{2,51},{4,196},{6,55},{8,200},{10,59},{12,204},{14,63},{16... | collective-permute-start | bytes 1572872 | tf_op jit(solution)/shard_map/ppermute | solution.py:35
  55.3 2.7 %assemble.2.refs_4_ = f32[4096,4,128]{2,1,0:T(4,128)S(1)} custom-call(s32[16]{0:T(128)S(1)} %fusion.20.base_ref, f32[256,4,128]{2,1,0:T(4,128)S(1)} %copy.28.refs_0_, f32[256,4,128]{2,1,0:T(4,128)S(1)} %collective-permute-done.6.refs_1_, f32[256,4,128]{2,1,0:T(4,128)S(1)} %collective-permute-done.refs_2_, f32[256,4,128]{2,1,0:T(4,128)S(1)} %collective-permute-done.2.refs_3_, ...), custom_call_target="tpu_custom_call" | custom-call | tf_op jit(solution)/shard_map/assemble/pallas_call | solution.py:226
  59.5 5.6 %collective-permute-done.14.refs_3_ = f32[256,4,128]{2,1,0:T(4,128)} collective-permute-done((f32[256,4,128]{2,1,0:T(4,128)}, f32[256,4,128]{2,1,0:T(4,128)}, u32[]{:S(2)}, u32[]{:S(2)}) %collective-permute-start.14) | collective-permute-done | bytes 524320 | tf_op jit(solution)/shard_map/ppermute | solution.py:35
  65.1 2.1 %assemble.3.table = f32[4096,4,128]{2,1,0:T(4,128)S(1)} custom-call(s32[16]{0:T(128)S(1)} %fusion.20.base_ref, f32[256,4,128]{2,1,0:T(4,128)} %collective-permute-done.4.refs_0_, f32[256,4,128]{2,1,0:T(4,128)} %collective-permute-done.9.refs_1_, f32[256,4,128]{2,1,0:T(4,128)} %collective-permute-done.12.refs_2_, ...), custom_call_target="tpu_custom_call", output_to_operand_aliasing={{}: (5, {})} | custom-call | tf_op jit(solution)/shard_map/assemble/pallas_call | solution.py:226
  67.3 7.9 %sigma_partial.2 = (f32[16,64,128]{2,1,0:T(8,128)S(1)}, f32[16,64,128]{2,1,0:T(8,128)S(1)}) custom-call(f32[4096,4,128]{2,1,0:T(4,128)S(1)} %assemble.3.table, s32[2048]{0:T(1024)S(1)} %slice.89.src_ref, s32[256]{0:T(256)S(1)} %pad_add_fusion.tgt_ref, f32[8,256]{1,0:T(8,128)S(1)} %slice.91.sign_ref, f32[256,256]{1,0:T(8,128)S(1)} %mul.53.vb_ref, ...), custom_call_target="tpu_custom_call" | custom-call | flops 4000000000 | bytes 8388608 | tf_op jit(solution)/shard_map/sigma_partial/pallas_call | solution.py:244
  75.3 7.9 %sigma_partial.3 = (f32[16,64,128]{2,1,0:T(8,128)S(1)}, f32[16,64,128]{2,1,0:T(8,128)S(1)}) custom-call(f32[4096,4,128]{2,1,0:T(4,128)S(1)} %assemble.3.table, s32[2048]{0:T(1024)S(1)} %slice.102.src_ref, s32[256]{0:T(256)S(1)} %pad_add_fusion.tgt_ref, f32[8,256]{1,0:T(8,128)S(1)} %slice.104.sign_ref, f32[256,256]{1,0:T(8,128)S(1)} %mul.53.vb_ref, ...), custom_call_target="tpu_custom_call" | custom-call | flops 4000000000 | bytes 8388608 | tf_op jit(solution)/shard_map/sigma_partial/pallas_call | solution.py:244
  83.9 2.4 %collective-permute-start.17 = (f32[4,64,128]{2,1,0:T(8,128)S(1)}, f32[4,64,128]{2,1,0:T(8,128)S(1)}, u32[]{:S(2)}, u32[]{:S(2)}) collective-permute-start(f32[4,64,128]{2,1,0:T(8,128)S(1)} %get-tuple-element.38), channel_id=1, source_target_pairs={{0,8},{2,10},{4,12},{6,14},{8,0},{10,2},{12,4},{14,6},{1,9},{3,11}... | collective-permute-start | bytes 393224 | tf_op jit(solution)/shard_map/ppermute | solution.py:274
  86.3 2.0 %collective-permute-start.19 = (f32[4,64,128]{2,1,0:T(8,128)S(1)}, f32[4,64,128]{2,1,0:T(8,128)S(1)}, u32[]{:S(2)}, u32[]{:S(2)}) collective-permute-start(f32[4,64,128]{2,1,0:T(8,128)S(1)} %get-tuple-element.39), channel_id=1, source_target_pairs={{0,12},{2,14},{4,0},{6,2},{8,4},{10,6},{12,8},{14,10},{1,13},{3,15... | collective-permute-start | bytes 393224 | tf_op jit(solution)/shard_map/ppermute | solution.py:274
  89.9 2.6 %collective-permute-start.22 = (f32[4,64,128]{2,1,0:T(8,128)S(1)}, f32[4,64,128]{2,1,0:T(8,128)S(1)}, u32[]{:S(2)}, u32[]{:S(2)}) collective-permute-start(f32[4,64,128]{2,1,0:T(8,128)S(1)} %get-tuple-element.37), channel_id=1, source_target_pairs={{0,4},{2,6},{4,8},{6,10},{8,12},{10,14},{12,0},{14,2},{1,5},{3,7},... | collective-permute-start | bytes 393224 | tf_op jit(solution)/shard_map/ppermute | solution.py:274
  92.5 2.3 %collective-permute-done.18 = f32[4,64,128]{2,1,0:T(8,128)S(1)} collective-permute-done((f32[4,64,128]{2,1,0:T(8,128)S(1)}, f32[4,64,128]{2,1,0:T(8,128)S(1)}, u32[]{:S(2)}, u32[]{:S(2)}) %collective-permute-start.18) | collective-permute-done | bytes 131104 | tf_op jit(solution)/shard_map/ppermute | solution.py:274
  94.9 2.4 %collective-permute-start.24 = (f32[4,64,128]{2,1,0:T(8,128)S(1)}, f32[4,64,128]{2,1,0:T(8,128)S(1)}, u32[]{:S(2)}, u32[]{:S(2)}) collective-permute-start(f32[4,64,128]{2,1,0:T(8,128)S(1)} %fusion.7), channel_id=1, source_target_pairs={{0,1},{1,0},{2,3},{3,2},{4,5},{5,4},{6,7},{7,6},{8,9},{9,8},{10,11... | collective-permute-start | bytes 393224 | tf_op jit(solution)/shard_map/ppermute | solution.py:275
  97.5 2.0 %collective-permute-done.22 = f32[4,64,128]{2,1,0:T(8,128)S(1)} collective-permute-done((f32[4,64,128]{2,1,0:T(8,128)S(1)}, f32[4,64,128]{2,1,0:T(8,128)S(1)}, u32[]{:S(2)}, u32[]{:S(2)}) %collective-permute-start.22) | collective-permute-done | bytes 131104 | tf_op jit(solution)/shard_map/ppermute | solution.py:274
  99.6 2.6 %collective-permute-start.25 = (f32[4,64,128]{2,1,0:T(8,128)S(1)}, f32[4,64,128]{2,1,0:T(8,128)S(1)}, u32[]{:S(2)}, u32[]{:S(2)}) collective-permute-start(f32[4,64,128]{2,1,0:T(8,128)S(1)} %fusion.4), channel_id=1, source_target_pairs={{0,1},{1,0},{2,3},{3,2},{4,5},{5,4},{6,7},{7,6},{8,9},{9,8},{10,11... | collective-permute-start | bytes 393224 | tf_op jit(solution)/shard_map/ppermute | solution.py:275
  102.1 4.8 %collective-permute-done.24 = f32[4,64,128]{2,1,0:T(8,128)S(1)} collective-permute-done((f32[4,64,128]{2,1,0:T(8,128)S(1)}, f32[4,64,128]{2,1,0:T(8,128)S(1)}, u32[]{:S(2)}, u32[]{:S(2)}) %collective-permute-start.24) | collective-permute-done | bytes 131104 | tf_op jit(solution)/shard_map/ppermute | solution.py:275
  107.0 5.5 %collective-permute-done.25 = f32[4,64,128]{2,1,0:T(8,128)S(1)} collective-permute-done((f32[4,64,128]{2,1,0:T(8,128)S(1)}, f32[4,64,128]{2,1,0:T(8,128)S(1)}, u32[]{:S(2)}, u32[]{:S(2)}) %collective-permute-start.25) | collective-permute-done | bytes 131104 | tf_op jit(solution)/shard_map/ppermute | solution.py:275
  (77 shorter events, 23.6 us)
Async XLA Ops:
  1.3 24.3 %collective-permute-start.2 = (f32[256,4,128]{2,1,0:T(4,128)S(1)}, f32[256,4,128]{2,1,0:T(4,128)S(1)}, u32[]{:S(2)}, u32[]{:S(2)}) collective-permute-start(f32[256,4,128]{2,1,0:T(4,128)S(1)} %copy.28.refs_0_), channel_id=1, source_target_pairs={{0,16},{2,66},{4,20},{6,70},{8,24},{10,74},{12,28},{14,78},{16,32}... | collective-permute-start | bytes 1572872 | tf_op jit(solution)/shard_map/ppermute | solution.py:35
  3.3 12.6 %collective-permute-start = (f32[256,4,128]{2,1,0:T(4,128)S(1)}, f32[256,4,128]{2,1,0:T(4,128)S(1)}, u32[]{:S(2)}, u32[]{:S(2)}) collective-permute-start(f32[256,4,128]{2,1,0:T(4,128)S(1)} %copy.28.refs_0_), channel_id=1, source_target_pairs={{0,49},{2,194},{4,53},{6,198},{8,57},{10,202},{12,61},{14,206},{16... | collective-permute-start | bytes 1572872 | tf_op jit(solution)/shard_map/ppermute | solution.py:35
  7.3 10.4 %collective-permute-start.6 = (f32[256,4,128]{2,1,0:T(4,128)S(1)}, f32[256,4,128]{2,1,0:T(4,128)S(1)}, u32[]{:S(2)}, u32[]{:S(2)}) collective-permute-start(f32[256,4,128]{2,1,0:T(4,128)S(1)} %copy.28.refs_0_), channel_id=1, source_target_pairs={{0,64},{2,18},{4,68},{6,22},{8,72},{10,26},{12,76},{14,30},{16,80}... | collective-permute-start | bytes 1572872 | tf_op jit(solution)/shard_map/ppermute | solution.py:35
  10.2 15.3 %collective-permute-start.10 = (f32[48,128]{1,0:T(8,128)S(1)}, f32[48,128]{1,0:T(8,128)S(1)}, u32[]{:S(2)}, u32[]{:S(2)}) collective-permute-start(f32[48,128]{1,0:T(8,128)S(1)} %select_maximum_fusion), channel_id=1, source_target_pairs={{0,1},{1,0},{2,3},{3,2},{4,5},{5,4},{6,7},{7,6},{8,9},{9,8},{10,11... | collective-permute-start | bytes 73736 | tf_op jit(solution)/shard_map/ppermute | solution.py:68
  17.7 11.3 %collective-permute-start.7 = (f32[256,4,128]{2,1,0:T(4,128)S(1)}, f32[256,4,128]{2,1,0:T(4,128)S(1)}, u32[]{:S(2)}, u32[]{:S(2)}) collective-permute-start(f32[256,4,128]{2,1,0:T(4,128)S(1)} %collective-permute-done.refs_2_), channel_id=1, source_target_pairs={{0,192},{2,51},{4,196},{6,55},{8,200},{10,59},{12,204},{14,63},{16... | collective-permute-start | bytes 1572872 | tf_op jit(solution)/shard_map/ppermute | solution.py:35
  19.2 16.8 %collective-permute-start.5 = (f32[256,4,128]{2,1,0:T(4,128)S(1)}, f32[256,4,128]{2,1,0:T(4,128)S(1)}, u32[]{:S(2)}, u32[]{:S(2)}) collective-permute-start(f32[256,4,128]{2,1,0:T(4,128)S(1)} %collective-permute-done.refs_2_), channel_id=1, source_target_pairs={{0,49},{2,194},{4,53},{6,198},{8,57},{10,202},{12,61},{14,206},{16... | collective-permute-start | bytes 1572872 | tf_op jit(solution)/shard_map/ppermute | solution.py:35
  25.6 17.1 %collective-permute-start.11 = (f32[256,4,128]{2,1,0:T(4,128)S(1)}, f32[256,4,128]{2,1,0:T(4,128)}, u32[]{:S(2)}, u32[]{:S(2)}) collective-permute-start(f32[256,4,128]{2,1,0:T(4,128)S(1)} %collective-permute-done.2.refs_3_), channel_id=1, source_target_pairs={{0,192},{2,51},{4,196},{6,55},{8,200},{10,59},{12,204},{14,63},{16... | collective-permute-start | bytes 1572872 | tf_op jit(solution)/shard_map/ppermute | solution.py:35
  26.5 19.4 %collective-permute-start.3 = (f32[256,4,128]{2,1,0:T(4,128)S(1)}, f32[256,4,128]{2,1,0:T(4,128)}, u32[]{:S(2)}, u32[]{:S(2)}) collective-permute-start(f32[256,4,128]{2,1,0:T(4,128)S(1)} %collective-permute-done.2.refs_3_), channel_id=1, source_target_pairs={{0,64},{2,18},{4,68},{6,22},{8,72},{10,26},{12,76},{14,30},{16,80}... | collective-permute-start | bytes 1572872 | tf_op jit(solution)/shard_map/ppermute | solution.py:35
  27.7 14.9 %collective-permute-start.1 = (f32[256,4,128]{2,1,0:T(4,128)S(1)}, f32[256,4,128]{2,1,0:T(4,128)}, u32[]{:S(2)}, u32[]{:S(2)}) collective-permute-start(f32[256,4,128]{2,1,0:T(4,128)S(1)} %collective-permute-done.refs_2_), channel_id=1, source_target_pairs={{0,64},{2,18},{4,68},{6,22},{8,72},{10,26},{12,76},{14,30},{16,80}... | collective-permute-start | bytes 1572872 | tf_op jit(solution)/shard_map/ppermute | solution.py:35
  36.0 12.3 %collective-permute-start.8 = (f32[256,4,128]{2,1,0:T(4,128)S(1)}, f32[256,4,128]{2,1,0:T(4,128)}, u32[]{:S(2)}, u32[]{:S(2)}) collective-permute-start(f32[256,4,128]{2,1,0:T(4,128)S(1)} %collective-permute-done.5.refs_4_), channel_id=1, source_target_pairs={{0,192},{2,51},{4,196},{6,55},{8,200},{10,59},{12,204},{14,63},{16... | collective-permute-start | bytes 1572872 | tf_op jit(solution)/shard_map/ppermute | solution.py:35
  36.7 11.5 %collective-permute-start.13 = (f32[256,4,128]{2,1,0:T(4,128)S(1)}, f32[256,4,128]{2,1,0:T(4,128)}, u32[]{:S(2)}, u32[]{:S(2)}) collective-permute-start(f32[256,4,128]{2,1,0:T(4,128)S(1)} %collective-permute-done.6.refs_1_), channel_id=1, source_target_pairs={{0,64},{2,18},{4,68},{6,22},{8,72},{10,26},{12,76},{14,30},{16,80}... | collective-permute-start | bytes 1572872 | tf_op jit(solution)/shard_map/ppermute | solution.py:35
  42.7 12.7 %collective-permute-start.15 = (f32[256,4,128]{2,1,0:T(4,128)S(1)}, f32[256,4,128]{2,1,0:T(4,128)}, u32[]{:S(2)}, u32[]{:S(2)}) collective-permute-start(f32[256,4,128]{2,1,0:T(4,128)S(1)} %collective-permute-done.5.refs_4_), channel_id=1, source_target_pairs={{0,64},{2,18},{4,68},{6,22},{8,72},{10,26},{12,76},{14,30},{16,80}... | collective-permute-start | bytes 1572872 | tf_op jit(solution)/shard_map/ppermute | solution.py:35
  42.7 15.4 %collective-permute-start.12 = (f32[256,4,128]{2,1,0:T(4,128)S(1)}, f32[256,4,128]{2,1,0:T(4,128)}, u32[]{:S(2)}, u32[]{:S(2)}) collective-permute-start(f32[256,4,128]{2,1,0:T(4,128)S(1)} %copy.28.refs_0_), channel_id=1, source_target_pairs={{0,192},{2,51},{4,196},{6,55},{8,200},{10,59},{12,204},{14,63},{16... | collective-permute-start | bytes 1572872 | tf_op jit(solution)/shard_map/ppermute | solution.py:35
  45.9 13.6 %collective-permute-start.4 = (f32[256,4,128]{2,1,0:T(4,128)}, f32[256,4,128]{2,1,0:T(4,128)}, u32[]{:S(2)}, u32[]{:S(2)}) collective-permute-start(f32[256,4,128]{2,1,0:T(4,128)} %collective-permute-done.1.refs_5_), channel_id=1, source_target_pairs={{0,64},{2,18},{4,68},{6,22},{8,72},{10,26},{12,76},{14,30},{16,80}... | collective-permute-start | bytes 1572872 | tf_op jit(solution)/shard_map/ppermute | solution.py:35
  48.3 16.9 %collective-permute-start.14 = (f32[256,4,128]{2,1,0:T(4,128)}, f32[256,4,128]{2,1,0:T(4,128)}, u32[]{:S(2)}, u32[]{:S(2)}) collective-permute-start(f32[256,4,128]{2,1,0:T(4,128)} %collective-permute-done.3.refs_7_), channel_id=1, source_target_pairs={{0,64},{2,18},{4,68},{6,22},{8,72},{10,26},{12,76},{14,30},{16,80}... | collective-permute-start | bytes 1572872 | tf_op jit(solution)/shard_map/ppermute | solution.py:35
  48.3 16.8 %collective-permute-start.9 = (f32[256,4,128]{2,1,0:T(4,128)}, f32[256,4,128]{2,1,0:T(4,128)}, u32[]{:S(2)}, u32[]{:S(2)}) collective-permute-start(f32[256,4,128]{2,1,0:T(4,128)} %collective-permute-done.8.refs_11_), channel_id=1, source_target_pairs={{0,192},{2,51},{4,196},{6,55},{8,200},{10,59},{12,204},{14,63},{16... | collective-permute-start | bytes 1572872 | tf_op jit(solution)/shard_map/ppermute | solution.py:35
  75.2 8.6 %collective-permute-start.16 = (f32[16,64,128]{2,1,0:T(8,128)S(1)}, f32[16,64,128]{2,1,0:T(8,128)S(1)}, u32[]{:S(2)}, u32[]{:S(2)}) collective-permute-start(f32[16,64,128]{2,1,0:T(8,128)S(1)} %get-tuple-element.32), channel_id=1, source_target_pairs={{0,2},{2,0},{4,6},{6,4},{8,10},{10,8},{12,14},{14,12},{1,3},{3,1},... | collective-permute-start | bytes 1572872 | tf_op jit(solution)/shard_map/ppermute | solution.py:269
  83.9 8.6 %collective-permute-start.17 = (f32[4,64,128]{2,1,0:T(8,128)S(1)}, f32[4,64,128]{2,1,0:T(8,128)S(1)}, u32[]{:S(2)}, u32[]{:S(2)}) collective-permute-start(f32[4,64,128]{2,1,0:T(8,128)S(1)} %get-tuple-element.38), channel_id=1, source_target_pairs={{0,8},{2,10},{4,12},{6,14},{8,0},{10,2},{12,4},{14,6},{1,9},{3,11}... | collective-permute-start | bytes 393224 | tf_op jit(solution)/shard_map/ppermute | solution.py:274
  86.3 8.6 %collective-permute-start.18 = (f32[4,64,128]{2,1,0:T(8,128)S(1)}, f32[4,64,128]{2,1,0:T(8,128)S(1)}, u32[]{:S(2)}, u32[]{:S(2)}) collective-permute-start(f32[4,64,128]{2,1,0:T(8,128)S(1)} %get-tuple-element.40), channel_id=1, source_target_pairs={{0,4},{2,6},{4,8},{6,10},{8,12},{10,14},{12,0},{14,2},{1,5},{3,7},... | collective-permute-start | bytes 393224 | tf_op jit(solution)/shard_map/ppermute | solution.py:274
  86.3 8.6 %collective-permute-start.19 = (f32[4,64,128]{2,1,0:T(8,128)S(1)}, f32[4,64,128]{2,1,0:T(8,128)S(1)}, u32[]{:S(2)}, u32[]{:S(2)}) collective-permute-start(f32[4,64,128]{2,1,0:T(8,128)S(1)} %get-tuple-element.39), channel_id=1, source_target_pairs={{0,12},{2,14},{4,0},{6,2},{8,4},{10,6},{12,8},{14,10},{1,13},{3,15... | collective-permute-start | bytes 393224 | tf_op jit(solution)/shard_map/ppermute | solution.py:274
  88.4 9.1 %collective-permute-start.21 = (f32[4,64,128]{2,1,0:T(8,128)S(1)}, f32[4,64,128]{2,1,0:T(8,128)S(1)}, u32[]{:S(2)}, u32[]{:S(2)}) collective-permute-start(f32[4,64,128]{2,1,0:T(8,128)S(1)} %get-tuple-element.35), channel_id=1, source_target_pairs={{0,8},{2,10},{4,12},{6,14},{8,0},{10,2},{12,4},{14,6},{1,9},{3,11}... | collective-permute-start | bytes 393224 | tf_op jit(solution)/shard_map/ppermute | solution.py:274
  89.9 9.7 %collective-permute-start.22 = (f32[4,64,128]{2,1,0:T(8,128)S(1)}, f32[4,64,128]{2,1,0:T(8,128)S(1)}, u32[]{:S(2)}, u32[]{:S(2)}) collective-permute-start(f32[4,64,128]{2,1,0:T(8,128)S(1)} %get-tuple-element.37), channel_id=1, source_target_pairs={{0,4},{2,6},{4,8},{6,10},{8,12},{10,14},{12,0},{14,2},{1,5},{3,7},... | collective-permute-start | bytes 393224 | tf_op jit(solution)/shard_map/ppermute | solution.py:274
  94.9 12.1 %collective-permute-start.24 = (f32[4,64,128]{2,1,0:T(8,128)S(1)}, f32[4,64,128]{2,1,0:T(8,128)S(1)}, u32[]{:S(2)}, u32[]{:S(2)}) collective-permute-start(f32[4,64,128]{2,1,0:T(8,128)S(1)} %fusion.7), channel_id=1, source_target_pairs={{0,1},{1,0},{2,3},{3,2},{4,5},{5,4},{6,7},{7,6},{8,9},{9,8},{10,11... | collective-permute-start | bytes 393224 | tf_op jit(solution)/shard_map/ppermute | solution.py:275
  99.6 12.9 %collective-permute-start.25 = (f32[4,64,128]{2,1,0:T(8,128)S(1)}, f32[4,64,128]{2,1,0:T(8,128)S(1)}, u32[]{:S(2)}, u32[]{:S(2)}) collective-permute-start(f32[4,64,128]{2,1,0:T(8,128)S(1)} %fusion.4), channel_id=1, source_target_pairs={{0,1},{1,0},{2,3},{3,2},{4,5},{5,4},{6,7},{7,6},{8,9},{9,8},{10,11... | collective-permute-start | bytes 393224 | tf_op jit(solution)/shard_map/ppermute | solution.py:275
  (4 other events, 30.5 us)

commit v5 on v4

--- a/solution.py
+++ b/solution.py
@@ -12,7 +12,8 @@
 RING = 4
 CORES = 2
 CHUNKS = 2
-UNROLL = 4
+UNROLL = 8
+MIXES = 4
 FLIGHT = 5
 AXES = ("alpha", "beta", "ints")
 
@@ -77,7 +78,7 @@
     return ACROSS["_" + second if second else ""] * RING + ALONG[first]
 
 
-def assemble(copies, held, base_ref, *refs):
+def assemble(copies, base_ref, *refs):
     arrays, table, sems = refs[: len(copies)], refs[-2], refs[-1]
     dmas = []
     for n, slot in enumerate(copies):
@@ -89,16 +90,25 @@
         dma.wait()
 
 
-def kernel(
-    steps, pairs, slots,
-    table, src_ref, tgt_ref, sign_ref, vb_ref, off_ref, bs_ref, keep_hbm, give_hbm,
-    g_ref, y_ref, vhi_ref, vlo_ref, acc_ref, sem_out,
-):
+def kernel(steps, pairs, slots, copies, *refs):
+    src_ref, tgt_ref, sign_ref, vb_ref, off_ref, bs_ref, table = refs[:7]
+    late = len(copies)
+    keep_hbm, give_hbm, g_ref, y_ref, vhi_ref, vlo_ref, acc_ref, sem_out = refs[-8 - bool(late) :][:8]
+    dmas = []
+    if late:
+        base_ref, arrays, table, sems = refs[7], refs[8 : 8 + late], refs[8 + late], refs[-1]
+        for n, slot in enumerate(copies):
+            rows = arrays[n].shape[0]
+            dmas.append(pltpu.make_async_copy(arrays[n], table.at[pl.ds(base_ref[slot], rows)], sems.at[n]))
+    for dma in dmas:
+        dma.start()
     v = vb_ref[...]
     high = v.astype(jnp.bfloat16)
     vhi_ref[...] = high
     vlo_ref[...] = (v - high.astype(jnp.float32)).astype(jnp.bfloat16)
     acc_ref[...] = jnp.zeros_like(acc_ref)
+    for dma in dmas:
+        dma.wait()
     rows = GROUP * pairs
 
     def fetch(step, buffer):
@@ -124,15 +134,14 @@
 
     fetch(0, 0)
 
-    def two(half, carry):
-        step = half * 2
-        fetch(step + 1, 1)
-        mix(step, 0)
-        fetch(jnp.minimum(step + 2, steps - 1), 0)
-        mix(step + 1, 1)
+    def some_steps(part, carry):
+        for n in range(MIXES):
+            step = part * MIXES + n
+            fetch(jnp.minimum(step + 1, steps - 1), (n + 1) % 2)
+            mix(step, n % 2)
         return carry
 
-    lax.fori_loop(0, steps // 2, two, 0)
+    lax.fori_loop(0, steps // MIXES, some_steps, 0)
     lines = lax.broadcasted_iota(jnp.int32, (LANES, LANES), 0)
     tiles = acc_ref.shape[0]
 
@@ -220,19 +229,17 @@
     smem = pl.BlockSpec(memory_space=pltpu.SMEM)
     vmem = pl.BlockSpec(memory_space=pltpu.VMEM)
     hbm = pl.BlockSpec(memory_space=pl.ANY)
-    table = None
-    for names in (tuple(n for n in pieces if n not in LAST), LAST):
-        old = [] if table is None else [table]
-        table = pl.pallas_call(
-            functools.partial(assemble, tuple(slot_of(n) for n in names), len(old)),
-            out_shape=jax.ShapeDtypeStruct((lax.axis_size("alpha") * cols_a, slots, tile), jnp.float32),
-            in_specs=[smem] + [hbm] * len(names) + [vmem] * len(old),
-            out_specs=vmem,
-            scratch_shapes=[pltpu.SemaphoreType.DMA((len(names),))],
-            input_output_aliases={1 + len(names): 0} if old else {},
-            compiler_params=pltpu.CompilerParams(vmem_limit_bytes=12 * 1024 * 1024),
-            name="assemble",
-        )(base, *[pieces[n] for n in names], *old)
+    whole = jax.ShapeDtypeStruct((lax.axis_size("alpha") * cols_a, slots, tile), jnp.float32)
+    early = tuple(n for n in pieces if n not in LAST)
+    table = pl.pallas_call(
+        functools.partial(assemble, tuple(slot_of(n) for n in early)),
+        out_shape=whole,
+        in_specs=[smem] + [hbm] * len(early),
+        out_specs=vmem,
+        scratch_shapes=[pltpu.SemaphoreType.DMA((len(early),))],
+        compiler_params=pltpu.CompilerParams(vmem_limit_bytes=12 * 1024 * 1024),
+        name="assemble",
+    )(base, *[pieces[n] for n in early])
     width = cols // CHUNKS
     offsets = beta_offsets.reshape(pairs * tiles, tile)
     signs = beta_sign.reshape(pairs * tiles, tile)
@@ -241,11 +248,12 @@
     part_steps = steps // CHUNKS
     sums = []
     for chunk in range(CHUNKS):
-        keep, give = pl.pallas_call(
-            functools.partial(kernel, part_steps, pairs, slots),
-            out_shape=(half, half),
-            in_specs=[vmem] + [smem] * 2 + [vmem] * 4,
-            out_specs=(hbm, hbm),
+        late = LAST if chunk == 0 else ()
+        outs = pl.pallas_call(
+            functools.partial(kernel, part_steps, pairs, slots, tuple(slot_of(n) for n in late)),
+            out_shape=((whole,) if late else ()) + (half, half),
+            in_specs=[smem] * 2 + [vmem] * 5 + [smem] * bool(late) + [hbm] * len(late),
+            out_specs=((vmem,) if late else ()) + (hbm, hbm),
             scratch_shapes=[
                 pltpu.VMEM((2, GROUP * pairs, slots, tile), jnp.float32),
                 pltpu.VMEM((pairs, slots, width, tile), jnp.float32),
@@ -253,19 +261,27 @@
                 pltpu.VMEM((GROUP * pairs, GROUP * pairs), jnp.bfloat16),
                 pltpu.VMEM((tiles, width, tile), jnp.float32),
                 pltpu.SemaphoreType.DMA((2,)),
-            ],
+            ]
+            + [pltpu.SemaphoreType.DMA((len(late),))] * bool(late),
+            input_output_aliases={6: 0} if late else {},
             compiler_params=pltpu.CompilerParams(vmem_limit_bytes=12 * 1024 * 1024),
             cost_estimate=pl.CostEstimate(flops=4 * 10**9, bytes_accessed=2**23, transcendentals=0),
             name="sigma_partial",
         )(
-            table,
             lax.slice_in_dim(source, chunk * width * pairs, (chunk + 1) * width * pairs),
             target,
             lax.slice_in_dim(sign, chunk * part_steps, (chunk + 1) * part_steps),
             vb,
             offsets,
             signs,
+            table,
+            *([base] * bool(late)),
+            *[pieces[n] for n in late],
         )
+        if late:
+            table, keep, give = outs
+        else:
+            keep, give = outs
         came = lax.ppermute(give, "beta", across)
         total = keep[:slots] + came[:slots]
         for far in (2, 1, 3):

time: 114 us -> 109 us (0.956)
  waiting for transfers between devices: 38.1 us -> 28.1 us
  starting transfers between devices: 43.2 us -> 50 us
  Pallas kernels: 20.7 us -> 17.8 us
    ppermute x15, waiting for transfers between devices: 23.2 us -> 17.7 us  [move(): return lax.ppermute(value, AXES, pairs)]
    ppermute x2, starting transfers between devices: 4.97 us -> 9.47 us  [local(): sums.append((total, lax.ppermute(total, 'ints', swap)))]
    pallas_call x4 -> x3, Pallas kernels: 20.7 us -> 17.8 us  [the longest x2 15.2 us: local(): pl.pallas_call(functools.partial(kernel, part_steps, pairs, slots, tuple(...]
    ppermute x15, starting transfers between devices: 24.5 us -> 26.8 us  [move(): return lax.ppermute(value, AXES, pairs)]
    ppermute x6, waiting for transfers between devices: 4.58 us -> 2.3 us  [local(): total = total + lax.ppermute(part, 'beta', pairs_y)]
    ppermute x2, waiting for transfers between devices: 10.3 us -> 8.11 us  [local(): sums.append((total, lax.ppermute(total, 'ints', swap)))]
where the time goes in v5:
time: 109 us; the launch traced here: 108 us
  starting transfers between devices  50 us (46%)
  waiting for transfers between devices  28.1 us (26%)
  Pallas kernels  17.8 us (16%)
  local copies, waits for them, and re-layouts  6.81 us (6%)
  other arithmetic  4.6 us (4%)
    ppermute x15, starting transfers between devices, move(): return lax.ppermute(value, AXES, pairs)  26.8 us
    ppermute x15, waiting for transfers between devices, move(): return lax.ppermute(value, AXES, pairs)  17.7 us
    pallas_call x2, Pallas kernels, local(): pl.pallas_call(functools.partial(kernel, part_steps, pairs, slots, tuple(...  15.2 us
    ppermute x2, starting transfers between devices, local(): sums.append((total, lax.ppermute(total, 'ints', swap)))  9.47 us
    ppermute x6, starting transfers between devices, local(): total = total + lax.ppermute(part, 'beta', pairs_y)  8.52 us
    ppermute x2, waiting for transfers between devices, local(): sums.append((total, lax.ppermute(total, 'ints', swap)))  8.11 us
    ppermute x1, starting transfers between devices, spread(): held[name] = lax.ppermute(value, 'ints', [(0, 1), (1, 0)])  4.48 us
    pallas_call x1, Pallas kernels, local(): pl.pallas_call(functools.partial(assemble, tuple((slot_of(n) for n in ear...  2.67 us
  transfers between devices with their start and end apart: 26, of which 12 were waited for; matrix products, arithmetic and copies ran while one was open for 8% of the time, Pallas kernels for 9%

profile of v5, /device:TPU:8, one launch (start us, length us, event | category | flops | bytes accessed | tf_op | source)
XLA Modules:
  0.0 107.5 jit_solution(17381270151642024311)
XLA Ops:
  1.3 2.0 %collective-permute-start.3 = (f32[256,4,128]{2,1,0:T(4,128)S(1)}, f32[256,4,128]{2,1,0:T(4,128)S(1)}, u32[]{:S(2)}, u32[]{:S(2)}) collective-permute-start(f32[256,4,128]{2,1,0:T(4,128)S(1)} %copy.28.refs_0_), channel_id=1, source_target_pairs={{0,16},{2,66},{4,20},{6,70},{8,24},{10,74},{12,28},{14,78},{16,32}... | collective-permute-start | bytes 1572872 | tf_op jit(solution)/shard_map/ppermute | solution.py:36
  3.3 4.0 %collective-permute-start.2 = (f32[256,4,128]{2,1,0:T(4,128)S(1)}, f32[256,4,128]{2,1,0:T(4,128)S(1)}, u32[]{:S(2)}, u32[]{:S(2)}) collective-permute-start(f32[256,4,128]{2,1,0:T(4,128)S(1)} %copy.28.refs_0_), channel_id=1, source_target_pairs={{0,49},{2,194},{4,53},{6,198},{8,57},{10,202},{12,61},{14,206},{16... | collective-permute-start | bytes 1572872 | tf_op jit(solution)/shard_map/ppermute | solution.py:36
  10.2 4.5 %collective-permute-start = (f32[48,128]{1,0:T(8,128)S(1)}, f32[48,128]{1,0:T(8,128)S(1)}, u32[]{:S(2)}, u32[]{:S(2)}) collective-permute-start(f32[48,128]{1,0:T(8,128)S(1)} %select_maximum_fusion), channel_id=1, source_target_pairs={{0,1},{1,0},{2,3},{3,2},{4,5},{5,4},{6,7},{7,6},{8,9},{9,8},{10,11... | collective-permute-start | bytes 73736 | tf_op jit(solution)/shard_map/ppermute | solution.py:69
  15.9 2.1 %collective-permute-start.4 = (f32[256,4,128]{2,1,0:T(4,128)S(1)}, f32[256,4,128]{2,1,0:T(4,128)S(1)}, u32[]{:S(2)}, u32[]{:S(2)}) collective-permute-start(f32[256,4,128]{2,1,0:T(4,128)S(1)} %collective-permute-done.2.refs_2_), channel_id=1, source_target_pairs={{0,49},{2,194},{4,53},{6,198},{8,57},{10,202},{12,61},{14,206},{16... | collective-permute-start | bytes 1572872 | tf_op jit(solution)/shard_map/ppermute | solution.py:36
  18.0 3.2 %collective-permute-start.6 = (f32[256,4,128]{2,1,0:T(4,128)S(1)}, f32[256,4,128]{2,1,0:T(4,128)S(1)}, u32[]{:S(2)}, u32[]{:S(2)}) collective-permute-start(f32[256,4,128]{2,1,0:T(4,128)S(1)} %collective-permute-done.2.refs_2_), channel_id=1, source_target_pairs={{0,192},{2,51},{4,196},{6,55},{8,200},{10,59},{12,204},{14,63},{16... | collective-permute-start | bytes 1572872 | tf_op jit(solution)/shard_map/ppermute | solution.py:36
  21.3 1.9 %reshape.53.refs_5_ = s32[1024,128]{1,0:T(8,128)} reshape(s32[32,4096]{1,0:T(8,128)} %param.13) | data formatting | bytes 1048576 | tf_op jit(solution)/shard_map/reshape | solution.py:245
  24.1 2.4 %collective-permute-start.8 = (f32[256,4,128]{2,1,0:T(4,128)S(1)}, f32[256,4,128]{2,1,0:T(4,128)}, u32[]{:S(2)}, u32[]{:S(2)}) collective-permute-start(f32[256,4,128]{2,1,0:T(4,128)S(1)} %collective-permute-done.3.refs_3_), channel_id=1, source_target_pairs={{0,192},{2,51},{4,196},{6,55},{8,200},{10,59},{12,204},{14,63},{16... | collective-permute-start | bytes 1572872 | tf_op jit(solution)/shard_map/ppermute | solution.py:36
  28.1 3.6 %collective-permute-start.11 = (f32[256,4,128]{2,1,0:T(4,128)S(1)}, f32[256,4,128]{2,1,0:T(4,128)}, u32[]{:S(2)}, u32[]{:S(2)}) collective-permute-start(f32[256,4,128]{2,1,0:T(4,128)S(1)} %collective-permute-done.4.refs_4_), channel_id=1, source_target_pairs={{0,192},{2,51},{4,196},{6,55},{8,200},{10,59},{12,204},{14,63},{16... | collective-permute-start | bytes 1572872 | tf_op jit(solution)/shard_map/ppermute | solution.py:36
  33.8 3.6 %collective-permute-start.14 = (f32[256,4,128]{2,1,0:T(4,128)S(1)}, f32[256,4,128]{2,1,0:T(4,128)}, u32[]{:S(2)}, u32[]{:S(2)}) collective-permute-start(f32[256,4,128]{2,1,0:T(4,128)S(1)} %copy.28.refs_0_), channel_id=1, source_target_pairs={{0,192},{2,51},{4,196},{6,55},{8,200},{10,59},{12,204},{14,63},{16... | collective-permute-start | bytes 1572872 | tf_op jit(solution)/shard_map/ppermute | solution.py:36
  37.4 2.1 %collective-permute-done.5.refs_5_ = f32[256,4,128]{2,1,0:T(4,128)} collective-permute-done((f32[256,4,128]{2,1,0:T(4,128)S(1)}, f32[256,4,128]{2,1,0:T(4,128)}, u32[]{:S(2)}, u32[]{:S(2)}) %collective-permute-start.5) | collective-permute-done | bytes 524320 | tf_op jit(solution)/shard_map/ppermute | solution.py:36
  40.5 2.4 %collective-permute-start.13 = (f32[256,4,128]{2,1,0:T(4,128)}, f32[256,4,128]{2,1,0:T(4,128)}, u32[]{:S(2)}, u32[]{:S(2)}) collective-permute-start(f32[256,4,128]{2,1,0:T(4,128)} %collective-permute-done.11.refs_11_), channel_id=1, source_target_pairs={{0,192},{2,51},{4,196},{6,55},{8,200},{10,59},{12,204},{14,63},{16... | collective-permute-start | bytes 1572872 | tf_op jit(solution)/shard_map/ppermute | solution.py:36
  43.0 2.1 %collective-permute-done.9.refs_9_ = f32[256,4,128]{2,1,0:T(4,128)} collective-permute-done((f32[256,4,128]{2,1,0:T(4,128)S(1)}, f32[256,4,128]{2,1,0:T(4,128)}, u32[]{:S(2)}, u32[]{:S(2)}) %collective-permute-start.9) | collective-permute-done | bytes 524320 | tf_op jit(solution)/shard_map/ppermute | solution.py:36
  48.9 1.8 %collective-permute-done.10.refs_10_ = f32[256,4,128]{2,1,0:T(4,128)} collective-permute-done((f32[256,4,128]{2,1,0:T(4,128)S(1)}, f32[256,4,128]{2,1,0:T(4,128)}, u32[]{:S(2)}, u32[]{:S(2)}) %collective-permute-start.10) | collective-permute-done | bytes 524320 | tf_op jit(solution)/shard_map/ppermute | solution.py:36
  50.7 2.7 %assemble.1.refs_6_ = f32[4096,4,128]{2,1,0:T(4,128)S(1)} custom-call(s32[16]{0:T(128)S(1)} %fusion.21.base_ref.refs_7_, f32[256,4,128]{2,1,0:T(4,128)S(1)} %copy.28.refs_0_, f32[256,4,128]{2,1,0:T(4,128)S(1)} %collective-permute-done.1.refs_1_, f32[256,4,128]{2,1,0:T(4,128)S(1)} %collective-permute-done.2.refs_2_, ...), custom_call_target="tpu_custom_call" | custom-call | tf_op jit(solution)/shard_map/assemble/pallas_call | solution.py:234
  53.3 2.9 %collective-permute-done.12.refs_8_ = f32[256,4,128]{2,1,0:T(4,128)} collective-permute-done((f32[256,4,128]{2,1,0:T(4,128)}, f32[256,4,128]{2,1,0:T(4,128)}, u32[]{:S(2)}, u32[]{:S(2)}) %collective-permute-start.12) | collective-permute-done | bytes 524320 | tf_op jit(solution)/shard_map/ppermute | solution.py:36
  56.3 5.6 %collective-permute-done.15.refs_11_ = f32[256,4,128]{2,1,0:T(4,128)} collective-permute-done((f32[256,4,128]{2,1,0:T(4,128)}, f32[256,4,128]{2,1,0:T(4,128)}, u32[]{:S(2)}, u32[]{:S(2)}) %collective-permute-start.15) | collective-permute-done | bytes 524320 | tf_op jit(solution)/shard_map/ppermute | solution.py:36
  61.9 8.3 %sigma_partial.2 = (f32[4096,4,128]{2,1,0:T(4,128)S(1)}, f32[16,64,128]{2,1,0:T(8,128)S(1)}, f32[16,64,128]{2,1,0:T(8,128)S(1)}) custom-call(s32[2048]{0:T(1024)S(1)} %slice.89.refs_0_, s32[256]{0:T(256)S(1)} %pad_add_fusion.refs_1_, f32[8,256]{1,0:T(8,128)S(1)} %slice.91.refs_2_, f32[256,256]{1,0:T(8,128)S(1)} %mul.51.refs_3_, ...), custom_call_target="tpu_custom_call", output_to_operand_aliasing={{0}: (6, {})} | custom-call | flops 4000000000 | bytes 8388608 | tf_op jit(solution)/shard_map/sigma_partial/pallas_call | solution.py:252
  70.3 6.8 %sigma_partial.3 = (f32[16,64,128]{2,1,0:T(8,128)S(1)}, f32[16,64,128]{2,1,0:T(8,128)S(1)}) custom-call(s32[2048]{0:T(1024)S(1)} %slice.102.refs_0_, s32[256]{0:T(256)S(1)} %pad_add_fusion.refs_1_, f32[8,256]{1,0:T(8,128)S(1)} %slice.104.refs_2_, f32[256,256]{1,0:T(8,128)S(1)} %mul.51.refs_3_, s32[1024,128]{1,0:T(8,128)S(1)} %bitcast.18, ...), custom_call_target="tpu_custom_call" | custom-call | flops 4000000000 | bytes 8388608 | tf_op jit(solution)/shard_map/sigma_partial/pallas_call | solution.py:252
  77.8 2.4 %collective-permute-start.17 = (f32[4,64,128]{2,1,0:T(8,128)S(1)}, f32[4,64,128]{2,1,0:T(8,128)S(1)}, u32[]{:S(2)}, u32[]{:S(2)}) collective-permute-start(f32[4,64,128]{2,1,0:T(8,128)S(1)} %get-tuple-element.40), channel_id=1, source_target_pairs={{0,8},{2,10},{4,12},{6,14},{8,0},{10,2},{12,4},{14,6},{1,9},{3,11}... | collective-permute-start | bytes 393224 | tf_op jit(solution)/shard_map/ppermute | solution.py:290
  82.3 2.5 %collective-permute-start.21 = (f32[4,64,128]{2,1,0:T(8,128)S(1)}, f32[4,64,128]{2,1,0:T(8,128)S(1)}, u32[]{:S(2)}, u32[]{:S(2)}) collective-permute-start(f32[4,64,128]{2,1,0:T(8,128)S(1)} %get-tuple-element.37), channel_id=1, source_target_pairs={{0,8},{2,10},{4,12},{6,14},{8,0},{10,2},{12,4},{14,6},{1,9},{3,11}... | collective-permute-start | bytes 393224 | tf_op jit(solution)/shard_map/ppermute | solution.py:290
  88.8 4.8 %collective-permute-start.24 = (f32[4,64,128]{2,1,0:T(8,128)S(1)}, f32[4,64,128]{2,1,0:T(8,128)S(1)}, u32[]{:S(2)}, u32[]{:S(2)}) collective-permute-start(f32[4,64,128]{2,1,0:T(8,128)S(1)} %fusion.7), channel_id=1, source_target_pairs={{0,1},{1,0},{2,3},{3,2},{4,5},{5,4},{6,7},{7,6},{8,9},{9,8},{10,11... | collective-permute-start | bytes 393224 | tf_op jit(solution)/shard_map/ppermute | solution.py:291
  93.7 4.6 %collective-permute-start.25 = (f32[4,64,128]{2,1,0:T(8,128)S(1)}, f32[4,64,128]{2,1,0:T(8,128)S(1)}, u32[]{:S(2)}, u32[]{:S(2)}) collective-permute-start(f32[4,64,128]{2,1,0:T(8,128)S(1)} %fusion.4), channel_id=1, source_target_pairs={{0,1},{1,0},{2,3},{3,2},{4,5},{5,4},{6,7},{7,6},{8,9},{9,8},{10,11... | collective-permute-start | bytes 393224 | tf_op jit(solution)/shard_map/ppermute | solution.py:291
  98.3 3.0 %collective-permute-done.24 = f32[4,64,128]{2,1,0:T(8,128)S(1)} collective-permute-done((f32[4,64,128]{2,1,0:T(8,128)S(1)}, f32[4,64,128]{2,1,0:T(8,128)S(1)}, u32[]{:S(2)}, u32[]{:S(2)}) %collective-permute-start.24) | collective-permute-done | bytes 131104 | tf_op jit(solution)/shard_map/ppermute | solution.py:291
  101.3 5.2 %collective-permute-done.25 = f32[4,64,128]{2,1,0:T(8,128)S(1)} collective-permute-done((f32[4,64,128]{2,1,0:T(8,128)S(1)}, f32[4,64,128]{2,1,0:T(8,128)S(1)}, u32[]{:S(2)}, u32[]{:S(2)}) %collective-permute-start.25) | collective-permute-done | bytes 131104 | tf_op jit(solution)/shard_map/ppermute | solution.py:291
  (76 shorter events, 22.8 us)
Async XLA Ops:
  1.3 21.9 %collective-permute-start.3 = (f32[256,4,128]{2,1,0:T(4,128)S(1)}, f32[256,4,128]{2,1,0:T(4,128)S(1)}, u32[]{:S(2)}, u32[]{:S(2)}) collective-permute-start(f32[256,4,128]{2,1,0:T(4,128)S(1)} %copy.28.refs_0_), channel_id=1, source_target_pairs={{0,16},{2,66},{4,20},{6,70},{8,24},{10,74},{12,28},{14,78},{16,32}... | collective-permute-start | bytes 1572872 | tf_op jit(solution)/shard_map/ppermute | solution.py:36
  3.3 12.6 %collective-permute-start.2 = (f32[256,4,128]{2,1,0:T(4,128)S(1)}, f32[256,4,128]{2,1,0:T(4,128)S(1)}, u32[]{:S(2)}, u32[]{:S(2)}) collective-permute-start(f32[256,4,128]{2,1,0:T(4,128)S(1)} %copy.28.refs_0_), channel_id=1, source_target_pairs={{0,49},{2,194},{4,53},{6,198},{8,57},{10,202},{12,61},{14,206},{16... | collective-permute-start | bytes 1572872 | tf_op jit(solution)/shard_map/ppermute | solution.py:36
  7.3 10.7 %collective-permute-start.1 = (f32[256,4,128]{2,1,0:T(4,128)S(1)}, f32[256,4,128]{2,1,0:T(4,128)S(1)}, u32[]{:S(2)}, u32[]{:S(2)}) collective-permute-start(f32[256,4,128]{2,1,0:T(4,128)S(1)} %copy.28.refs_0_), channel_id=1, source_target_pairs={{0,64},{2,18},{4,68},{6,22},{8,72},{10,26},{12,76},{14,30},{16,80}... | collective-permute-start | bytes 1572872 | tf_op jit(solution)/shard_map/ppermute | solution.py:36
  10.2 13.0 %collective-permute-start = (f32[48,128]{1,0:T(8,128)S(1)}, f32[48,128]{1,0:T(8,128)S(1)}, u32[]{:S(2)}, u32[]{:S(2)}) collective-permute-start(f32[48,128]{1,0:T(8,128)S(1)} %select_maximum_fusion), channel_id=1, source_target_pairs={{0,1},{1,0},{2,3},{3,2},{4,5},{5,4},{6,7},{7,6},{8,9},{9,8},{10,11... | collective-permute-start | bytes 73736 | tf_op jit(solution)/shard_map/ppermute | solution.py:69
  15.9 11.8 %collective-permute-start.4 = (f32[256,4,128]{2,1,0:T(4,128)S(1)}, f32[256,4,128]{2,1,0:T(4,128)S(1)}, u32[]{:S(2)}, u32[]{:S(2)}) collective-permute-start(f32[256,4,128]{2,1,0:T(4,128)S(1)} %collective-permute-done.2.refs_2_), channel_id=1, source_target_pairs={{0,49},{2,194},{4,53},{6,198},{8,57},{10,202},{12,61},{14,206},{16... | collective-permute-start | bytes 1572872 | tf_op jit(solution)/shard_map/ppermute | solution.py:36
  18.0 10.1 %collective-permute-start.6 = (f32[256,4,128]{2,1,0:T(4,128)S(1)}, f32[256,4,128]{2,1,0:T(4,128)S(1)}, u32[]{:S(2)}, u32[]{:S(2)}) collective-permute-start(f32[256,4,128]{2,1,0:T(4,128)S(1)} %collective-permute-done.2.refs_2_), channel_id=1, source_target_pairs={{0,192},{2,51},{4,196},{6,55},{8,200},{10,59},{12,204},{14,63},{16... | collective-permute-start | bytes 1572872 | tf_op jit(solution)/shard_map/ppermute | solution.py:36
  23.2 14.1 %collective-permute-start.7 = (f32[256,4,128]{2,1,0:T(4,128)S(1)}, f32[256,4,128]{2,1,0:T(4,128)}, u32[]{:S(2)}, u32[]{:S(2)}) collective-permute-start(f32[256,4,128]{2,1,0:T(4,128)S(1)} %collective-permute-done.3.refs_3_), channel_id=1, source_target_pairs={{0,64},{2,18},{4,68},{6,22},{8,72},{10,26},{12,76},{14,30},{16,80}... | collective-permute-start | bytes 1572872 | tf_op jit(solution)/shard_map/ppermute | solution.py:36
  24.1 9.7 %collective-permute-start.8 = (f32[256,4,128]{2,1,0:T(4,128)S(1)}, f32[256,4,128]{2,1,0:T(4,128)}, u32[]{:S(2)}, u32[]{:S(2)}) collective-permute-start(f32[256,4,128]{2,1,0:T(4,128)S(1)} %collective-permute-done.3.refs_3_), channel_id=1, source_target_pairs={{0,192},{2,51},{4,196},{6,55},{8,200},{10,59},{12,204},{14,63},{16... | collective-permute-start | bytes 1572872 | tf_op jit(solution)/shard_map/ppermute | solution.py:36
  26.5 12.9 %collective-permute-start.5 = (f32[256,4,128]{2,1,0:T(4,128)S(1)}, f32[256,4,128]{2,1,0:T(4,128)}, u32[]{:S(2)}, u32[]{:S(2)}) collective-permute-start(f32[256,4,128]{2,1,0:T(4,128)S(1)} %collective-permute-done.2.refs_2_), channel_id=1, source_target_pairs={{0,64},{2,18},{4,68},{6,22},{8,72},{10,26},{12,76},{14,30},{16,80}... | collective-permute-start | bytes 1572872 | tf_op jit(solution)/shard_map/ppermute | solution.py:36
  28.1 12.5 %collective-permute-start.11 = (f32[256,4,128]{2,1,0:T(4,128)S(1)}, f32[256,4,128]{2,1,0:T(4,128)}, u32[]{:S(2)}, u32[]{:S(2)}) collective-permute-start(f32[256,4,128]{2,1,0:T(4,128)S(1)} %collective-permute-done.4.refs_4_), channel_id=1, source_target_pairs={{0,192},{2,51},{4,196},{6,55},{8,200},{10,59},{12,204},{14,63},{16... | collective-permute-start | bytes 1572872 | tf_op jit(solution)/shard_map/ppermute | solution.py:36
  31.6 13.4 %collective-permute-start.9 = (f32[256,4,128]{2,1,0:T(4,128)S(1)}, f32[256,4,128]{2,1,0:T(4,128)}, u32[]{:S(2)}, u32[]{:S(2)}) collective-permute-start(f32[256,4,128]{2,1,0:T(4,128)S(1)} %collective-permute-done.1.refs_1_), channel_id=1, source_target_pairs={{0,64},{2,18},{4,68},{6,22},{8,72},{10,26},{12,76},{14,30},{16,80}... | collective-permute-start | bytes 1572872 | tf_op jit(solution)/shard_map/ppermute | solution.py:36
  33.8 19.5 %collective-permute-start.14 = (f32[256,4,128]{2,1,0:T(4,128)S(1)}, f32[256,4,128]{2,1,0:T(4,128)}, u32[]{:S(2)}, u32[]{:S(2)}) collective-permute-start(f32[256,4,128]{2,1,0:T(4,128)S(1)} %copy.28.refs_0_), channel_id=1, source_target_pairs={{0,192},{2,51},{4,196},{6,55},{8,200},{10,59},{12,204},{14,63},{16... | collective-permute-start | bytes 1572872 | tf_op jit(solution)/shard_map/ppermute | solution.py:36
  39.4 11.2 %collective-permute-start.10 = (f32[256,4,128]{2,1,0:T(4,128)S(1)}, f32[256,4,128]{2,1,0:T(4,128)}, u32[]{:S(2)}, u32[]{:S(2)}) collective-permute-start(f32[256,4,128]{2,1,0:T(4,128)S(1)} %collective-permute-done.4.refs_4_), channel_id=1, source_target_pairs={{0,64},{2,18},{4,68},{6,22},{8,72},{10,26},{12,76},{14,30},{16,80}... | collective-permute-start | bytes 1572872 | tf_op jit(solution)/shard_map/ppermute | solution.py:36
  39.4 16.8 %collective-permute-start.12 = (f32[256,4,128]{2,1,0:T(4,128)}, f32[256,4,128]{2,1,0:T(4,128)}, u32[]{:S(2)}, u32[]{:S(2)}) collective-permute-start(f32[256,4,128]{2,1,0:T(4,128)} %collective-permute-done.5.refs_5_), channel_id=1, source_target_pairs={{0,64},{2,18},{4,68},{6,22},{8,72},{10,26},{12,76},{14,30},{16,80}... | collective-permute-start | bytes 1572872 | tf_op jit(solution)/shard_map/ppermute | solution.py:36
  40.5 15.8 %collective-permute-start.13 = (f32[256,4,128]{2,1,0:T(4,128)}, f32[256,4,128]{2,1,0:T(4,128)}, u32[]{:S(2)}, u32[]{:S(2)}) collective-permute-start(f32[256,4,128]{2,1,0:T(4,128)} %collective-permute-done.11.refs_11_), channel_id=1, source_target_pairs={{0,192},{2,51},{4,196},{6,55},{8,200},{10,59},{12,204},{14,63},{16... | collective-permute-start | bytes 1572872 | tf_op jit(solution)/shard_map/ppermute | solution.py:36
  45.0 16.9 %collective-permute-start.15 = (f32[256,4,128]{2,1,0:T(4,128)}, f32[256,4,128]{2,1,0:T(4,128)}, u32[]{:S(2)}, u32[]{:S(2)}) collective-permute-start(f32[256,4,128]{2,1,0:T(4,128)} %collective-permute-done.7.refs_7_), channel_id=1, source_target_pairs={{0,64},{2,18},{4,68},{6,22},{8,72},{10,26},{12,76},{14,30},{16,80}... | collective-permute-start | bytes 1572872 | tf_op jit(solution)/shard_map/ppermute | solution.py:36
  70.2 7.6 %collective-permute-start.16 = (f32[16,64,128]{2,1,0:T(8,128)S(1)}, f32[16,64,128]{2,1,0:T(8,128)S(1)}, u32[]{:S(2)}, u32[]{:S(2)}) collective-permute-start(f32[16,64,128]{2,1,0:T(8,128)S(1)} %get-tuple-element.33), channel_id=1, source_target_pairs={{0,2},{2,0},{4,6},{6,4},{8,10},{10,8},{12,14},{14,12},{1,3},{3,1},... | collective-permute-start | bytes 1572872 | tf_op jit(solution)/shard_map/ppermute | solution.py:285
  77.8 7.9 %collective-permute-start.17 = (f32[4,64,128]{2,1,0:T(8,128)S(1)}, f32[4,64,128]{2,1,0:T(8,128)S(1)}, u32[]{:S(2)}, u32[]{:S(2)}) collective-permute-start(f32[4,64,128]{2,1,0:T(8,128)S(1)} %get-tuple-element.40), channel_id=1, source_target_pairs={{0,8},{2,10},{4,12},{6,14},{8,0},{10,2},{12,4},{14,6},{1,9},{3,11}... | collective-permute-start | bytes 393224 | tf_op jit(solution)/shard_map/ppermute | solution.py:290
  80.2 8.5 %collective-permute-start.19 = (f32[4,64,128]{2,1,0:T(8,128)S(1)}, f32[4,64,128]{2,1,0:T(8,128)S(1)}, u32[]{:S(2)}, u32[]{:S(2)}) collective-permute-start(f32[4,64,128]{2,1,0:T(8,128)S(1)} %get-tuple-element.41), channel_id=1, source_target_pairs={{0,12},{2,14},{4,0},{6,2},{8,4},{10,6},{12,8},{14,10},{1,13},{3,15... | collective-permute-start | bytes 393224 | tf_op jit(solution)/shard_map/ppermute | solution.py:290
  82.3 11.3 %collective-permute-start.21 = (f32[4,64,128]{2,1,0:T(8,128)S(1)}, f32[4,64,128]{2,1,0:T(8,128)S(1)}, u32[]{:S(2)}, u32[]{:S(2)}) collective-permute-start(f32[4,64,128]{2,1,0:T(8,128)S(1)} %get-tuple-element.37), channel_id=1, source_target_pairs={{0,8},{2,10},{4,12},{6,14},{8,0},{10,2},{12,4},{14,6},{1,9},{3,11}... | collective-permute-start | bytes 393224 | tf_op jit(solution)/shard_map/ppermute | solution.py:290
  84.8 8.8 %collective-permute-start.23 = (f32[4,64,128]{2,1,0:T(8,128)S(1)}, f32[4,64,128]{2,1,0:T(8,128)S(1)}, u32[]{:S(2)}, u32[]{:S(2)}) collective-permute-start(f32[4,64,128]{2,1,0:T(8,128)S(1)} %get-tuple-element.38), channel_id=1, source_target_pairs={{0,12},{2,14},{4,0},{6,2},{8,4},{10,6},{12,8},{14,10},{1,13},{3,15... | collective-permute-start | bytes 393224 | tf_op jit(solution)/shard_map/ppermute | solution.py:290
  85.8 7.8 %collective-permute-start.22 = (f32[4,64,128]{2,1,0:T(8,128)S(1)}, f32[4,64,128]{2,1,0:T(8,128)S(1)}, u32[]{:S(2)}, u32[]{:S(2)}) collective-permute-start(f32[4,64,128]{2,1,0:T(8,128)S(1)} %get-tuple-element.39), channel_id=1, source_target_pairs={{0,4},{2,6},{4,8},{6,10},{8,12},{10,14},{12,0},{14,2},{1,5},{3,7},... | collective-permute-start | bytes 393224 | tf_op jit(solution)/shard_map/ppermute | solution.py:290
  88.8 12.5 %collective-permute-start.24 = (f32[4,64,128]{2,1,0:T(8,128)S(1)}, f32[4,64,128]{2,1,0:T(8,128)S(1)}, u32[]{:S(2)}, u32[]{:S(2)}) collective-permute-start(f32[4,64,128]{2,1,0:T(8,128)S(1)} %fusion.7), channel_id=1, source_target_pairs={{0,1},{1,0},{2,3},{3,2},{4,5},{5,4},{6,7},{7,6},{8,9},{9,8},{10,11... | collective-permute-start | bytes 393224 | tf_op jit(solution)/shard_map/ppermute | solution.py:291
  93.7 12.8 %collective-permute-start.25 = (f32[4,64,128]{2,1,0:T(8,128)S(1)}, f32[4,64,128]{2,1,0:T(8,128)S(1)}, u32[]{:S(2)}, u32[]{:S(2)}) collective-permute-start(f32[4,64,128]{2,1,0:T(8,128)S(1)} %fusion.4), channel_id=1, source_target_pairs={{0,1},{1,0},{2,3},{3,2},{4,5},{5,4},{6,7},{7,6},{8,9},{9,8},{10,11... | collective-permute-start | bytes 393224 | tf_op jit(solution)/shard_map/ppermute | solution.py:291
  (4 other events, 38.3 us)

commit v6 on v5

--- a/solution.py
+++ b/solution.py
@@ -12,8 +12,8 @@
 RING = 4
 CORES = 2
 CHUNKS = 2
-UNROLL = 8
-MIXES = 4
+UNROLL = 16
+MIXES = 8
 FLIGHT = 5
 AXES = ("alpha", "beta", "ints")
 

time: 109 us -> 107 us (0.982)
  Pallas kernels: 17.8 us -> 15.8 us
    pallas_call x2, Pallas kernels: 15.2 us -> 13.2 us  [local(): pl.pallas_call(functools.partial(kernel, part_steps, pairs, slots, tuple(...]
  transfers between devices with their start and end apart: 26 -> 26, of which waited for: 12 -> 12; matrix products, arithmetic and copies ran while one was open for 8% -> 9% of each run, Pallas kernels for 9% -> 8%
where the time goes in v6:
time: 107 us; the launch traced here: 106 us
  starting transfers between devices  50.2 us (47%)
  waiting for transfers between devices  27.9 us (26%)
  Pallas kernels  15.8 us (15%)
  local copies, waits for them, and re-layouts  6.81 us (6%)
  other arithmetic  4.6 us (4%)
    ppermute x15, starting transfers between devices, move(): return lax.ppermute(value, AXES, pairs)  26.8 us
    ppermute x15, waiting for transfers between devices, move(): return lax.ppermute(value, AXES, pairs)  17.7 us
    pallas_call x2, Pallas kernels, local(): pl.pallas_call(functools.partial(kernel, part_steps, pairs, slots, tuple(...  13.2 us
    ppermute x2, starting transfers between devices, local(): sums.append((total, lax.ppermute(total, 'ints', swap)))  9.48 us
    ppermute x6, starting transfers between devices, local(): total = total + lax.ppermute(part, 'beta', pairs_y)  8.74 us
    ppermute x2, waiting for transfers between devices, local(): sums.append((total, lax.ppermute(total, 'ints', swap)))  8.12 us
    ppermute x1, starting transfers between devices, spread(): held[name] = lax.ppermute(value, 'ints', [(0, 1), (1, 0)])  4.48 us
    pallas_call x1, Pallas kernels, local(): pl.pallas_call(functools.partial(assemble, tuple((slot_of(n) for n in ear...  2.67 us
  transfers between devices with their start and end apart: 26, of which 12 were waited for; matrix products, arithmetic and copies ran while one was open for 9% of the time, Pallas kernels for 8%

profile of v6, /device:TPU:8, one launch (start us, length us, event | category | flops | bytes accessed | tf_op | source)
XLA Modules:
  0.0 105.5 jit_solution(14324958923138564462)
XLA Ops:
  1.3 2.0 %collective-permute-start.3 = (f32[256,4,128]{2,1,0:T(4,128)S(1)}, f32[256,4,128]{2,1,0:T(4,128)S(1)}, u32[]{:S(2)}, u32[]{:S(2)}) collective-permute-start(f32[256,4,128]{2,1,0:T(4,128)S(1)} %copy.28.refs_0_), channel_id=1, source_target_pairs={{0,16},{2,66},{4,20},{6,70},{8,24},{10,74},{12,28},{14,78},{16,32}... | collective-permute-start | bytes 1572872 | tf_op jit(solution)/shard_map/ppermute | solution.py:36
  3.3 4.0 %collective-permute-start.2 = (f32[256,4,128]{2,1,0:T(4,128)S(1)}, f32[256,4,128]{2,1,0:T(4,128)S(1)}, u32[]{:S(2)}, u32[]{:S(2)}) collective-permute-start(f32[256,4,128]{2,1,0:T(4,128)S(1)} %copy.28.refs_0_), channel_id=1, source_target_pairs={{0,49},{2,194},{4,53},{6,198},{8,57},{10,202},{12,61},{14,206},{16... | collective-permute-start | bytes 1572872 | tf_op jit(solution)/shard_map/ppermute | solution.py:36
  10.2 4.5 %collective-permute-start = (f32[48,128]{1,0:T(8,128)S(1)}, f32[48,128]{1,0:T(8,128)S(1)}, u32[]{:S(2)}, u32[]{:S(2)}) collective-permute-start(f32[48,128]{1,0:T(8,128)S(1)} %select_maximum_fusion), channel_id=1, source_target_pairs={{0,1},{1,0},{2,3},{3,2},{4,5},{5,4},{6,7},{7,6},{8,9},{9,8},{10,11... | collective-permute-start | bytes 73736 | tf_op jit(solution)/shard_map/ppermute | solution.py:69
  15.9 2.1 %collective-permute-start.4 = (f32[256,4,128]{2,1,0:T(4,128)S(1)}, f32[256,4,128]{2,1,0:T(4,128)S(1)}, u32[]{:S(2)}, u32[]{:S(2)}) collective-permute-start(f32[256,4,128]{2,1,0:T(4,128)S(1)} %collective-permute-done.2.refs_2_), channel_id=1, source_target_pairs={{0,49},{2,194},{4,53},{6,198},{8,57},{10,202},{12,61},{14,206},{16... | collective-permute-start | bytes 1572872 | tf_op jit(solution)/shard_map/ppermute | solution.py:36
  18.0 3.2 %collective-permute-start.6 = (f32[256,4,128]{2,1,0:T(4,128)S(1)}, f32[256,4,128]{2,1,0:T(4,128)S(1)}, u32[]{:S(2)}, u32[]{:S(2)}) collective-permute-start(f32[256,4,128]{2,1,0:T(4,128)S(1)} %collective-permute-done.2.refs_2_), channel_id=1, source_target_pairs={{0,192},{2,51},{4,196},{6,55},{8,200},{10,59},{12,204},{14,63},{16... | collective-permute-start | bytes 1572872 | tf_op jit(solution)/shard_map/ppermute | solution.py:36
  21.3 1.9 %reshape.53.refs_5_ = s32[1024,128]{1,0:T(8,128)} reshape(s32[32,4096]{1,0:T(8,128)} %param.13) | data formatting | bytes 1048576 | tf_op jit(solution)/shard_map/reshape | solution.py:245
  24.1 2.4 %collective-permute-start.8 = (f32[256,4,128]{2,1,0:T(4,128)S(1)}, f32[256,4,128]{2,1,0:T(4,128)}, u32[]{:S(2)}, u32[]{:S(2)}) collective-permute-start(f32[256,4,128]{2,1,0:T(4,128)S(1)} %collective-permute-done.3.refs_3_), channel_id=1, source_target_pairs={{0,192},{2,51},{4,196},{6,55},{8,200},{10,59},{12,204},{14,63},{16... | collective-permute-start | bytes 1572872 | tf_op jit(solution)/shard_map/ppermute | solution.py:36
  28.1 3.6 %collective-permute-start.11 = (f32[256,4,128]{2,1,0:T(4,128)S(1)}, f32[256,4,128]{2,1,0:T(4,128)}, u32[]{:S(2)}, u32[]{:S(2)}) collective-permute-start(f32[256,4,128]{2,1,0:T(4,128)S(1)} %collective-permute-done.4.refs_4_), channel_id=1, source_target_pairs={{0,192},{2,51},{4,196},{6,55},{8,200},{10,59},{12,204},{14,63},{16... | collective-permute-start | bytes 1572872 | tf_op jit(solution)/shard_map/ppermute | solution.py:36
  33.8 3.6 %collective-permute-start.14 = (f32[256,4,128]{2,1,0:T(4,128)S(1)}, f32[256,4,128]{2,1,0:T(4,128)}, u32[]{:S(2)}, u32[]{:S(2)}) collective-permute-start(f32[256,4,128]{2,1,0:T(4,128)S(1)} %copy.28.refs_0_), channel_id=1, source_target_pairs={{0,192},{2,51},{4,196},{6,55},{8,200},{10,59},{12,204},{14,63},{16... | collective-permute-start | bytes 1572872 | tf_op jit(solution)/shard_map/ppermute | solution.py:36
  37.4 2.1 %collective-permute-done.5.refs_5_ = f32[256,4,128]{2,1,0:T(4,128)} collective-permute-done((f32[256,4,128]{2,1,0:T(4,128)S(1)}, f32[256,4,128]{2,1,0:T(4,128)}, u32[]{:S(2)}, u32[]{:S(2)}) %collective-permute-start.5) | collective-permute-done | bytes 524320 | tf_op jit(solution)/shard_map/ppermute | solution.py:36
  40.5 2.4 %collective-permute-start.13 = (f32[256,4,128]{2,1,0:T(4,128)}, f32[256,4,128]{2,1,0:T(4,128)}, u32[]{:S(2)}, u32[]{:S(2)}) collective-permute-start(f32[256,4,128]{2,1,0:T(4,128)} %collective-permute-done.11.refs_11_), channel_id=1, source_target_pairs={{0,192},{2,51},{4,196},{6,55},{8,200},{10,59},{12,204},{14,63},{16... | collective-permute-start | bytes 1572872 | tf_op jit(solution)/shard_map/ppermute | solution.py:36
  43.0 2.1 %collective-permute-done.9.refs_9_ = f32[256,4,128]{2,1,0:T(4,128)} collective-permute-done((f32[256,4,128]{2,1,0:T(4,128)S(1)}, f32[256,4,128]{2,1,0:T(4,128)}, u32[]{:S(2)}, u32[]{:S(2)}) %collective-permute-start.9) | collective-permute-done | bytes 524320 | tf_op jit(solution)/shard_map/ppermute | solution.py:36
  48.9 1.8 %collective-permute-done.10.refs_10_ = f32[256,4,128]{2,1,0:T(4,128)} collective-permute-done((f32[256,4,128]{2,1,0:T(4,128)S(1)}, f32[256,4,128]{2,1,0:T(4,128)}, u32[]{:S(2)}, u32[]{:S(2)}) %collective-permute-start.10) | collective-permute-done | bytes 524320 | tf_op jit(solution)/shard_map/ppermute | solution.py:36
  50.7 2.7 %assemble.1.refs_6_ = f32[4096,4,128]{2,1,0:T(4,128)S(1)} custom-call(s32[16]{0:T(128)S(1)} %fusion.21.base_ref.refs_7_, f32[256,4,128]{2,1,0:T(4,128)S(1)} %copy.28.refs_0_, f32[256,4,128]{2,1,0:T(4,128)S(1)} %collective-permute-done.1.refs_1_, f32[256,4,128]{2,1,0:T(4,128)S(1)} %collective-permute-done.2.refs_2_, ...), custom_call_target="tpu_custom_call" | custom-call | tf_op jit(solution)/shard_map/assemble/pallas_call | solution.py:234
  53.3 2.9 %collective-permute-done.12.refs_8_ = f32[256,4,128]{2,1,0:T(4,128)} collective-permute-done((f32[256,4,128]{2,1,0:T(4,128)}, f32[256,4,128]{2,1,0:T(4,128)}, u32[]{:S(2)}, u32[]{:S(2)}) %collective-permute-start.12) | collective-permute-done | bytes 524320 | tf_op jit(solution)/shard_map/ppermute | solution.py:36
  56.3 5.6 %collective-permute-done.15.refs_11_ = f32[256,4,128]{2,1,0:T(4,128)} collective-permute-done((f32[256,4,128]{2,1,0:T(4,128)}, f32[256,4,128]{2,1,0:T(4,128)}, u32[]{:S(2)}, u32[]{:S(2)}) %collective-permute-start.15) | collective-permute-done | bytes 524320 | tf_op jit(solution)/shard_map/ppermute | solution.py:36
  61.9 7.4 %sigma_partial.2 = (f32[4096,4,128]{2,1,0:T(4,128)S(1)}, f32[16,64,128]{2,1,0:T(8,128)S(1)}, f32[16,64,128]{2,1,0:T(8,128)S(1)}) custom-call(s32[2048]{0:T(1024)S(1)} %slice.89.refs_0_, s32[256]{0:T(256)S(1)} %pad_add_fusion.refs_1_, f32[8,256]{1,0:T(8,128)S(1)} %slice.91.refs_2_, f32[256,256]{1,0:T(8,128)S(1)} %mul.51.refs_3_, ...), custom_call_target="tpu_custom_call", output_to_operand_aliasing={{0}: (6, {})} | custom-call | flops 4000000000 | bytes 8388608 | tf_op jit(solution)/shard_map/sigma_partial/pallas_call | solution.py:252
  69.4 5.8 %sigma_partial.3 = (f32[16,64,128]{2,1,0:T(8,128)S(1)}, f32[16,64,128]{2,1,0:T(8,128)S(1)}) custom-call(s32[2048]{0:T(1024)S(1)} %slice.102.refs_0_, s32[256]{0:T(256)S(1)} %pad_add_fusion.refs_1_, f32[8,256]{1,0:T(8,128)S(1)} %slice.104.refs_2_, f32[256,256]{1,0:T(8,128)S(1)} %mul.51.refs_3_, s32[1024,128]{1,0:T(8,128)S(1)} %bitcast.18, ...), custom_call_target="tpu_custom_call" | custom-call | flops 4000000000 | bytes 8388608 | tf_op jit(solution)/shard_map/sigma_partial/pallas_call | solution.py:252
  75.8 2.4 %collective-permute-start.17 = (f32[4,64,128]{2,1,0:T(8,128)S(1)}, f32[4,64,128]{2,1,0:T(8,128)S(1)}, u32[]{:S(2)}, u32[]{:S(2)}) collective-permute-start(f32[4,64,128]{2,1,0:T(8,128)S(1)} %get-tuple-element.40), channel_id=1, source_target_pairs={{0,8},{2,10},{4,12},{6,14},{8,0},{10,2},{12,4},{14,6},{1,9},{3,11}... | collective-permute-start | bytes 393224 | tf_op jit(solution)/shard_map/ppermute | solution.py:290
  80.3 2.8 %collective-permute-start.21 = (f32[4,64,128]{2,1,0:T(8,128)S(1)}, f32[4,64,128]{2,1,0:T(8,128)S(1)}, u32[]{:S(2)}, u32[]{:S(2)}) collective-permute-start(f32[4,64,128]{2,1,0:T(8,128)S(1)} %get-tuple-element.37), channel_id=1, source_target_pairs={{0,8},{2,10},{4,12},{6,14},{8,0},{10,2},{12,4},{14,6},{1,9},{3,11}... | collective-permute-start | bytes 393224 | tf_op jit(solution)/shard_map/ppermute | solution.py:290
  86.8 4.8 %collective-permute-start.24 = (f32[4,64,128]{2,1,0:T(8,128)S(1)}, f32[4,64,128]{2,1,0:T(8,128)S(1)}, u32[]{:S(2)}, u32[]{:S(2)}) collective-permute-start(f32[4,64,128]{2,1,0:T(8,128)S(1)} %fusion.7), channel_id=1, source_target_pairs={{0,1},{1,0},{2,3},{3,2},{4,5},{5,4},{6,7},{7,6},{8,9},{9,8},{10,11... | collective-permute-start | bytes 393224 | tf_op jit(solution)/shard_map/ppermute | solution.py:291
  91.6 4.7 %collective-permute-start.25 = (f32[4,64,128]{2,1,0:T(8,128)S(1)}, f32[4,64,128]{2,1,0:T(8,128)S(1)}, u32[]{:S(2)}, u32[]{:S(2)}) collective-permute-start(f32[4,64,128]{2,1,0:T(8,128)S(1)} %fusion.4), channel_id=1, source_target_pairs={{0,1},{1,0},{2,3},{3,2},{4,5},{5,4},{6,7},{7,6},{8,9},{9,8},{10,11... | collective-permute-start | bytes 393224 | tf_op jit(solution)/shard_map/ppermute | solution.py:291
  96.3 3.0 %collective-permute-done.24 = f32[4,64,128]{2,1,0:T(8,128)S(1)} collective-permute-done((f32[4,64,128]{2,1,0:T(8,128)S(1)}, f32[4,64,128]{2,1,0:T(8,128)S(1)}, u32[]{:S(2)}, u32[]{:S(2)}) %collective-permute-start.24) | collective-permute-done | bytes 131104 | tf_op jit(solution)/shard_map/ppermute | solution.py:291
  99.3 5.2 %collective-permute-done.25 = f32[4,64,128]{2,1,0:T(8,128)S(1)} collective-permute-done((f32[4,64,128]{2,1,0:T(8,128)S(1)}, f32[4,64,128]{2,1,0:T(8,128)S(1)}, u32[]{:S(2)}, u32[]{:S(2)}) %collective-permute-start.25) | collective-permute-done | bytes 131104 | tf_op jit(solution)/shard_map/ppermute | solution.py:291
  (76 shorter events, 22.6 us)
Async XLA Ops:
  1.3 21.9 %collective-permute-start.3 = (f32[256,4,128]{2,1,0:T(4,128)S(1)}, f32[256,4,128]{2,1,0:T(4,128)S(1)}, u32[]{:S(2)}, u32[]{:S(2)}) collective-permute-start(f32[256,4,128]{2,1,0:T(4,128)S(1)} %copy.28.refs_0_), channel_id=1, source_target_pairs={{0,16},{2,66},{4,20},{6,70},{8,24},{10,74},{12,28},{14,78},{16,32}... | collective-permute-start | bytes 1572872 | tf_op jit(solution)/shard_map/ppermute | solution.py:36
  3.3 12.6 %collective-permute-start.2 = (f32[256,4,128]{2,1,0:T(4,128)S(1)}, f32[256,4,128]{2,1,0:T(4,128)S(1)}, u32[]{:S(2)}, u32[]{:S(2)}) collective-permute-start(f32[256,4,128]{2,1,0:T(4,128)S(1)} %copy.28.refs_0_), channel_id=1, source_target_pairs={{0,49},{2,194},{4,53},{6,198},{8,57},{10,202},{12,61},{14,206},{16... | collective-permute-start | bytes 1572872 | tf_op jit(solution)/shard_map/ppermute | solution.py:36
  7.3 10.7 %collective-permute-start.1 = (f32[256,4,128]{2,1,0:T(4,128)S(1)}, f32[256,4,128]{2,1,0:T(4,128)S(1)}, u32[]{:S(2)}, u32[]{:S(2)}) collective-permute-start(f32[256,4,128]{2,1,0:T(4,128)S(1)} %copy.28.refs_0_), channel_id=1, source_target_pairs={{0,64},{2,18},{4,68},{6,22},{8,72},{10,26},{12,76},{14,30},{16,80}... | collective-permute-start | bytes 1572872 | tf_op jit(solution)/shard_map/ppermute | solution.py:36
  10.2 13.0 %collective-permute-start = (f32[48,128]{1,0:T(8,128)S(1)}, f32[48,128]{1,0:T(8,128)S(1)}, u32[]{:S(2)}, u32[]{:S(2)}) collective-permute-start(f32[48,128]{1,0:T(8,128)S(1)} %select_maximum_fusion), channel_id=1, source_target_pairs={{0,1},{1,0},{2,3},{3,2},{4,5},{5,4},{6,7},{7,6},{8,9},{9,8},{10,11... | collective-permute-start | bytes 73736 | tf_op jit(solution)/shard_map/ppermute | solution.py:69
  15.9 11.8 %collective-permute-start.4 = (f32[256,4,128]{2,1,0:T(4,128)S(1)}, f32[256,4,128]{2,1,0:T(4,128)S(1)}, u32[]{:S(2)}, u32[]{:S(2)}) collective-permute-start(f32[256,4,128]{2,1,0:T(4,128)S(1)} %collective-permute-done.2.refs_2_), channel_id=1, source_target_pairs={{0,49},{2,194},{4,53},{6,198},{8,57},{10,202},{12,61},{14,206},{16... | collective-permute-start | bytes 1572872 | tf_op jit(solution)/shard_map/ppermute | solution.py:36
  18.0 10.1 %collective-permute-start.6 = (f32[256,4,128]{2,1,0:T(4,128)S(1)}, f32[256,4,128]{2,1,0:T(4,128)S(1)}, u32[]{:S(2)}, u32[]{:S(2)}) collective-permute-start(f32[256,4,128]{2,1,0:T(4,128)S(1)} %collective-permute-done.2.refs_2_), channel_id=1, source_target_pairs={{0,192},{2,51},{4,196},{6,55},{8,200},{10,59},{12,204},{14,63},{16... | collective-permute-start | bytes 1572872 | tf_op jit(solution)/shard_map/ppermute | solution.py:36
  23.2 14.1 %collective-permute-start.7 = (f32[256,4,128]{2,1,0:T(4,128)S(1)}, f32[256,4,128]{2,1,0:T(4,128)}, u32[]{:S(2)}, u32[]{:S(2)}) collective-permute-start(f32[256,4,128]{2,1,0:T(4,128)S(1)} %collective-permute-done.3.refs_3_), channel_id=1, source_target_pairs={{0,64},{2,18},{4,68},{6,22},{8,72},{10,26},{12,76},{14,30},{16,80}... | collective-permute-start | bytes 1572872 | tf_op jit(solution)/shard_map/ppermute | solution.py:36
  24.1 9.7 %collective-permute-start.8 = (f32[256,4,128]{2,1,0:T(4,128)S(1)}, f32[256,4,128]{2,1,0:T(4,128)}, u32[]{:S(2)}, u32[]{:S(2)}) collective-permute-start(f32[256,4,128]{2,1,0:T(4,128)S(1)} %collective-permute-done.3.refs_3_), channel_id=1, source_target_pairs={{0,192},{2,51},{4,196},{6,55},{8,200},{10,59},{12,204},{14,63},{16... | collective-permute-start | bytes 1572872 | tf_op jit(solution)/shard_map/ppermute | solution.py:36
  26.5 12.9 %collective-permute-start.5 = (f32[256,4,128]{2,1,0:T(4,128)S(1)}, f32[256,4,128]{2,1,0:T(4,128)}, u32[]{:S(2)}, u32[]{:S(2)}) collective-permute-start(f32[256,4,128]{2,1,0:T(4,128)S(1)} %collective-permute-done.2.refs_2_), channel_id=1, source_target_pairs={{0,64},{2,18},{4,68},{6,22},{8,72},{10,26},{12,76},{14,30},{16,80}... | collective-permute-start | bytes 1572872 | tf_op jit(solution)/shard_map/ppermute | solution.py:36
  28.1 12.5 %collective-permute-start.11 = (f32[256,4,128]{2,1,0:T(4,128)S(1)}, f32[256,4,128]{2,1,0:T(4,128)}, u32[]{:S(2)}, u32[]{:S(2)}) collective-permute-start(f32[256,4,128]{2,1,0:T(4,128)S(1)} %collective-permute-done.4.refs_4_), channel_id=1, source_target_pairs={{0,192},{2,51},{4,196},{6,55},{8,200},{10,59},{12,204},{14,63},{16... | collective-permute-start | bytes 1572872 | tf_op jit(solution)/shard_map/ppermute | solution.py:36
  31.6 13.4 %collective-permute-start.9 = (f32[256,4,128]{2,1,0:T(4,128)S(1)}, f32[256,4,128]{2,1,0:T(4,128)}, u32[]{:S(2)}, u32[]{:S(2)}) collective-permute-start(f32[256,4,128]{2,1,0:T(4,128)S(1)} %collective-permute-done.1.refs_1_), channel_id=1, source_target_pairs={{0,64},{2,18},{4,68},{6,22},{8,72},{10,26},{12,76},{14,30},{16,80}... | collective-permute-start | bytes 1572872 | tf_op jit(solution)/shard_map/ppermute | solution.py:36
  33.8 19.5 %collective-permute-start.14 = (f32[256,4,128]{2,1,0:T(4,128)S(1)}, f32[256,4,128]{2,1,0:T(4,128)}, u32[]{:S(2)}, u32[]{:S(2)}) collective-permute-start(f32[256,4,128]{2,1,0:T(4,128)S(1)} %copy.28.refs_0_), channel_id=1, source_target_pairs={{0,192},{2,51},{4,196},{6,55},{8,200},{10,59},{12,204},{14,63},{16... | collective-permute-start | bytes 1572872 | tf_op jit(solution)/shard_map/ppermute | solution.py:36
  39.4 11.2 %collective-permute-start.10 = (f32[256,4,128]{2,1,0:T(4,128)S(1)}, f32[256,4,128]{2,1,0:T(4,128)}, u32[]{:S(2)}, u32[]{:S(2)}) collective-permute-start(f32[256,4,128]{2,1,0:T(4,128)S(1)} %collective-permute-done.4.refs_4_), channel_id=1, source_target_pairs={{0,64},{2,18},{4,68},{6,22},{8,72},{10,26},{12,76},{14,30},{16,80}... | collective-permute-start | bytes 1572872 | tf_op jit(solution)/shard_map/ppermute | solution.py:36
  39.4 16.8 %collective-permute-start.12 = (f32[256,4,128]{2,1,0:T(4,128)}, f32[256,4,128]{2,1,0:T(4,128)}, u32[]{:S(2)}, u32[]{:S(2)}) collective-permute-start(f32[256,4,128]{2,1,0:T(4,128)} %collective-permute-done.5.refs_5_), channel_id=1, source_target_pairs={{0,64},{2,18},{4,68},{6,22},{8,72},{10,26},{12,76},{14,30},{16,80}... | collective-permute-start | bytes 1572872 | tf_op jit(solution)/shard_map/ppermute | solution.py:36
  40.5 15.8 %collective-permute-start.13 = (f32[256,4,128]{2,1,0:T(4,128)}, f32[256,4,128]{2,1,0:T(4,128)}, u32[]{:S(2)}, u32[]{:S(2)}) collective-permute-start(f32[256,4,128]{2,1,0:T(4,128)} %collective-permute-done.11.refs_11_), channel_id=1, source_target_pairs={{0,192},{2,51},{4,196},{6,55},{8,200},{10,59},{12,204},{14,63},{16... | collective-permute-start | bytes 1572872 | tf_op jit(solution)/shard_map/ppermute | solution.py:36
  45.0 16.9 %collective-permute-start.15 = (f32[256,4,128]{2,1,0:T(4,128)}, f32[256,4,128]{2,1,0:T(4,128)}, u32[]{:S(2)}, u32[]{:S(2)}) collective-permute-start(f32[256,4,128]{2,1,0:T(4,128)} %collective-permute-done.7.refs_7_), channel_id=1, source_target_pairs={{0,64},{2,18},{4,68},{6,22},{8,72},{10,26},{12,76},{14,30},{16,80}... | collective-permute-start | bytes 1572872 | tf_op jit(solution)/shard_map/ppermute | solution.py:36
  75.8 7.9 %collective-permute-start.17 = (f32[4,64,128]{2,1,0:T(8,128)S(1)}, f32[4,64,128]{2,1,0:T(8,128)S(1)}, u32[]{:S(2)}, u32[]{:S(2)}) collective-permute-start(f32[4,64,128]{2,1,0:T(8,128)S(1)} %get-tuple-element.40), channel_id=1, source_target_pairs={{0,8},{2,10},{4,12},{6,14},{8,0},{10,2},{12,4},{14,6},{1,9},{3,11}... | collective-permute-start | bytes 393224 | tf_op jit(solution)/shard_map/ppermute | solution.py:290
  78.2 8.5 %collective-permute-start.19 = (f32[4,64,128]{2,1,0:T(8,128)S(1)}, f32[4,64,128]{2,1,0:T(8,128)S(1)}, u32[]{:S(2)}, u32[]{:S(2)}) collective-permute-start(f32[4,64,128]{2,1,0:T(8,128)S(1)} %get-tuple-element.41), channel_id=1, source_target_pairs={{0,12},{2,14},{4,0},{6,2},{8,4},{10,6},{12,8},{14,10},{1,13},{3,15... | collective-permute-start | bytes 393224 | tf_op jit(solution)/shard_map/ppermute | solution.py:290
  79.6 7.1 %collective-permute-start.18 = (f32[4,64,128]{2,1,0:T(8,128)S(1)}, f32[4,64,128]{2,1,0:T(8,128)S(1)}, u32[]{:S(2)}, u32[]{:S(2)}) collective-permute-start(f32[4,64,128]{2,1,0:T(8,128)S(1)} %get-tuple-element.42), channel_id=1, source_target_pairs={{0,4},{2,6},{4,8},{6,10},{8,12},{10,14},{12,0},{14,2},{1,5},{3,7},... | collective-permute-start | bytes 393224 | tf_op jit(solution)/shard_map/ppermute | solution.py:290
  80.3 11.3 %collective-permute-start.21 = (f32[4,64,128]{2,1,0:T(8,128)S(1)}, f32[4,64,128]{2,1,0:T(8,128)S(1)}, u32[]{:S(2)}, u32[]{:S(2)}) collective-permute-start(f32[4,64,128]{2,1,0:T(8,128)S(1)} %get-tuple-element.37), channel_id=1, source_target_pairs={{0,8},{2,10},{4,12},{6,14},{8,0},{10,2},{12,4},{14,6},{1,9},{3,11}... | collective-permute-start | bytes 393224 | tf_op jit(solution)/shard_map/ppermute | solution.py:290
  83.1 8.5 %collective-permute-start.23 = (f32[4,64,128]{2,1,0:T(8,128)S(1)}, f32[4,64,128]{2,1,0:T(8,128)S(1)}, u32[]{:S(2)}, u32[]{:S(2)}) collective-permute-start(f32[4,64,128]{2,1,0:T(8,128)S(1)} %get-tuple-element.38), channel_id=1, source_target_pairs={{0,12},{2,14},{4,0},{6,2},{8,4},{10,6},{12,8},{14,10},{1,13},{3,15... | collective-permute-start | bytes 393224 | tf_op jit(solution)/shard_map/ppermute | solution.py:290
  83.8 7.8 %collective-permute-start.22 = (f32[4,64,128]{2,1,0:T(8,128)S(1)}, f32[4,64,128]{2,1,0:T(8,128)S(1)}, u32[]{:S(2)}, u32[]{:S(2)}) collective-permute-start(f32[4,64,128]{2,1,0:T(8,128)S(1)} %get-tuple-element.39), channel_id=1, source_target_pairs={{0,4},{2,6},{4,8},{6,10},{8,12},{10,14},{12,0},{14,2},{1,5},{3,7},... | collective-permute-start | bytes 393224 | tf_op jit(solution)/shard_map/ppermute | solution.py:290
  86.8 12.5 %collective-permute-start.24 = (f32[4,64,128]{2,1,0:T(8,128)S(1)}, f32[4,64,128]{2,1,0:T(8,128)S(1)}, u32[]{:S(2)}, u32[]{:S(2)}) collective-permute-start(f32[4,64,128]{2,1,0:T(8,128)S(1)} %fusion.7), channel_id=1, source_target_pairs={{0,1},{1,0},{2,3},{3,2},{4,5},{5,4},{6,7},{7,6},{8,9},{9,8},{10,11... | collective-permute-start | bytes 393224 | tf_op jit(solution)/shard_map/ppermute | solution.py:291
  91.6 12.8 %collective-permute-start.25 = (f32[4,64,128]{2,1,0:T(8,128)S(1)}, f32[4,64,128]{2,1,0:T(8,128)S(1)}, u32[]{:S(2)}, u32[]{:S(2)}) collective-permute-start(f32[4,64,128]{2,1,0:T(8,128)S(1)} %fusion.4), channel_id=1, source_target_pairs={{0,1},{1,0},{2,3},{3,2},{4,5},{5,4},{6,7},{7,6},{8,9},{9,8},{10,11... | collective-permute-start | bytes 393224 | tf_op jit(solution)/shard_map/ppermute | solution.py:291
  (4 other events, 37.6 us)

commit v7 on v6

--- a/solution.py
+++ b/solution.py
@@ -12,7 +12,7 @@
 RING = 4
 CORES = 2
 CHUNKS = 2
-UNROLL = 16
+UNROLL = 32
 MIXES = 8
 FLIGHT = 5
 AXES = ("alpha", "beta", "ints")
@@ -289,10 +289,9 @@
             part = keep[far * slots : (far + 1) * slots] + came[far * slots : (far + 1) * slots]
             total = total + lax.ppermute(part, "beta", pairs_y)
         sums.append((total, lax.ppermute(total, "ints", swap)))
-    mine_all = jnp.concatenate([m for m, _ in sums], 1)
-    other_all = jnp.concatenate([o for _, o in sums], 1)
-    joined = jnp.concatenate([jnp.where(first, mine_all, other_all), jnp.where(first, other_all, mine_all)], 1)
-    return joined.transpose(0, 2, 1).reshape(rows_b, cols_a)
+    mine_all = jnp.concatenate([m for m, _ in sums], 1).transpose(0, 2, 1).reshape(rows_b, cols)
+    other_all = jnp.concatenate([o for _, o in sums], 1).transpose(0, 2, 1).reshape(rows_b, cols)
+    return jnp.concatenate([jnp.where(first, mine_all, other_all), jnp.where(first, other_all, mine_all)], 1)
 
 
 def solution(mesh):

time: 107 us -> 106 us (level)
  no operation moved by 1% of the time
where the time goes in v7:
time: 106 us; the launch traced here: 105 us
  starting transfers between devices  50 us (47%)
  waiting for transfers between devices  28.1 us (27%)
  Pallas kernels  15.3 us (14%)
  local copies, waits for them, and re-layouts  6.07 us (6%)
  other arithmetic  5.4 us (5%)
    ppermute x15, starting transfers between devices, move(): return lax.ppermute(value, AXES, pairs)  26.8 us
    ppermute x15, waiting for transfers between devices, move(): return lax.ppermute(value, AXES, pairs)  17.7 us
    pallas_call x2, Pallas kernels, local(): pl.pallas_call(functools.partial(kernel, part_steps, pairs, slots, tuple(...  12.7 us
    ppermute x2, starting transfers between devices, local(): sums.append((total, lax.ppermute(total, 'ints', swap)))  9.47 us
    ppermute x6, starting transfers between devices, local(): total = total + lax.ppermute(part, 'beta', pairs_y)  8.51 us
    ppermute x2, waiting for transfers between devices, local(): sums.append((total, lax.ppermute(total, 'ints', swap)))  8.16 us
    ppermute x1, starting transfers between devices, spread(): held[name] = lax.ppermute(value, 'ints', [(0, 1), (1, 0)])  4.48 us
    pallas_call x1, Pallas kernels, local(): pl.pallas_call(functools.partial(assemble, tuple((slot_of(n) for n in ear...  2.67 us
  transfers between devices with their start and end apart: 26, of which 12 were waited for; matrix products, arithmetic and copies ran while one was open for 9% of the time, Pallas kernels for 8%

profile of v7, /device:TPU:8, one launch (start us, length us, event | category | flops | bytes accessed | tf_op | source)
XLA Modules:
  0.0 105.1 jit_solution(3926722079180108330)
XLA Ops:
  1.3 2.0 %collective-permute-start.3 = (f32[256,4,128]{2,1,0:T(4,128)S(1)}, f32[256,4,128]{2,1,0:T(4,128)S(1)}, u32[]{:S(2)}, u32[]{:S(2)}) collective-permute-start(f32[256,4,128]{2,1,0:T(4,128)S(1)} %copy.30.refs_0_), channel_id=1, source_target_pairs={{0,16},{2,66},{4,20},{6,70},{8,24},{10,74},{12,28},{14,78},{16,32}... | collective-permute-start | bytes 1572872 | tf_op jit(solution)/shard_map/ppermute | solution.py:36
  3.3 4.0 %collective-permute-start.2 = (f32[256,4,128]{2,1,0:T(4,128)S(1)}, f32[256,4,128]{2,1,0:T(4,128)S(1)}, u32[]{:S(2)}, u32[]{:S(2)}) collective-permute-start(f32[256,4,128]{2,1,0:T(4,128)S(1)} %copy.30.refs_0_), channel_id=1, source_target_pairs={{0,49},{2,194},{4,53},{6,198},{8,57},{10,202},{12,61},{14,206},{16... | collective-permute-start | bytes 1572872 | tf_op jit(solution)/shard_map/ppermute | solution.py:36
  10.2 4.5 %collective-permute-start = (f32[48,128]{1,0:T(8,128)S(1)}, f32[48,128]{1,0:T(8,128)S(1)}, u32[]{:S(2)}, u32[]{:S(2)}) collective-permute-start(f32[48,128]{1,0:T(8,128)S(1)} %select_maximum_fusion), channel_id=1, source_target_pairs={{0,1},{1,0},{2,3},{3,2},{4,5},{5,4},{6,7},{7,6},{8,9},{9,8},{10,11... | collective-permute-start | bytes 73736 | tf_op jit(solution)/shard_map/ppermute | solution.py:69
  15.9 2.1 %collective-permute-start.4 = (f32[256,4,128]{2,1,0:T(4,128)S(1)}, f32[256,4,128]{2,1,0:T(4,128)S(1)}, u32[]{:S(2)}, u32[]{:S(2)}) collective-permute-start(f32[256,4,128]{2,1,0:T(4,128)S(1)} %collective-permute-done.2.refs_2_), channel_id=1, source_target_pairs={{0,49},{2,194},{4,53},{6,198},{8,57},{10,202},{12,61},{14,206},{16... | collective-permute-start | bytes 1572872 | tf_op jit(solution)/shard_map/ppermute | solution.py:36
  18.0 3.2 %collective-permute-start.6 = (f32[256,4,128]{2,1,0:T(4,128)S(1)}, f32[256,4,128]{2,1,0:T(4,128)S(1)}, u32[]{:S(2)}, u32[]{:S(2)}) collective-permute-start(f32[256,4,128]{2,1,0:T(4,128)S(1)} %collective-permute-done.2.refs_2_), channel_id=1, source_target_pairs={{0,192},{2,51},{4,196},{6,55},{8,200},{10,59},{12,204},{14,63},{16... | collective-permute-start | bytes 1572872 | tf_op jit(solution)/shard_map/ppermute | solution.py:36
  21.3 1.9 %reshape.56.refs_5_ = s32[1024,128]{1,0:T(8,128)} reshape(s32[32,4096]{1,0:T(8,128)} %param.13) | data formatting | bytes 1048576 | tf_op jit(solution)/shard_map/reshape | solution.py:245
  24.1 2.4 %collective-permute-start.8 = (f32[256,4,128]{2,1,0:T(4,128)S(1)}, f32[256,4,128]{2,1,0:T(4,128)}, u32[]{:S(2)}, u32[]{:S(2)}) collective-permute-start(f32[256,4,128]{2,1,0:T(4,128)S(1)} %collective-permute-done.3.refs_3_), channel_id=1, source_target_pairs={{0,192},{2,51},{4,196},{6,55},{8,200},{10,59},{12,204},{14,63},{16... | collective-permute-start | bytes 1572872 | tf_op jit(solution)/shard_map/ppermute | solution.py:36
  28.1 3.6 %collective-permute-start.11 = (f32[256,4,128]{2,1,0:T(4,128)S(1)}, f32[256,4,128]{2,1,0:T(4,128)}, u32[]{:S(2)}, u32[]{:S(2)}) collective-permute-start(f32[256,4,128]{2,1,0:T(4,128)S(1)} %collective-permute-done.4.refs_4_), channel_id=1, source_target_pairs={{0,192},{2,51},{4,196},{6,55},{8,200},{10,59},{12,204},{14,63},{16... | collective-permute-start | bytes 1572872 | tf_op jit(solution)/shard_map/ppermute | solution.py:36
  33.8 3.6 %collective-permute-start.14 = (f32[256,4,128]{2,1,0:T(4,128)S(1)}, f32[256,4,128]{2,1,0:T(4,128)}, u32[]{:S(2)}, u32[]{:S(2)}) collective-permute-start(f32[256,4,128]{2,1,0:T(4,128)S(1)} %copy.30.refs_0_), channel_id=1, source_target_pairs={{0,192},{2,51},{4,196},{6,55},{8,200},{10,59},{12,204},{14,63},{16... | collective-permute-start | bytes 1572872 | tf_op jit(solution)/shard_map/ppermute | solution.py:36
  37.4 2.1 %collective-permute-done.5.refs_5_ = f32[256,4,128]{2,1,0:T(4,128)} collective-permute-done((f32[256,4,128]{2,1,0:T(4,128)S(1)}, f32[256,4,128]{2,1,0:T(4,128)}, u32[]{:S(2)}, u32[]{:S(2)}) %collective-permute-start.5) | collective-permute-done | bytes 524320 | tf_op jit(solution)/shard_map/ppermute | solution.py:36
  40.5 2.4 %collective-permute-start.13 = (f32[256,4,128]{2,1,0:T(4,128)}, f32[256,4,128]{2,1,0:T(4,128)}, u32[]{:S(2)}, u32[]{:S(2)}) collective-permute-start(f32[256,4,128]{2,1,0:T(4,128)} %collective-permute-done.11.refs_11_), channel_id=1, source_target_pairs={{0,192},{2,51},{4,196},{6,55},{8,200},{10,59},{12,204},{14,63},{16... | collective-permute-start | bytes 1572872 | tf_op jit(solution)/shard_map/ppermute | solution.py:36
  43.0 2.1 %collective-permute-done.9.refs_9_ = f32[256,4,128]{2,1,0:T(4,128)} collective-permute-done((f32[256,4,128]{2,1,0:T(4,128)S(1)}, f32[256,4,128]{2,1,0:T(4,128)}, u32[]{:S(2)}, u32[]{:S(2)}) %collective-permute-start.9) | collective-permute-done | bytes 524320 | tf_op jit(solution)/shard_map/ppermute | solution.py:36
  48.9 1.8 %collective-permute-done.10.refs_10_ = f32[256,4,128]{2,1,0:T(4,128)} collective-permute-done((f32[256,4,128]{2,1,0:T(4,128)S(1)}, f32[256,4,128]{2,1,0:T(4,128)}, u32[]{:S(2)}, u32[]{:S(2)}) %collective-permute-start.10) | collective-permute-done | bytes 524320 | tf_op jit(solution)/shard_map/ppermute | solution.py:36
  50.7 2.7 %assemble.1.refs_6_ = f32[4096,4,128]{2,1,0:T(4,128)S(1)} custom-call(s32[16]{0:T(128)S(1)} %fusion.19.base_ref.refs_7_, f32[256,4,128]{2,1,0:T(4,128)S(1)} %copy.30.refs_0_, f32[256,4,128]{2,1,0:T(4,128)S(1)} %collective-permute-done.1.refs_1_, f32[256,4,128]{2,1,0:T(4,128)S(1)} %collective-permute-done.2.refs_2_, ...), custom_call_target="tpu_custom_call" | custom-call | tf_op jit(solution)/shard_map/assemble/pallas_call | solution.py:234
  53.3 2.9 %collective-permute-done.12.refs_8_ = f32[256,4,128]{2,1,0:T(4,128)} collective-permute-done((f32[256,4,128]{2,1,0:T(4,128)}, f32[256,4,128]{2,1,0:T(4,128)}, u32[]{:S(2)}, u32[]{:S(2)}) %collective-permute-start.12) | collective-permute-done | bytes 524320 | tf_op jit(solution)/shard_map/ppermute | solution.py:36
  56.3 5.6 %collective-permute-done.15.refs_11_ = f32[256,4,128]{2,1,0:T(4,128)} collective-permute-done((f32[256,4,128]{2,1,0:T(4,128)}, f32[256,4,128]{2,1,0:T(4,128)}, u32[]{:S(2)}, u32[]{:S(2)}) %collective-permute-start.15) | collective-permute-done | bytes 524320 | tf_op jit(solution)/shard_map/ppermute | solution.py:36
  61.9 7.1 %sigma_partial.2 = (f32[4096,4,128]{2,1,0:T(4,128)S(1)}, f32[16,64,128]{2,1,0:T(8,128)S(1)}, f32[16,64,128]{2,1,0:T(8,128)S(1)}) custom-call(s32[2048]{0:T(1024)S(1)} %slice.89.refs_0_, s32[256]{0:T(256)S(1)} %pad_add_fusion.refs_1_, f32[8,256]{1,0:T(8,128)S(1)} %slice.91.refs_2_, f32[256,256]{1,0:T(8,128)S(1)} %mul.51.refs_3_, ...), custom_call_target="tpu_custom_call", output_to_operand_aliasing={{0}: (6, {})} | custom-call | flops 4000000000 | bytes 8388608 | tf_op jit(solution)/shard_map/sigma_partial/pallas_call | solution.py:252
  69.1 5.6 %sigma_partial.3 = (f32[16,64,128]{2,1,0:T(8,128)S(1)}, f32[16,64,128]{2,1,0:T(8,128)S(1)}) custom-call(s32[2048]{0:T(1024)S(1)} %slice.102.refs_0_, s32[256]{0:T(256)S(1)} %pad_add_fusion.refs_1_, f32[8,256]{1,0:T(8,128)S(1)} %slice.104.refs_2_, f32[256,256]{1,0:T(8,128)S(1)} %mul.51.refs_3_, s32[1024,128]{1,0:T(8,128)S(1)} %bitcast.21, ...), custom_call_target="tpu_custom_call" | custom-call | flops 4000000000 | bytes 8388608 | tf_op jit(solution)/shard_map/sigma_partial/pallas_call | solution.py:252
  75.3 2.4 %collective-permute-start.17 = (f32[4,64,128]{2,1,0:T(8,128)S(1)}, f32[4,64,128]{2,1,0:T(8,128)S(1)}, u32[]{:S(2)}, u32[]{:S(2)}) collective-permute-start(f32[4,64,128]{2,1,0:T(8,128)S(1)} %get-tuple-element.40), channel_id=1, source_target_pairs={{0,8},{2,10},{4,12},{6,14},{8,0},{10,2},{12,4},{14,6},{1,9},{3,11}... | collective-permute-start | bytes 393224 | tf_op jit(solution)/shard_map/ppermute | solution.py:290
  79.8 2.5 %collective-permute-start.21 = (f32[4,64,128]{2,1,0:T(8,128)S(1)}, f32[4,64,128]{2,1,0:T(8,128)S(1)}, u32[]{:S(2)}, u32[]{:S(2)}) collective-permute-start(f32[4,64,128]{2,1,0:T(8,128)S(1)} %get-tuple-element.37), channel_id=1, source_target_pairs={{0,8},{2,10},{4,12},{6,14},{8,0},{10,2},{12,4},{14,6},{1,9},{3,11}... | collective-permute-start | bytes 393224 | tf_op jit(solution)/shard_map/ppermute | solution.py:290
  86.2 4.8 %collective-permute-start.24 = (f32[4,64,128]{2,1,0:T(8,128)S(1)}, f32[4,64,128]{2,1,0:T(8,128)S(1)}, u32[]{:S(2)}, u32[]{:S(2)}) collective-permute-start(f32[4,64,128]{2,1,0:T(8,128)S(1)} %fusion.5), channel_id=1, source_target_pairs={{0,1},{1,0},{2,3},{3,2},{4,5},{5,4},{6,7},{7,6},{8,9},{9,8},{10,11... | collective-permute-start | bytes 393224 | tf_op jit(solution)/shard_map/ppermute | solution.py:291
  91.1 4.6 %collective-permute-start.25 = (f32[4,64,128]{2,1,0:T(8,128)S(1)}, f32[4,64,128]{2,1,0:T(8,128)S(1)}, u32[]{:S(2)}, u32[]{:S(2)}) collective-permute-start(f32[4,64,128]{2,1,0:T(8,128)S(1)} %fusion.2), channel_id=1, source_target_pairs={{0,1},{1,0},{2,3},{3,2},{4,5},{5,4},{6,7},{7,6},{8,9},{9,8},{10,11... | collective-permute-start | bytes 393224 | tf_op jit(solution)/shard_map/ppermute | solution.py:291
  95.8 3.0 %collective-permute-done.24 = f32[4,64,128]{2,1,0:T(8,128)S(1)} collective-permute-done((f32[4,64,128]{2,1,0:T(8,128)S(1)}, f32[4,64,128]{2,1,0:T(8,128)S(1)}, u32[]{:S(2)}, u32[]{:S(2)}) %collective-permute-start.24) | collective-permute-done | bytes 131104 | tf_op jit(solution)/shard_map/ppermute | solution.py:291
  98.8 5.2 %collective-permute-done.25 = f32[4,64,128]{2,1,0:T(8,128)S(1)} collective-permute-done((f32[4,64,128]{2,1,0:T(8,128)S(1)}, f32[4,64,128]{2,1,0:T(8,128)S(1)}, u32[]{:S(2)}, u32[]{:S(2)}) %collective-permute-start.25) | collective-permute-done | bytes 131104 | tf_op jit(solution)/shard_map/ppermute | solution.py:291
  (77 shorter events, 22.8 us)
Async XLA Ops:
  1.3 21.9 %collective-permute-start.3 = (f32[256,4,128]{2,1,0:T(4,128)S(1)}, f32[256,4,128]{2,1,0:T(4,128)S(1)}, u32[]{:S(2)}, u32[]{:S(2)}) collective-permute-start(f32[256,4,128]{2,1,0:T(4,128)S(1)} %copy.30.refs_0_), channel_id=1, source_target_pairs={{0,16},{2,66},{4,20},{6,70},{8,24},{10,74},{12,28},{14,78},{16,32}... | collective-permute-start | bytes 1572872 | tf_op jit(solution)/shard_map/ppermute | solution.py:36
  3.3 12.6 %collective-permute-start.2 = (f32[256,4,128]{2,1,0:T(4,128)S(1)}, f32[256,4,128]{2,1,0:T(4,128)S(1)}, u32[]{:S(2)}, u32[]{:S(2)}) collective-permute-start(f32[256,4,128]{2,1,0:T(4,128)S(1)} %copy.30.refs_0_), channel_id=1, source_target_pairs={{0,49},{2,194},{4,53},{6,198},{8,57},{10,202},{12,61},{14,206},{16... | collective-permute-start | bytes 1572872 | tf_op jit(solution)/shard_map/ppermute | solution.py:36
  7.3 10.7 %collective-permute-start.1 = (f32[256,4,128]{2,1,0:T(4,128)S(1)}, f32[256,4,128]{2,1,0:T(4,128)S(1)}, u32[]{:S(2)}, u32[]{:S(2)}) collective-permute-start(f32[256,4,128]{2,1,0:T(4,128)S(1)} %copy.30.refs_0_), channel_id=1, source_target_pairs={{0,64},{2,18},{4,68},{6,22},{8,72},{10,26},{12,76},{14,30},{16,80}... | collective-permute-start | bytes 1572872 | tf_op jit(solution)/shard_map/ppermute | solution.py:36
  10.2 13.0 %collective-permute-start = (f32[48,128]{1,0:T(8,128)S(1)}, f32[48,128]{1,0:T(8,128)S(1)}, u32[]{:S(2)}, u32[]{:S(2)}) collective-permute-start(f32[48,128]{1,0:T(8,128)S(1)} %select_maximum_fusion), channel_id=1, source_target_pairs={{0,1},{1,0},{2,3},{3,2},{4,5},{5,4},{6,7},{7,6},{8,9},{9,8},{10,11... | collective-permute-start | bytes 73736 | tf_op jit(solution)/shard_map/ppermute | solution.py:69
  15.9 11.8 %collective-permute-start.4 = (f32[256,4,128]{2,1,0:T(4,128)S(1)}, f32[256,4,128]{2,1,0:T(4,128)S(1)}, u32[]{:S(2)}, u32[]{:S(2)}) collective-permute-start(f32[256,4,128]{2,1,0:T(4,128)S(1)} %collective-permute-done.2.refs_2_), channel_id=1, source_target_pairs={{0,49},{2,194},{4,53},{6,198},{8,57},{10,202},{12,61},{14,206},{16... | collective-permute-start | bytes 1572872 | tf_op jit(solution)/shard_map/ppermute | solution.py:36
  18.0 10.1 %collective-permute-start.6 = (f32[256,4,128]{2,1,0:T(4,128)S(1)}, f32[256,4,128]{2,1,0:T(4,128)S(1)}, u32[]{:S(2)}, u32[]{:S(2)}) collective-permute-start(f32[256,4,128]{2,1,0:T(4,128)S(1)} %collective-permute-done.2.refs_2_), channel_id=1, source_target_pairs={{0,192},{2,51},{4,196},{6,55},{8,200},{10,59},{12,204},{14,63},{16... | collective-permute-start | bytes 1572872 | tf_op jit(solution)/shard_map/ppermute | solution.py:36
  23.2 14.1 %collective-permute-start.7 = (f32[256,4,128]{2,1,0:T(4,128)S(1)}, f32[256,4,128]{2,1,0:T(4,128)}, u32[]{:S(2)}, u32[]{:S(2)}) collective-permute-start(f32[256,4,128]{2,1,0:T(4,128)S(1)} %collective-permute-done.3.refs_3_), channel_id=1, source_target_pairs={{0,64},{2,18},{4,68},{6,22},{8,72},{10,26},{12,76},{14,30},{16,80}... | collective-permute-start | bytes 1572872 | tf_op jit(solution)/shard_map/ppermute | solution.py:36
  24.1 9.7 %collective-permute-start.8 = (f32[256,4,128]{2,1,0:T(4,128)S(1)}, f32[256,4,128]{2,1,0:T(4,128)}, u32[]{:S(2)}, u32[]{:S(2)}) collective-permute-start(f32[256,4,128]{2,1,0:T(4,128)S(1)} %collective-permute-done.3.refs_3_), channel_id=1, source_target_pairs={{0,192},{2,51},{4,196},{6,55},{8,200},{10,59},{12,204},{14,63},{16... | collective-permute-start | bytes 1572872 | tf_op jit(solution)/shard_map/ppermute | solution.py:36
  26.5 12.9 %collective-permute-start.5 = (f32[256,4,128]{2,1,0:T(4,128)S(1)}, f32[256,4,128]{2,1,0:T(4,128)}, u32[]{:S(2)}, u32[]{:S(2)}) collective-permute-start(f32[256,4,128]{2,1,0:T(4,128)S(1)} %collective-permute-done.2.refs_2_), channel_id=1, source_target_pairs={{0,64},{2,18},{4,68},{6,22},{8,72},{10,26},{12,76},{14,30},{16,80}... | collective-permute-start | bytes 1572872 | tf_op jit(solution)/shard_map/ppermute | solution.py:36
  28.1 12.5 %collective-permute-start.11 = (f32[256,4,128]{2,1,0:T(4,128)S(1)}, f32[256,4,128]{2,1,0:T(4,128)}, u32[]{:S(2)}, u32[]{:S(2)}) collective-permute-start(f32[256,4,128]{2,1,0:T(4,128)S(1)} %collective-permute-done.4.refs_4_), channel_id=1, source_target_pairs={{0,192},{2,51},{4,196},{6,55},{8,200},{10,59},{12,204},{14,63},{16... | collective-permute-start | bytes 1572872 | tf_op jit(solution)/shard_map/ppermute | solution.py:36
  31.6 13.4 %collective-permute-start.9 = (f32[256,4,128]{2,1,0:T(4,128)S(1)}, f32[256,4,128]{2,1,0:T(4,128)}, u32[]{:S(2)}, u32[]{:S(2)}) collective-permute-start(f32[256,4,128]{2,1,0:T(4,128)S(1)} %collective-permute-done.1.refs_1_), channel_id=1, source_target_pairs={{0,64},{2,18},{4,68},{6,22},{8,72},{10,26},{12,76},{14,30},{16,80}... | collective-permute-start | bytes 1572872 | tf_op jit(solution)/shard_map/ppermute | solution.py:36
  33.8 19.5 %collective-permute-start.14 = (f32[256,4,128]{2,1,0:T(4,128)S(1)}, f32[256,4,128]{2,1,0:T(4,128)}, u32[]{:S(2)}, u32[]{:S(2)}) collective-permute-start(f32[256,4,128]{2,1,0:T(4,128)S(1)} %copy.30.refs_0_), channel_id=1, source_target_pairs={{0,192},{2,51},{4,196},{6,55},{8,200},{10,59},{12,204},{14,63},{16... | collective-permute-start | bytes 1572872 | tf_op jit(solution)/shard_map/ppermute | solution.py:36
  39.4 11.2 %collective-permute-start.10 = (f32[256,4,128]{2,1,0:T(4,128)S(1)}, f32[256,4,128]{2,1,0:T(4,128)}, u32[]{:S(2)}, u32[]{:S(2)}) collective-permute-start(f32[256,4,128]{2,1,0:T(4,128)S(1)} %collective-permute-done.4.refs_4_), channel_id=1, source_target_pairs={{0,64},{2,18},{4,68},{6,22},{8,72},{10,26},{12,76},{14,30},{16,80}... | collective-permute-start | bytes 1572872 | tf_op jit(solution)/shard_map/ppermute | solution.py:36
  39.4 16.8 %collective-permute-start.12 = (f32[256,4,128]{2,1,0:T(4,128)}, f32[256,4,128]{2,1,0:T(4,128)}, u32[]{:S(2)}, u32[]{:S(2)}) collective-permute-start(f32[256,4,128]{2,1,0:T(4,128)} %collective-permute-done.5.refs_5_), channel_id=1, source_target_pairs={{0,64},{2,18},{4,68},{6,22},{8,72},{10,26},{12,76},{14,30},{16,80}... | collective-permute-start | bytes 1572872 | tf_op jit(solution)/shard_map/ppermute | solution.py:36
  40.5 15.8 %collective-permute-start.13 = (f32[256,4,128]{2,1,0:T(4,128)}, f32[256,4,128]{2,1,0:T(4,128)}, u32[]{:S(2)}, u32[]{:S(2)}) collective-permute-start(f32[256,4,128]{2,1,0:T(4,128)} %collective-permute-done.11.refs_11_), channel_id=1, source_target_pairs={{0,192},{2,51},{4,196},{6,55},{8,200},{10,59},{12,204},{14,63},{16... | collective-permute-start | bytes 1572872 | tf_op jit(solution)/shard_map/ppermute | solution.py:36
  45.0 16.9 %collective-permute-start.15 = (f32[256,4,128]{2,1,0:T(4,128)}, f32[256,4,128]{2,1,0:T(4,128)}, u32[]{:S(2)}, u32[]{:S(2)}) collective-permute-start(f32[256,4,128]{2,1,0:T(4,128)} %collective-permute-done.7.refs_7_), channel_id=1, source_target_pairs={{0,64},{2,18},{4,68},{6,22},{8,72},{10,26},{12,76},{14,30},{16,80}... | collective-permute-start | bytes 1572872 | tf_op jit(solution)/shard_map/ppermute | solution.py:36
  75.3 7.9 %collective-permute-start.17 = (f32[4,64,128]{2,1,0:T(8,128)S(1)}, f32[4,64,128]{2,1,0:T(8,128)S(1)}, u32[]{:S(2)}, u32[]{:S(2)}) collective-permute-start(f32[4,64,128]{2,1,0:T(8,128)S(1)} %get-tuple-element.40), channel_id=1, source_target_pairs={{0,8},{2,10},{4,12},{6,14},{8,0},{10,2},{12,4},{14,6},{1,9},{3,11}... | collective-permute-start | bytes 393224 | tf_op jit(solution)/shard_map/ppermute | solution.py:290
  77.7 8.5 %collective-permute-start.19 = (f32[4,64,128]{2,1,0:T(8,128)S(1)}, f32[4,64,128]{2,1,0:T(8,128)S(1)}, u32[]{:S(2)}, u32[]{:S(2)}) collective-permute-start(f32[4,64,128]{2,1,0:T(8,128)S(1)} %get-tuple-element.41), channel_id=1, source_target_pairs={{0,12},{2,14},{4,0},{6,2},{8,4},{10,6},{12,8},{14,10},{1,13},{3,15... | collective-permute-start | bytes 393224 | tf_op jit(solution)/shard_map/ppermute | solution.py:290
  79.1 7.1 %collective-permute-start.18 = (f32[4,64,128]{2,1,0:T(8,128)S(1)}, f32[4,64,128]{2,1,0:T(8,128)S(1)}, u32[]{:S(2)}, u32[]{:S(2)}) collective-permute-start(f32[4,64,128]{2,1,0:T(8,128)S(1)} %get-tuple-element.42), channel_id=1, source_target_pairs={{0,4},{2,6},{4,8},{6,10},{8,12},{10,14},{12,0},{14,2},{1,5},{3,7},... | collective-permute-start | bytes 393224 | tf_op jit(solution)/shard_map/ppermute | solution.py:290
  79.8 11.3 %collective-permute-start.21 = (f32[4,64,128]{2,1,0:T(8,128)S(1)}, f32[4,64,128]{2,1,0:T(8,128)S(1)}, u32[]{:S(2)}, u32[]{:S(2)}) collective-permute-start(f32[4,64,128]{2,1,0:T(8,128)S(1)} %get-tuple-element.37), channel_id=1, source_target_pairs={{0,8},{2,10},{4,12},{6,14},{8,0},{10,2},{12,4},{14,6},{1,9},{3,11}... | collective-permute-start | bytes 393224 | tf_op jit(solution)/shard_map/ppermute | solution.py:290
  82.3 8.7 %collective-permute-start.23 = (f32[4,64,128]{2,1,0:T(8,128)S(1)}, f32[4,64,128]{2,1,0:T(8,128)S(1)}, u32[]{:S(2)}, u32[]{:S(2)}) collective-permute-start(f32[4,64,128]{2,1,0:T(8,128)S(1)} %get-tuple-element.38), channel_id=1, source_target_pairs={{0,12},{2,14},{4,0},{6,2},{8,4},{10,6},{12,8},{14,10},{1,13},{3,15... | collective-permute-start | bytes 393224 | tf_op jit(solution)/shard_map/ppermute | solution.py:290
  83.3 7.8 %collective-permute-start.22 = (f32[4,64,128]{2,1,0:T(8,128)S(1)}, f32[4,64,128]{2,1,0:T(8,128)S(1)}, u32[]{:S(2)}, u32[]{:S(2)}) collective-permute-start(f32[4,64,128]{2,1,0:T(8,128)S(1)} %get-tuple-element.39), channel_id=1, source_target_pairs={{0,4},{2,6},{4,8},{6,10},{8,12},{10,14},{12,0},{14,2},{1,5},{3,7},... | collective-permute-start | bytes 393224 | tf_op jit(solution)/shard_map/ppermute | solution.py:290
  86.2 12.5 %collective-permute-start.24 = (f32[4,64,128]{2,1,0:T(8,128)S(1)}, f32[4,64,128]{2,1,0:T(8,128)S(1)}, u32[]{:S(2)}, u32[]{:S(2)}) collective-permute-start(f32[4,64,128]{2,1,0:T(8,128)S(1)} %fusion.5), channel_id=1, source_target_pairs={{0,1},{1,0},{2,3},{3,2},{4,5},{5,4},{6,7},{7,6},{8,9},{9,8},{10,11... | collective-permute-start | bytes 393224 | tf_op jit(solution)/shard_map/ppermute | solution.py:291
  91.1 12.8 %collective-permute-start.25 = (f32[4,64,128]{2,1,0:T(8,128)S(1)}, f32[4,64,128]{2,1,0:T(8,128)S(1)}, u32[]{:S(2)}, u32[]{:S(2)}) collective-permute-start(f32[4,64,128]{2,1,0:T(8,128)S(1)} %fusion.2), channel_id=1, source_target_pairs={{0,1},{1,0},{2,3},{3,2},{4,5},{5,4},{6,7},{7,6},{8,9},{9,8},{10,11... | collective-permute-start | bytes 393224 | tf_op jit(solution)/shard_map/ppermute | solution.py:291
  (4 other events, 37.4 us)
